TPU v7x, 32 devices: a whole 2x2x4 slice. The times are simulated.
32 devices in a mesh: groups: 2 (over x), tm: 16 (over z, y, core).
Axes of the slice: x: 2, y: 2, z: 4, core: 2. Of those that a mesh axis runs over, the one named last changes fastest.
Arguments:
- audio: bfloat16 [16777216], P(('groups', 'tm')), parts along dimension 0, may hold values from -6 to 6
- kernel: bfloat16 [2304, 1024], replicated, may hold values from -0.1875 to 0.1875
- templates: bfloat16 [1152, 512], replicated, may hold values from 0.005 to 0.7, as said below
- activations: bfloat16 [512, 32768], P(None, ('groups', 'tm')), parts along dimension 1, may hold values from 0.01 to 1, as said below
Outputs:
- new_activations: bfloat16 [512, 32768], P(None, ('groups', 'tm')), parts along dimension 1
- new_templates: bfloat16 [2304, 512], P('groups'), parts along dimension 0
There are 2 independent parts, one for each index of `groups`. A program takes and returns all parts, laid end to end along the dimension named above; an argument that names none is the same for every part. Nothing has to cross between parts.
Inputs may be any that keep to these rules, and one draw needn't show every extreme that they name: `templates`: Positive. `activations`: Positive.
All inputs are finite; a program needn't handle non-finite values.
Results may differ from a plain program's by a relative error of at most 0.0051.
Values may be sent and summed in bfloat16 or wider, within the bound.
No kernel may reach another device: no remote copies, remote signals or barrier semaphores. Data moves between devices by JAX's collectives and lax.ppermute only.
A program may use at most 64 MiB of HBM per device.

v0:
```python
import jax
import jax.numpy as jnp
from jax import lax
from jax.sharding import PartitionSpec as P

HOP = 512
ITERS = 2
HALF = 256


def with_halo(x, sides, width):
    for axis, dim in sides:
        peers, length = (lax.axis_size(axis), x.shape[dim])
        up = [(i, (i + 1) % peers) for i in range(peers - 1)]
        down = [(j, i) for i, j in up]
        last = lax.slice_in_dim(x, length - width, length, axis=dim)
        initial = lax.slice_in_dim(x, 0, width, axis=dim)
        before = lax.ppermute(last, axis, up)
        after = lax.ppermute(initial, axis, down)
        x = jnp.concatenate([before, x, after], axis=dim)
    return x


def on_device(audio, kernel, templates, activations):
    padded = with_halo(audio, (("tm", 0),), HALF)
    frames = activations.shape[1]
    blocks = padded.reshape(frames + 1, HOP)
    dims = (((1,), (1,)), ((), ()))
    spec = lax.dot_general(kernel[:, :HOP], blocks[:-1], dims, preferred_element_type=jnp.float32)
    spec = spec + lax.dot_general(
        kernel[:, HOP:], blocks[1:], dims, preferred_element_type=jnp.float32
    )
    bins = templates.shape[0]
    power = (
        (spec[:bins] * spec[:bins] + spec[bins:] * spec[bins:])
        .astype(jnp.bfloat16)
        .astype(jnp.float32)
    )
    weights = templates
    acts = activations
    for step in range(ITERS):
        model = jnp.dot(weights, acts, preferred_element_type=jnp.float32)
        ratio = (power / model).astype(jnp.bfloat16)
        numer = lax.dot_general(
            weights, ratio, (((0,), (0,)), ((), ())), preferred_element_type=jnp.float32
        )
        colsum = jnp.sum(weights.astype(jnp.float32), axis=0)
        acts = (acts.astype(jnp.float32) * numer / colsum[:, None]).astype(jnp.bfloat16)
        model = jnp.dot(weights, acts, preferred_element_type=jnp.float32)
        ratio_two = (power / model).astype(jnp.bfloat16)
        own_totals = jnp.sum(acts.astype(jnp.float32), axis=1)
        numw = lax.dot_general(
            ratio_two, acts, (((1,), (1,)), ((), ())), preferred_element_type=jnp.float32
        )
        numw, rowsum = lax.psum((numw, own_totals), "tm")
        weights = (weights.astype(jnp.float32) * numw / rowsum[None, :]).astype(jnp.bfloat16)
    return (acts, weights)


def solution(mesh):
    in_specs = (P(("groups", "tm")), P(), P(), P(None, ("groups", "tm")))
    out_specs = (P(None, ("groups", "tm")), P("groups", None))
    return jax.shard_map(
        on_device, mesh=mesh, in_specs=in_specs, out_specs=out_specs, check_vma=False
    )
```

profile of v0, /device:TPU:0, one launch (start us, length us, event | category | flops | bytes accessed | tf_op | source)
XLA Modules:
  0.0 268.2 jit_solution(16667687040819516247)
XLA Ops:
  7.2 0.8 fusion.20
  8.0 2.3 collective-permute-start
  10.4 1.3 collective-permute-start.1
  11.7 1.5 convert_reduce_fusion.1
  13.2 2.3 copy.6
  15.5 0.4 pad_maximum_fusion.1
  15.9 0.7 slice.44
  16.6 0.7 slice.40
  17.3 4.3 %fusion.10 = f32[1024,2304]{1,0:T(8,128)S(1)} fusion(bf16[1024,512]{1,0:T(8,128)(2,1)S(1)} %slice.44, bf16[2304,1024]{1,0:T(8,128)(2,1)} %param.5), kind=kOutput, calls=%fused_computation.23 | convolution fusion | flops 2415919104 | bytes 12845056 | tf_op jit(solution)/shard_map/dot_general | solution.py:30
  21.6 4.5 %add_bitcast_fusion = f32[2304,1024]{0,1:T(8,128)S(1)} fusion(f32[1024,2304]{1,0:T(8,128)S(1)} %fusion.10, bf16[1024,512]{1,0:T(8,128)(2,1)S(1)} %slice.40, bf16[2304,1024]{1,0:T(8,128)(2,1)} %param.5), kind=kOutput, calls=%fused_computation | convolution fusion | flops 2418278400 | bytes 22282240 | tf_op jit(solution)/shard_map/dot_general | solution.py:29
  26.1 2.1 fusion.5
  28.1 0.5 copy-done.4
  28.7 5.6 %convert_reduce_fusion.2 = (f32[512]{0:T(512)S(1)}, bf16[512,1024]{0,1:T(8,128)(2,1)}) fusion(f32[512]{0:T(512)S(1)} %convert_reduce_fusion.1, bf16[1152,512]{1,0:T(8,128)(2,1)S(1)} %copy-done, bf16[1152,1024]{0,1:T(8,128)(2,1)} %fusion.5, bf16[512,1024]{1,0:T(8,128)(2,1)S(1)} %copy-done.3, bf16[512,1024]{0,1:T(8,128)(2,1)S(1)} %copy-done.4), kind=kOutput, calls=%fused_computation.18 | convolution fusion | flops 2422603264 | bytes 6688768 | tf_op jit(solution)/shard_map/dot_general | solution.py:44
  34.3 6.9 %fusion.18 = f32[1152,512]{1,0:T(8,128)} fusion(bf16[512,1024]{0,1:T(8,128)(2,1)} %get-tuple-element.11, bf16[1152,1024]{0,1:T(8,128)(2,1)} %fusion.5, bf16[1152,512]{1,0:T(8,128)(2,1)S(1)} %copy-done), kind=kOutput, calls=%fused_computation.33 | convolution fusion | flops 2419458048 | bytes 6946816 | tf_op jit(solution)/shard_map/dot_general | solution.py:52
  41.3 36.7 %psum.29 = f32[512]{0:T(512)S(1)} all-reduce(f32[512]{0:T(512)S(1)} %get-tuple-element.10), channel_id=1, replica_groups=mesh['groups'=2,'tm'=16] {'tm'}, use_global_device_ids=true, to_apply=%region_3.0 | all-reduce | flops 512 | bytes 4096 | tf_op jit(solution)/shard_map/psum | solution.py:55
  78.0 67.2 %all-reduce.3.cloned.1.call-done = f32[1152,512]{1,0:T(8,128)} async-done(((f32[1152,512]{1,0:T(8,128)}), f32[1152,512]{1,0:T(8,128)}) %all-reduce.3.cloned.1.call-update) | async-done | bytes 2359312 | tf_op jit(solution)/shard_map/psum | solution.py:55
  145.2 2.1 convert_reduce_fusion
  147.3 6.3 %convert_reduce_fusion.3 = (f32[512]{0:T(512)S(1)}, bf16[512,1024]{0,1:T(8,128)(2,1)}) fusion(f32[512]{0:T(512)S(1)} %get-tuple-element.4, bf16[1152,512]{1,0:T(8,128)(2,1)S(1)} %get-tuple-element.5, bf16[1152,1024]{0,1:T(8,128)(2,1)} %fusion.5, bf16[512,1024]{0,1:T(8,128)(2,1)} %get-tuple-element.11), kind=kOutput, calls=%fused_computation.31 | convolution fusion | flops 2422603264 | bytes 5640192 | tf_op jit(solution)/shard_map/dot_general | solution.py:44
  153.6 6.1 %fusion.17 = f32[1152,512]{1,0:T(8,128)} fusion(bf16[512,1024]{0,1:T(8,128)(2,1)} %get-tuple-element.13, bf16[1152,1024]{0,1:T(8,128)(2,1)S(1)} %copy-done.1, bf16[1152,512]{1,0:T(8,128)(2,1)S(1)} %get-tuple-element.5), kind=kOutput, calls=%fused_computation.32 | convolution fusion | flops 2419458048 | bytes 6946816 | tf_op jit(solution)/shard_map/dot_general | solution.py:52
  159.8 1.2 copy-done.5
  161.0 1.3 copy.8
  162.3 30.3 %psum.31 = f32[512]{0:T(512)S(1)} all-reduce(f32[512]{0:T(512)S(1)} %get-tuple-element.12), channel_id=1, replica_groups=mesh['groups'=2,'tm'=16] {'tm'}, use_global_device_ids=true, to_apply=%region_7.0 | all-reduce | flops 512 | bytes 4096 | tf_op jit(solution)/shard_map/psum | solution.py:55
  192.6 65.7 %all-reduce.5.cloned.1.call-done = f32[1152,512]{1,0:T(8,128)} async-done(((f32[1152,512]{1,0:T(8,128)}), f32[1152,512]{1,0:T(8,128)}) %all-reduce.5.cloned.1.call-update) | async-done | bytes 2359312 | tf_op jit(solution)/shard_map/psum | solution.py:55
  258.3 3.1 %fusion.9 = bf16[1152,512]{1,0:T(8,128)(2,1)} fusion(f32[1152,512]{1,0:T(8,128)} %all-reduce.5.cloned.1.call-done, bf16[1152,512]{1,0:T(8,128)(2,1)S(1)} %get-tuple-element.5, f32[512]{0:T(512)S(1)} %psum.31), kind=kLoop, calls=%fused_computation.22 | loop fusion | flops 2359296 | bytes 4720640 | tf_op jit(solution)/shard_map/convert_element_type | solution.py:56
  (16 shorter events, 0.2 us)
Async XLA Ops:
  7.2 8.3 %copy-start.2 = (bf16[524288]{0:T(1024)(128)(2,1)S(1)}, bf16[524288]{0:T(1024)(128)(2,1)}, u32[]{:S(2)}) copy-start(bf16[524288]{0:T(1024)(128)(2,1)} %param.4) | copy-start | bytes 3145732
  7.2 138.0 %all-reduce.3.cloned.1.call-start = ((), (), s32[]{:S(2)}) async-start(), calls=%async_computation | async-start | bytes 4718592 | tf_op jit(solution)/shard_map/psum | solution.py:55
  8.0 7.4 %collective-permute-start = (bf16[256]{0:T(256)(128)(2,1)S(1)}, bf16[256]{0:T(256)(128)(2,1)S(1)}, u32[]{:S(2)}, u32[]{:S(2)}) collective-permute-start(bf16[256]{0:T(256)(128)(2,1)S(1)} %get-tuple-element.8), channel_id=1, source_target_pairs={{0,1},{1,2},{2,3},{3,4},{4,5},{5,6},{6,7},{7,8},{8,9},{9,10},{10,1... | collective-permute-start | bytes 1544 | tf_op jit(solution)/shard_map/ppermute | solution.py:18
  10.4 5.2 %collective-permute-start.1 = (bf16[256]{0:T(256)(128)(2,1)S(1)}, bf16[256]{0:T(256)(128)(2,1)S(1)}, u32[]{:S(2)}, u32[]{:S(2)}) collective-permute-start(bf16[256]{0:T(256)(128)(2,1)S(1)} %get-tuple-element.9), channel_id=1, source_target_pairs={{1,0},{2,1},{3,2},{4,3},{5,4},{6,5},{7,6},{8,7},{9,8},{10,9},{11,1... | collective-permute-start | bytes 1544 | tf_op jit(solution)/shard_map/ppermute | solution.py:19
  26.0 2.1 copy-start
  26.1 2.1 copy-start.3
  26.1 2.6 copy-start.4
  41.2 217.1 %all-reduce.5.cloned.1.call-start = ((), (), s32[]{:S(2)}) async-start(), calls=%async_computation.1 | async-start | bytes 4718592 | tf_op jit(solution)/shard_map/psum | solution.py:55
  147.3 6.3 %copy-start.1 = (bf16[1152,1024]{0,1:T(8,128)(2,1)S(1)}, bf16[1152,1024]{0,1:T(8,128)(2,1)}, u32[]{:S(2)}) copy-start(bf16[1152,1024]{0,1:T(8,128)(2,1)} %fusion.5) | copy-start | bytes 7077892
  159.7 1.2 copy-start.5
Sparse Core Ops, SparseCore 0:
  41.3 103.8 all-reduce.2
  159.9 98.3 all-reduce.4
where the time goes:
time: 269 us; the launch traced here: 268 us
  waiting for transfers between devices  133 us (49%)
  blocking collectives  67.1 us (25%)
  matrix products  33.7 us (13%)
  between operations  14.1 us (5%)
  other arithmetic  9.17 us (3%)
  local copies, waits for them, and re-layouts  7.47 us (3%)
  starting transfers between devices  3.72 us (1%)
    psum x2, waiting for transfers between devices, on_device(): numw, rowsum = lax.psum((numw, own_totals), 'tm')  133 us
    psum x2, blocking collectives, on_device(): numw, rowsum = lax.psum((numw, own_totals), 'tm')  67.1 us
    dot_general x2, matrix products, on_device(): lax.dot_general(ratio_two, acts, (((1,), (1,)), ((), ())), preferred_elem...  13 us
    dot_general x2, matrix products, on_device(): lax.dot_general(weights, ratio, (((0,), (0,)), ((), ())), preferred_eleme...  12 us
  transfers between devices with their start and end apart: 4, of which 3 were waited for; matrix products, arithmetic and copies ran while one was open for 2% of the time, Pallas kernels for 0%

commit v1 on v0

v1 whole, which is shorter than its diff:
```python
import jax
import jax.numpy as jnp
from jax import lax
from jax.sharding import PartitionSpec as P

HOP = 512
ITERS = 2
HALF = 256
HALVES = 2
bf16 = jnp.bfloat16
f32 = jnp.float32


def with_halo(x, axis, width):
    peers, length = lax.axis_size(axis), x.shape[0]
    up = [(i, (i + 1) % peers) for i in range(peers - 1)]
    down = [(j, i) for i, j in up]
    before = lax.ppermute(x[length - width :], axis, up)
    after = lax.ppermute(x[:width], axis, down)
    return jnp.concatenate([before, x, after], axis=0)


def exchanges(peers):
    me = lax.axis_index("tm")
    bits = [1 << b for b in range(peers.bit_length() - 1)]
    even = bits[:]
    odd = bits[:]
    if len(bits) > 2:
        odd[1], odd[2] = bits[2], bits[1]
    steps = []
    for e, o in zip(even, odd):
        bit = jnp.where(me % 2 == 0, (me // e) % 2, (me // o) % 2)
        steps.append((bit, [(i, i ^ (e if i % 2 == 0 else o)) for i in range(peers)]))
    return steps


def swap_totals(totals):
    hi = totals.astype(bf16)
    lo = (totals - hi.astype(f32)).astype(bf16)
    return hi, lo


def scatter_sum(cur, totals, steps, scattered):
    for number, (bit, perm) in enumerate(steps):
        if number < scattered:
            rows = cur.shape[0] // 2
            send = lax.dynamic_slice_in_dim(cur, (1 - bit) * rows, rows, 0).astype(bf16)
            cur = lax.dynamic_slice_in_dim(cur, bit * rows, rows, 0)
        else:
            rows = cur.shape[0]
            send = cur.astype(bf16)
            cur = send.astype(f32)
        if totals is not None:
            hi, lo = swap_totals(totals)
            pad = jnp.zeros((6, hi.shape[0]), bf16)
            send = jnp.concatenate([send, hi[None], lo[None], pad], axis=0)
        got = lax.ppermute(send, "tm", perm)
        cur = cur + got[:rows].astype(f32)
        if totals is not None:
            totals = (hi.astype(f32) + lo.astype(f32)) + (
                got[rows].astype(f32) + got[rows + 1].astype(f32)
            )
    return cur, totals


def gather(part, steps, scattered):
    for bit, perm in reversed(steps[:scattered]):
        got = lax.ppermute(part, "tm", perm)
        part = jnp.where(
            bit == 0,
            jnp.concatenate([part, got], axis=0),
            jnp.concatenate([got, part], axis=0),
        )
    return part


def on_device(audio, kernel, templates, activations):
    peers = lax.axis_size("tm")
    padded = with_halo(audio, "tm", HALF)
    frames = activations.shape[1]
    blocks = padded.reshape(frames + 1, HOP)
    dims = (((1,), (1,)), ((), ()))
    spec = lax.dot_general(kernel[:, :HOP], blocks[:-1], dims, preferred_element_type=f32)
    spec = spec + lax.dot_general(kernel[:, HOP:], blocks[1:], dims, preferred_element_type=f32)
    bins = templates.shape[0]
    power = (spec[:bins] * spec[:bins] + spec[bins:] * spec[bins:]).astype(bf16).astype(f32)
    part = bins // HALVES
    powers = [power[i * part : (i + 1) * part] for i in range(HALVES)]
    weights = [templates[i * part : (i + 1) * part] for i in range(HALVES)]
    steps = exchanges(peers)
    scattered = min(3, len(steps))
    acts = activations
    for step in range(ITERS):
        numer = 0.0
        colsum = 0.0
        for w, p in zip(weights, powers):
            model = jnp.dot(w, acts, preferred_element_type=f32)
            ratio = (p / model).astype(bf16)
            numer = numer + lax.dot_general(
                w, ratio, (((0,), (0,)), ((), ())), preferred_element_type=f32
            )
            colsum = colsum + jnp.sum(w.astype(f32), axis=0)
        acts = (acts.astype(f32) * numer / colsum[:, None]).astype(bf16)
        totals = jnp.sum(acts.astype(f32), axis=1)
        news = []
        for i, (w, p) in enumerate(zip(weights, powers)):
            model = jnp.dot(w, acts, preferred_element_type=f32)
            ratio = (p / model).astype(bf16)
            numw = lax.dot_general(ratio, acts, (((1,), (1,)), ((), ())), preferred_element_type=f32)
            numw, sums = scatter_sum(numw, totals if i == 0 else None, steps, scattered)
            if i == 0:
                rowsum = sums
            own = w
            for bit, _ in steps[:scattered]:
                rows = own.shape[0] // 2
                own = lax.dynamic_slice_in_dim(own, bit * rows, rows, 0)
            own = (own.astype(f32) * numw / rowsum[None, :]).astype(bf16)
            news.append(gather(own, steps, scattered))
        weights = news
    return (acts, jnp.concatenate(weights, axis=0))


def solution(mesh):
    in_specs = (P(("groups", "tm")), P(), P(), P(None, ("groups", "tm")))
    out_specs = (P(None, ("groups", "tm")), P("groups", None))
    return jax.shard_map(
        on_device, mesh=mesh, in_specs=in_specs, out_specs=out_specs, check_vma=False
    )
```

time: 269 us -> 150 us (0.56)
  waiting for transfers between devices: 133 us -> 44.1 us
  blocking collectives: 67.1 us -> 0 us
  starting transfers between devices: 3.72 us -> 34.3 us
  matrix products: 33.7 us -> 50.1 us
  between operations: 14.1 us -> 1.23 us
    psum x2 -> x0, waiting for transfers between devices: 133 us -> none  [on_device(): numw, rowsum = lax.psum((numw, own_totals), 'tm')]
    psum x2 -> x0, blocking collectives: 67.1 us -> none  [on_device(): numw, rowsum = lax.psum((numw, own_totals), 'tm')]
    ppermute x2 -> x30, waiting for transfers between devices: 0.08 us -> 44.1 us  [the longest x16 25.2 us: scatter_sum(): got = lax.ppermute(send, 'tm', perm)]
    ppermute x2 -> x30, starting transfers between devices: 3.64 us -> 34.3 us  [the longest x16 22.6 us: scatter_sum(): got = lax.ppermute(send, 'tm', perm)]
    dot_general x4 -> x8, matrix products: 24.9 us -> 41 us  [the longest x4 21.2 us: on_device(): lax.dot_general(ratio, acts, (((1,), (1,)), ((), ())), preferred_element_...]
    concatenate x1 -> x10, other arithmetic: 0.41 us -> 3.28 us  [the longest x1 2.03 us: with_halo(): return jnp.concatenate([before, x, after], axis=0)]
  transfers between devices with their start and end apart: 4 -> 30, of which waited for: 3 -> 19; matrix products, arithmetic and copies ran while one was open for 2% -> 8% of each run, Pallas kernels for 0% -> 0%
where the time goes in v1:
time: 150 us
  matrix products  50.1 us (33%)
  waiting for transfers between devices  44.1 us (29%)
  starting transfers between devices  34.3 us (23%)
  other arithmetic  10.7 us (7%)
  local copies, waits for them, and re-layouts  9.4 us (6%)
    ppermute x16, waiting for transfers between devices, scatter_sum(): got = lax.ppermute(send, 'tm', perm)  25.2 us
    ppermute x16, starting transfers between devices, scatter_sum(): got = lax.ppermute(send, 'tm', perm)  22.6 us
    dot_general x4, matrix products, on_device(): lax.dot_general(ratio, acts, (((1,), (1,)), ((), ())), preferred_element_...  21.2 us
    dot_general x4, matrix products, on_device(): lax.dot_general(w, ratio, (((0,), (0,)), ((), ())), preferred_element_typ...  19.8 us
    ppermute x12, waiting for transfers between devices, gather(): got = lax.ppermute(part, 'tm', perm)  19 us
    ppermute x12, starting transfers between devices, gather(): got = lax.ppermute(part, 'tm', perm)  8.05 us
    dot_general x1, matrix products, on_device(): lax.dot_general(kernel[:, HOP:], blocks[1:], dims, preferred_element_type...  4.64 us
    dot_general x1, matrix products, on_device(): lax.dot_general(kernel[:, :HOP], blocks[:-1], dims, preferred_element_typ...  4.45 us
  transfers between devices with their start and end apart: 30, of which 19 were waited for; matrix products, arithmetic and copies ran while one was open for 8% of the time, Pallas kernels for 0%

profile of v1, /device:TPU:0, one launch (start us, length us, event | category | flops | bytes accessed | tf_op | source)
XLA Modules:
  0.0 149.8 jit_solution(3632431978119589292)
XLA Ops:
  1.5 2.3 %collective-permute-start = (bf16[256]{0:T(256)(128)(2,1)S(1)}, bf16[256]{0:T(256)(128)(2,1)S(1)}, u32[]{:S(2)}, u32[]{:S(2)}) collective-permute-start(bf16[256]{0:T(256)(128)(2,1)S(1)} %get-tuple-element.26), channel_id=1, source_target_pairs={{0,1},{1,2},{2,3},{3,4},{4,5},{5,6},{6,7},{7,8},{8,9},{9,10},{10,1... | collective-permute-start | bytes 1544 | tf_op jit(solution)/shard_map/ppermute | solution.py:18
  13.3 4.6 %fusion.5 = f32[1024,2304]{1,0:T(8,128)S(1)} fusion(bf16[1024,512]{1,0:T(8,128)(2,1)} %slice.128, bf16[2304,1024]{1,0:T(8,128)(2,1)} %param.5), kind=kOutput, calls=%fused_computation.18 | convolution fusion | flops 2415919104 | bytes 12845056 | tf_op jit(solution)/shard_map/dot_general | solution.py:84
  18.0 4.5 %add_bitcast_fusion = f32[2304,1024]{0,1:T(8,128)S(1)} fusion(f32[1024,2304]{1,0:T(8,128)S(1)} %fusion.5, bf16[1024,512]{1,0:T(8,128)(2,1)S(1)} %slice.124, bf16[2304,1024]{1,0:T(8,128)(2,1)} %param.5), kind=kOutput, calls=%fused_computation | convolution fusion | flops 2418278400 | bytes 22282240 | tf_op jit(solution)/shard_map/dot_general | solution.py:83
  22.4 2.6 %fusion.4 = f32[1152,1024]{0,1:T(8,128)} fusion(f32[2304,1024]{0,1:T(8,128)S(1)} %add_bitcast_fusion), kind=kLoop, calls=%fused_computation.17 | loop fusion | flops 5898240 | bytes 14155776 | tf_op jit(solution)/shard_map/convert_element_type | solution.py:86
  25.1 5.1 %fusion.12 = f32[1024,512]{1,0:T(8,128)} fusion(f32[1152,1024]{0,1:T(8,128)} %fusion.4, bf16[512,1024]{1,0:T(8,128)(2,1)S(1)} %copy-done.2, bf16[1152,512]{1,0:T(8,128)(2,1)S(1)} %copy-done), kind=kOutput, calls=%fused_computation.27 | convolution fusion | flops 1209139200 | bytes 6946816 | tf_op jit(solution)/shard_map/dot_general | solution.py:99
  30.1 5.3 %convert_reduce_fusion = (f32[512]{0:T(512)S(1)}, bf16[512,1024]{0,1:T(8,128)(2,1)}) fusion(f32[512]{0:T(512)S(1)} %add.348, f32[1024,512]{1,0:T(8,128)} %fusion.12, bf16[1152,512]{1,0:T(8,128)(2,1)S(1)} %copy-done, f32[1152,1024]{0,1:T(8,128)} %fusion.4, bf16[512,1024]{1,0:T(8,128)(2,1)S(1)} %copy-done.2, bf16[512,1024]{0,1:T(8,128)(2,1)S(1)} %copy-done.3), kind=kOutput, calls=%fused_computation.6 | convolution fusion | flops 1212808704 | bytes 9048064 | tf_op jit(solution)/shard_map/dot_general | solution.py:99
  35.5 5.1 %fusion.16 = f32[576,512]{1,0:T(8,128)S(1)} fusion(bf16[512,1024]{0,1:T(8,128)(2,1)} %get-tuple-element.33, f32[1152,1024]{0,1:T(8,128)} %fusion.4, bf16[1152,512]{1,0:T(8,128)(2,1)S(1)} %copy-done), kind=kOutput, calls=%fused_computation.31 | convolution fusion | flops 1209139200 | bytes 6488064 | tf_op jit(solution)/shard_map/dot_general | solution.py:109
  40.5 5.9 %fusion.17 = f32[576,512]{1,0:T(8,128)} fusion(bf16[512,1024]{0,1:T(8,128)(2,1)S(1)} %copy-done.6, f32[1152,1024]{0,1:T(8,128)} %fusion.4, bf16[1152,512]{1,0:T(8,128)(2,1)S(1)} %copy-done), kind=kOutput, calls=%fused_computation.32 | convolution fusion | flops 1209139200 | bytes 6488064 | tf_op jit(solution)/shard_map/dot_general | solution.py:109
  47.7 3.3 %collective-permute-start.9 = (bf16[288,512]{1,0:T(8,128)(2,1)S(1)}, bf16[288,512]{1,0:T(8,128)(2,1)S(1)}, u32[]{:S(2)}, u32[]{:S(2)}) collective-permute-start(bf16[288,512]{1,0:T(8,128)(2,1)S(1)} %dynamic-slice_convert_fusion.2), channel_id=1, source_target_pairs={{0,1},{1,0},{2,3},{3,2},{4,5},{5,4},{6,7},{7,6},{8,9},{9,8},{10,11... | collective-permute-start | bytes 884744 | tf_op jit(solution)/shard_map/ppermute | solution.py:57
  54.9 2.8 %collective-permute-done.10 = bf16[144,512]{1,0:T(8,128)(2,1)S(1)} collective-permute-done((bf16[144,512]{1,0:T(8,128)(2,1)S(1)}, bf16[144,512]{1,0:T(8,128)(2,1)S(1)}, u32[]{:S(2)}, u32[]{:S(2)}) %collective-permute-start.10) | collective-permute-done | bytes 147488 | tf_op jit(solution)/shard_map/ppermute | solution.py:57
  65.0 3.1 %collective-permute-start.5 = (bf16[80,512]{1,0:T(8,128)(2,1)S(1)}, bf16[80,512]{1,0:T(8,128)(2,1)S(1)}, u32[]{:S(2)}, u32[]{:S(2)}) collective-permute-start(bf16[80,512]{1,0:T(8,128)(2,1)S(1)} %pad_maximum_fusion.9), channel_id=1, source_target_pairs={{0,8},{1,9},{2,10},{3,11},{4,12},{5,13},{6,14},{7,15},{8,0},{9,1},... | collective-permute-start | bytes 245768 | tf_op jit(solution)/shard_map/ppermute | solution.py:57
  70.4 2.6 %collective-permute-done.5 = bf16[80,512]{1,0:T(8,128)(2,1)S(1)} collective-permute-done((bf16[80,512]{1,0:T(8,128)(2,1)S(1)}, bf16[80,512]{1,0:T(8,128)(2,1)S(1)}, u32[]{:S(2)}, u32[]{:S(2)}) %collective-permute-start.5) | collective-permute-done | bytes 81952 | tf_op jit(solution)/shard_map/ppermute | solution.py:57
  76.2 3.9 %collective-permute-done.13 = bf16[72,512]{1,0:T(8,128)(2,1)S(1)} collective-permute-done((bf16[72,512]{1,0:T(8,128)(2,1)S(1)}, bf16[72,512]{1,0:T(8,128)(2,1)S(1)}, u32[]{:S(2)}, u32[]{:S(2)}) %collective-permute-start.13) | collective-permute-done | bytes 73760 | tf_op jit(solution)/shard_map/ppermute | solution.py:68
  81.9 3.5 %collective-permute-done.14 = bf16[144,512]{1,0:T(8,128)(2,1)S(1)} collective-permute-done((bf16[144,512]{1,0:T(8,128)(2,1)S(1)}, bf16[144,512]{1,0:T(8,128)(2,1)S(1)}, u32[]{:S(2)}, u32[]{:S(2)}) %collective-permute-start.14) | collective-permute-done | bytes 147488 | tf_op jit(solution)/shard_map/ppermute | solution.py:68
  86.8 4.1 %collective-permute-done.7 = bf16[144,512]{1,0:T(8,128)(2,1)S(1)} collective-permute-done((bf16[144,512]{1,0:T(8,128)(2,1)S(1)}, bf16[144,512]{1,0:T(8,128)(2,1)S(1)}, u32[]{:S(2)}, u32[]{:S(2)}) %collective-permute-start.7) | collective-permute-done | bytes 147488 | tf_op jit(solution)/shard_map/ppermute | solution.py:68
  91.3 5.0 %fusion.13 = f32[512,1024]{0,1:T(8,128)} fusion(bf16[576,512]{1,0:T(8,128)(2,1)S(1)} %get-tuple-element.13, f32[1152,1024]{0,1:T(8,128)} %fusion.4, bf16[512,1024]{0,1:T(8,128)(2,1)S(1)} %copy-done.7), kind=kOutput, calls=%fused_computation.28 | convolution fusion | flops 1209139200 | bytes 6946816 | tf_op jit(solution)/shard_map/dot_general | solution.py:99
  96.6 4.4 %convert_reduce_fusion.1 = (f32[512]{0:T(512)S(1)}, bf16[512,1024]{0,1:T(8,128)(2,1)S(1)}) fusion(f32[512]{0:T(512)S(1)} %add.379, f32[512,1024]{0,1:T(8,128)} %fusion.13, bf16[576,512]{1,0:T(8,128)(2,1)S(1)} %get-tuple-element.15, f32[1152,1024]{0,1:T(8,128)} %fusion.4, bf16[512,1024]{0,1:T(8,128)(2,1)S(1)} %copy-done.7), kind=kOutput, calls=%fused_computation.26 | convolution fusion | flops 1212808704 | bytes 9048064 | tf_op jit(solution)/shard_map/dot_general | solution.py:99
  100.9 4.4 %fusion.14 = f32[576,512]{1,0:T(8,128)S(1)} fusion(bf16[512,1024]{0,1:T(8,128)(2,1)S(1)} %get-tuple-element.35, f32[1152,1024]{0,1:T(8,128)} %fusion.4, bf16[576,512]{1,0:T(8,128)(2,1)S(1)} %get-tuple-element.15), kind=kOutput, calls=%fused_computation.29 | convolution fusion | flops 1209139200 | bytes 6488064 | tf_op jit(solution)/shard_map/dot_general | solution.py:109
  105.3 5.9 %fusion.15 = f32[576,512]{1,0:T(8,128)} fusion(bf16[512,1024]{0,1:T(8,128)(2,1)S(1)} %get-tuple-element.35, f32[1152,1024]{0,1:T(8,128)} %fusion.4, bf16[576,512]{1,0:T(8,128)(2,1)S(1)} %get-tuple-element.13), kind=kOutput, calls=%fused_computation.30 | convolution fusion | flops 1209139200 | bytes 6488064 | tf_op jit(solution)/shard_map/dot_general | solution.py:109
  116.7 2.9 %collective-permute-done.24 = bf16[144,512]{1,0:T(8,128)(2,1)S(1)} collective-permute-done((bf16[144,512]{1,0:T(8,128)(2,1)S(1)}, bf16[144,512]{1,0:T(8,128)(2,1)S(1)}, u32[]{:S(2)}, u32[]{:S(2)}) %collective-permute-start.24) | collective-permute-done | bytes 147488 | tf_op jit(solution)/shard_map/ppermute | solution.py:57
  127.6 2.6 %collective-permute-start.26 = (bf16[72,512]{1,0:T(8,128)(2,1)S(1)}, bf16[72,512]{1,0:T(8,128)(2,1)S(1)}, u32[]{:S(2)}, u32[]{:S(2)}) collective-permute-start(bf16[72,512]{1,0:T(8,128)(2,1)S(1)} %add_convert_fusion), channel_id=1, source_target_pairs={{0,8},{1,9},{2,10},{3,11},{4,12},{5,13},{6,14},{7,15},{8,0},{9,1},... | collective-permute-start | bytes 221192 | tf_op jit(solution)/shard_map/ppermute | solution.py:57
  130.2 2.9 %collective-permute-done.19 = bf16[80,512]{1,0:T(8,128)(2,1)S(1)} collective-permute-done((bf16[80,512]{1,0:T(8,128)(2,1)S(1)}, bf16[80,512]{1,0:T(8,128)(2,1)S(1)}, u32[]{:S(2)}, u32[]{:S(2)}) %collective-permute-start.19) | collective-permute-done | bytes 81952 | tf_op jit(solution)/shard_map/ppermute | solution.py:57
  136.9 3.1 %collective-permute-done.27 = bf16[72,512]{1,0:T(8,128)(2,1)S(1)} collective-permute-done((bf16[72,512]{1,0:T(8,128)(2,1)S(1)}, bf16[72,512]{1,0:T(8,128)(2,1)S(1)}, u32[]{:S(2)}, u32[]{:S(2)}) %collective-permute-start.27) | collective-permute-done | bytes 73760 | tf_op jit(solution)/shard_map/ppermute | solution.py:68
  142.7 2.5 %collective-permute-done.28 = bf16[144,512]{1,0:T(8,128)(2,1)S(1)} collective-permute-done((bf16[144,512]{1,0:T(8,128)(2,1)S(1)}, bf16[144,512]{1,0:T(8,128)(2,1)S(1)}, u32[]{:S(2)}, u32[]{:S(2)}) %collective-permute-start.28) | collective-permute-done | bytes 147488 | tf_op jit(solution)/shard_map/ppermute | solution.py:68
  (139 shorter events, 56.2 us)
Async XLA Ops:
  1.5 7.7 %collective-permute-start = (bf16[256]{0:T(256)(128)(2,1)S(1)}, bf16[256]{0:T(256)(128)(2,1)S(1)}, u32[]{:S(2)}, u32[]{:S(2)}) collective-permute-start(bf16[256]{0:T(256)(128)(2,1)S(1)} %get-tuple-element.26), channel_id=1, source_target_pairs={{0,1},{1,2},{2,3},{3,4},{4,5},{5,6},{6,7},{7,8},{8,9},{9,10},{10,1... | collective-permute-start | bytes 1544 | tf_op jit(solution)/shard_map/ppermute | solution.py:18
  3.9 5.3 %collective-permute-start.1 = (bf16[256]{0:T(256)(128)(2,1)S(1)}, bf16[256]{0:T(256)(128)(2,1)S(1)}, u32[]{:S(2)}, u32[]{:S(2)}) collective-permute-start(bf16[256]{0:T(256)(128)(2,1)S(1)} %get-tuple-element.27), channel_id=1, source_target_pairs={{1,0},{2,1},{3,2},{4,3},{5,4},{6,5},{7,6},{8,7},{9,8},{10,9},{11,1... | collective-permute-start | bytes 1544 | tf_op jit(solution)/shard_map/ppermute | solution.py:19
  47.7 4.5 %collective-permute-start.9 = (bf16[288,512]{1,0:T(8,128)(2,1)S(1)}, bf16[288,512]{1,0:T(8,128)(2,1)S(1)}, u32[]{:S(2)}, u32[]{:S(2)}) collective-permute-start(bf16[288,512]{1,0:T(8,128)(2,1)S(1)} %dynamic-slice_convert_fusion.2), channel_id=1, source_target_pairs={{0,1},{1,0},{2,3},{3,2},{4,5},{5,4},{6,7},{7,6},{8,9},{9,8},{10,11... | collective-permute-start | bytes 884744 | tf_op jit(solution)/shard_map/ppermute | solution.py:57
  52.5 5.2 %collective-permute-start.10 = (bf16[144,512]{1,0:T(8,128)(2,1)S(1)}, bf16[144,512]{1,0:T(8,128)(2,1)S(1)}, u32[]{:S(2)}, u32[]{:S(2)}) collective-permute-start(bf16[144,512]{1,0:T(8,128)(2,1)S(1)} %dynamic-slice_convert_fusion.6), channel_id=1, source_target_pairs={{0,2},{1,5},{2,0},{3,7},{4,6},{5,1},{6,4},{7,3},{8,10},{9,13},{10,... | collective-permute-start | bytes 442376 | tf_op jit(solution)/shard_map/ppermute | solution.py:57
  54.8 5.3 %collective-permute-start.3 = (bf16[152,512]{1,0:T(8,128)(2,1)S(1)}, bf16[152,512]{1,0:T(8,128)(2,1)S(1)}, u32[]{:S(2)}, u32[]{:S(2)}) collective-permute-start(bf16[152,512]{1,0:T(8,128)(2,1)S(1)} %pad_maximum_fusion.6), channel_id=1, source_target_pairs={{0,2},{1,5},{2,0},{3,7},{4,6},{5,1},{6,4},{7,3},{8,10},{9,13},{10,... | collective-permute-start | bytes 466952 | tf_op jit(solution)/shard_map/ppermute | solution.py:57
  60.2 4.8 %collective-permute-start.4 = (bf16[80,512]{1,0:T(8,128)(2,1)S(1)}, bf16[80,512]{1,0:T(8,128)(2,1)S(1)}, u32[]{:S(2)}, u32[]{:S(2)}) collective-permute-start(bf16[80,512]{1,0:T(8,128)(2,1)S(1)} %pad_maximum_fusion.10), channel_id=1, source_target_pairs={{0,4},{1,3},{2,6},{3,1},{4,0},{5,7},{6,2},{7,5},{8,12},{9,11},{10,... | collective-permute-start | bytes 245768 | tf_op jit(solution)/shard_map/ppermute | solution.py:57
  62.5 5.6 %collective-permute-start.11 = (bf16[72,512]{1,0:T(8,128)(2,1)S(1)}, bf16[72,512]{1,0:T(8,128)(2,1)S(1)}, u32[]{:S(2)}, u32[]{:S(2)}) collective-permute-start(bf16[72,512]{1,0:T(8,128)(2,1)S(1)} %dynamic-slice_convert_fusion.10), channel_id=1, source_target_pairs={{0,4},{1,3},{2,6},{3,1},{4,0},{5,7},{6,2},{7,5},{8,12},{9,11},{10,... | collective-permute-start | bytes 221192 | tf_op jit(solution)/shard_map/ppermute | solution.py:57
  65.0 8.0 %collective-permute-start.5 = (bf16[80,512]{1,0:T(8,128)(2,1)S(1)}, bf16[80,512]{1,0:T(8,128)(2,1)S(1)}, u32[]{:S(2)}, u32[]{:S(2)}) collective-permute-start(bf16[80,512]{1,0:T(8,128)(2,1)S(1)} %pad_maximum_fusion.9), channel_id=1, source_target_pairs={{0,8},{1,9},{2,10},{3,11},{4,12},{5,13},{6,14},{7,15},{8,0},{9,1},... | collective-permute-start | bytes 245768 | tf_op jit(solution)/shard_map/ppermute | solution.py:57
  68.2 6.5 %collective-permute-start.12 = (bf16[72,512]{1,0:T(8,128)(2,1)S(1)}, bf16[72,512]{1,0:T(8,128)(2,1)S(1)}, u32[]{:S(2)}, u32[]{:S(2)}) collective-permute-start(bf16[72,512]{1,0:T(8,128)(2,1)S(1)} %add_convert_fusion.2), channel_id=1, source_target_pairs={{0,8},{1,9},{2,10},{3,11},{4,12},{5,13},{6,14},{7,15},{8,0},{9,1},... | collective-permute-start | bytes 221192 | tf_op jit(solution)/shard_map/ppermute | solution.py:57
  75.7 4.5 %collective-permute-start.13 = (bf16[72,512]{1,0:T(8,128)(2,1)S(1)}, bf16[72,512]{1,0:T(8,128)(2,1)S(1)}, u32[]{:S(2)}, u32[]{:S(2)}) collective-permute-start(bf16[72,512]{1,0:T(8,128)(2,1)S(1)} %get-tuple-element.31), channel_id=1, source_target_pairs={{0,4},{1,3},{2,6},{3,1},{4,0},{5,7},{6,2},{7,5},{8,12},{9,11},{10,... | collective-permute-start | bytes 221192 | tf_op jit(solution)/shard_map/ppermute | solution.py:68
  80.2 5.2 %collective-permute-start.14 = (bf16[144,512]{1,0:T(8,128)(2,1)S(1)}, bf16[144,512]{1,0:T(8,128)(2,1)S(1)}, u32[]{:S(2)}, u32[]{:S(2)}) collective-permute-start(bf16[144,512]{1,0:T(8,128)(2,1)S(1)} %maximum_select_fusion.9), channel_id=1, source_target_pairs={{0,2},{1,5},{2,0},{3,7},{4,6},{5,1},{6,4},{7,3},{8,10},{9,13},{10,... | collective-permute-start | bytes 442376 | tf_op jit(solution)/shard_map/ppermute | solution.py:68
  80.3 5.3 %collective-permute-start.6 = (bf16[72,512]{1,0:T(8,128)(2,1)S(1)}, bf16[72,512]{1,0:T(8,128)(2,1)S(1)}, u32[]{:S(2)}, u32[]{:S(2)}) collective-permute-start(bf16[72,512]{1,0:T(8,128)(2,1)S(1)} %get-tuple-element.30), channel_id=1, source_target_pairs={{0,4},{1,3},{2,6},{3,1},{4,0},{5,7},{6,2},{7,5},{8,12},{9,11},{10,... | collective-permute-start | bytes 221192 | tf_op jit(solution)/shard_map/ppermute | solution.py:68
  85.5 5.5 %collective-permute-start.15 = (bf16[288,512]{1,0:T(8,128)(2,1)S(1)}, bf16[288,512]{1,0:T(8,128)(2,1)S(1)}, u32[]{:S(2)}, u32[]{:S(2)}) collective-permute-start(bf16[288,512]{1,0:T(8,128)(2,1)S(1)} %maximum_select_fusion.5), channel_id=1, source_target_pairs={{0,1},{1,0},{2,3},{3,2},{4,5},{5,4},{6,7},{7,6},{8,9},{9,8},{10,11... | collective-permute-start | bytes 884744 | tf_op jit(solution)/shard_map/ppermute | solution.py:68
  85.6 5.2 %collective-permute-start.7 = (bf16[144,512]{1,0:T(8,128)(2,1)S(1)}, bf16[144,512]{1,0:T(8,128)(2,1)S(1)}, u32[]{:S(2)}, u32[]{:S(2)}) collective-permute-start(bf16[144,512]{1,0:T(8,128)(2,1)S(1)} %maximum_select_fusion.8), channel_id=1, source_target_pairs={{0,2},{1,5},{2,0},{3,7},{4,6},{5,1},{6,4},{7,3},{8,10},{9,13},{10,... | collective-permute-start | bytes 442376 | tf_op jit(solution)/shard_map/ppermute | solution.py:68
  90.9 5.4 %collective-permute-start.8 = (bf16[288,512]{1,0:T(8,128)(2,1)S(1)}, bf16[288,512]{1,0:T(8,128)(2,1)S(1)}, u32[]{:S(2)}, u32[]{:S(2)}) collective-permute-start(bf16[288,512]{1,0:T(8,128)(2,1)S(1)} %maximum_select_fusion.4), channel_id=1, source_target_pairs={{0,1},{1,0},{2,3},{3,2},{4,5},{5,4},{6,7},{7,6},{8,9},{9,8},{10,11... | collective-permute-start | bytes 884744 | tf_op jit(solution)/shard_map/ppermute | solution.py:68
  114.4 5.2 %collective-permute-start.24 = (bf16[144,512]{1,0:T(8,128)(2,1)S(1)}, bf16[144,512]{1,0:T(8,128)(2,1)S(1)}, u32[]{:S(2)}, u32[]{:S(2)}) collective-permute-start(bf16[144,512]{1,0:T(8,128)(2,1)S(1)} %dynamic-slice_convert_fusion.4), channel_id=1, source_target_pairs={{0,2},{1,5},{2,0},{3,7},{4,6},{5,1},{6,4},{7,3},{8,10},{9,13},{10,... | collective-permute-start | bytes 442376 | tf_op jit(solution)/shard_map/ppermute | solution.py:57
  115.6 5.6 %collective-permute-start.17 = (bf16[152,512]{1,0:T(8,128)(2,1)S(1)}, bf16[152,512]{1,0:T(8,128)(2,1)S(1)}, u32[]{:S(2)}, u32[]{:S(2)}) collective-permute-start(bf16[152,512]{1,0:T(8,128)(2,1)S(1)} %pad_maximum_fusion.5), channel_id=1, source_target_pairs={{0,2},{1,5},{2,0},{3,7},{4,6},{5,1},{6,4},{7,3},{8,10},{9,13},{10,... | collective-permute-start | bytes 466952 | tf_op jit(solution)/shard_map/ppermute | solution.py:57
  122.2 5.4 %collective-permute-start.25 = (bf16[72,512]{1,0:T(8,128)(2,1)S(1)}, bf16[72,512]{1,0:T(8,128)(2,1)S(1)}, u32[]{:S(2)}, u32[]{:S(2)}) collective-permute-start(bf16[72,512]{1,0:T(8,128)(2,1)S(1)} %dynamic-slice_convert_fusion.8), channel_id=1, source_target_pairs={{0,4},{1,3},{2,6},{3,1},{4,0},{5,7},{6,2},{7,5},{8,12},{9,11},{10,... | collective-permute-start | bytes 221192 | tf_op jit(solution)/shard_map/ppermute | solution.py:57
  125.9 7.2 %collective-permute-start.19 = (bf16[80,512]{1,0:T(8,128)(2,1)S(1)}, bf16[80,512]{1,0:T(8,128)(2,1)S(1)}, u32[]{:S(2)}, u32[]{:S(2)}) collective-permute-start(bf16[80,512]{1,0:T(8,128)(2,1)S(1)} %pad_maximum_fusion.7), channel_id=1, source_target_pairs={{0,8},{1,9},{2,10},{3,11},{4,12},{5,13},{6,14},{7,15},{8,0},{9,1},... | collective-permute-start | bytes 245768 | tf_op jit(solution)/shard_map/ppermute | solution.py:57
  127.6 7.1 %collective-permute-start.26 = (bf16[72,512]{1,0:T(8,128)(2,1)S(1)}, bf16[72,512]{1,0:T(8,128)(2,1)S(1)}, u32[]{:S(2)}, u32[]{:S(2)}) collective-permute-start(bf16[72,512]{1,0:T(8,128)(2,1)S(1)} %add_convert_fusion), channel_id=1, source_target_pairs={{0,8},{1,9},{2,10},{3,11},{4,12},{5,13},{6,14},{7,15},{8,0},{9,1},... | collective-permute-start | bytes 221192 | tf_op jit(solution)/shard_map/ppermute | solution.py:57
  134.8 5.2 %collective-permute-start.27 = (bf16[72,512]{1,0:T(8,128)(2,1)S(1)}, bf16[72,512]{1,0:T(8,128)(2,1)S(1)}, u32[]{:S(2)}, u32[]{:S(2)}) collective-permute-start(bf16[72,512]{1,0:T(8,128)(2,1)S(1)} %get-tuple-element.29), channel_id=1, source_target_pairs={{0,4},{1,3},{2,6},{3,1},{4,0},{5,7},{6,2},{7,5},{8,12},{9,11},{10,... | collective-permute-start | bytes 221192 | tf_op jit(solution)/shard_map/ppermute | solution.py:68
  135.2 6.3 %collective-permute-start.20 = (bf16[72,512]{1,0:T(8,128)(2,1)S(1)}, bf16[72,512]{1,0:T(8,128)(2,1)S(1)}, u32[]{:S(2)}, u32[]{:S(2)}) collective-permute-start(bf16[72,512]{1,0:T(8,128)(2,1)S(1)} %get-tuple-element.28), channel_id=1, source_target_pairs={{0,4},{1,3},{2,6},{3,1},{4,0},{5,7},{6,2},{7,5},{8,12},{9,11},{10,... | collective-permute-start | bytes 221192 | tf_op jit(solution)/shard_map/ppermute | solution.py:68
  140.0 5.2 %collective-permute-start.28 = (bf16[144,512]{1,0:T(8,128)(2,1)S(1)}, bf16[144,512]{1,0:T(8,128)(2,1)S(1)}, u32[]{:S(2)}, u32[]{:S(2)}) collective-permute-start(bf16[144,512]{1,0:T(8,128)(2,1)S(1)} %maximum_select_fusion.11), channel_id=1, source_target_pairs={{0,2},{1,5},{2,0},{3,7},{4,6},{5,1},{6,4},{7,3},{8,10},{9,13},{10,... | collective-permute-start | bytes 442376 | tf_op jit(solution)/shard_map/ppermute | solution.py:68
  141.6 5.2 %collective-permute-start.21 = (bf16[144,512]{1,0:T(8,128)(2,1)S(1)}, bf16[144,512]{1,0:T(8,128)(2,1)S(1)}, u32[]{:S(2)}, u32[]{:S(2)}) collective-permute-start(bf16[144,512]{1,0:T(8,128)(2,1)S(1)} %maximum_select_fusion.10), channel_id=1, source_target_pairs={{0,2},{1,5},{2,0},{3,7},{4,6},{5,1},{6,4},{7,3},{8,10},{9,13},{10,... | collective-permute-start | bytes 442376 | tf_op jit(solution)/shard_map/ppermute | solution.py:68
  (14 other events, 78.0 us)

commit v2 on v1

v2 whole, which is shorter than its diff:
```python
import functools

import jax
import jax.numpy as jnp
from jax import lax
from jax.experimental import pallas as pl
from jax.experimental.pallas import tpu as pltpu
from jax.sharding import PartitionSpec as P

HOP = 512
ITERS = 2
HALF = 256
TILE = 256
bf16 = jnp.bfloat16
f32 = jnp.float32
NT = (((1,), (1,)), ((), ()))


def inverse(x):
    r = pl.reciprocal(x, approx=True)
    return r * (2.0 - x * r)


def dot(a, b):
    return jnp.dot(a, b, preferred_element_type=f32)


def dot_nt(a, b):
    return lax.dot_general(a, b, NT, preferred_element_type=f32)


def row_blocks(rows):
    first = rows % TILE
    cuts = [0] + list(range(first + TILE if first else TILE, rows + 1, TILE))
    return list(zip(cuts[:-1], cuts[1:]))


def analyse_kernel(bins, cut, a_ref, halo_ref, k_ref, w_ref, h_ref, pa_ref, pb_ref, new_ref,
                   wide, frame, wt):
    frames = a_ref.shape[0]
    wide[8 : 8 + frames, :] = a_ref[...].astype(f32)
    wide[7:8, HALF:] = halo_ref[0:1, :]
    wide[8 + frames : 9 + frames, :HALF] = halo_ref[1:2, :]
    frame[:, HALF : HALF + HOP] = a_ref[...]
    frame[:, :HALF] = wide[7 : 7 + frames, HALF:].astype(bf16)
    frame[:, HALF + HOP :] = wide[9 : 9 + frames, :HALF].astype(bf16)
    wt[...] = w_ref[...].T
    inv = inverse(jnp.sum(wt[...].astype(f32), axis=1, keepdims=True))

    def body(i, _):
        tile = pl.ds(pl.multiple_of(i * TILE, TILE), TILE)
        f = frame[tile, :]
        h = h_ref[:, tile]
        numer = None
        for lo, hi in row_blocks(bins):
            re = dot_nt(k_ref[lo:hi, :], f)
            im = dot_nt(k_ref[bins + lo : bins + hi, :], f)
            p = (re * re + im * im).astype(bf16)
            if hi <= cut:
                pa_ref[lo:hi, tile] = p
            else:
                pb_ref[lo - cut : hi - cut, tile] = p
            model = dot(w_ref[lo:hi, :], h)
            ratio = (p.astype(f32) * inverse(model)).astype(bf16)
            part = dot(wt[:, lo:hi], ratio)
            numer = part if numer is None else numer + part
        new_ref[:, tile] = (h.astype(f32) * numer * inv).astype(bf16)
        return 0

    lax.fori_loop(0, frames // TILE, body, 0)


def template_kernel(p_ref, w_ref, h_ref, numw_ref, *tot_ref):
    frames = h_ref.shape[1]
    for lo, hi in row_blocks(p_ref.shape[0]):
        acc = None
        for t in range(0, frames, TILE):
            h = h_ref[:, t : t + TILE]
            model = dot(w_ref[lo:hi, :], h)
            ratio = (p_ref[lo:hi, t : t + TILE].astype(f32) * inverse(model)).astype(bf16)
            part = dot_nt(ratio, h)
            acc = part if acc is None else acc + part
        numw_ref[lo:hi, :] = acc
    if tot_ref:
        ones = jnp.ones((16, frames), bf16)
        tot_ref[0][...] = dot_nt(ones, h_ref[...])[:8]


def activation_kernel(first, p_ref, w_ref, h_ref, *refs):
    if first:
        numer_ref, col_ref, wt = refs
    else:
        old_ref, oldcol_ref, new_ref, wt = refs
    frames = h_ref.shape[1]
    wt[...] = w_ref[...].T
    col = jnp.sum(wt[...].astype(f32), axis=1, keepdims=True)
    if first:
        col_ref[...] = jnp.broadcast_to(col, col_ref.shape)
    else:
        inv = inverse(col + oldcol_ref[:, :1])
    for t in range(0, frames, TILE):
        tile = slice(t, t + TILE)
        h = h_ref[:, tile]
        numer = None if first else old_ref[:, tile]
        for lo, hi in row_blocks(p_ref.shape[0]):
            model = dot(w_ref[lo:hi, :], h)
            ratio = (p_ref[lo:hi, tile].astype(f32) * inverse(model)).astype(bf16)
            part = dot(wt[:, lo:hi], ratio)
            numer = part if numer is None else numer + part
        if first:
            numer_ref[:, tile] = numer
        else:
            new_ref[:, tile] = (h.astype(f32) * numer * inv).astype(bf16)


VMEM = pl.BlockSpec(memory_space=pltpu.VMEM)


def call(kernel, outs, scratch, flops, *args):
    size = sum(a.size * a.dtype.itemsize for a in args)
    size += sum(o.size * o.dtype.itemsize for o in outs)
    return pl.pallas_call(
        kernel,
        out_shape=tuple(outs),
        in_specs=[VMEM] * len(args),
        out_specs=tuple([VMEM] * len(outs)),
        scratch_shapes=scratch,
        cost_estimate=pl.CostEstimate(flops=flops, bytes_accessed=size, transcendentals=0),
        compiler_params=pltpu.CompilerParams(vmem_limit_bytes=40 * 1024 * 1024),
    )(*args)


def shape(dims, dtype):
    return jax.ShapeDtypeStruct(dims, dtype)


def analyse(audio, halo, kernel, weights, acts, cut):
    bins, comps = weights.shape
    frames = acts.shape[1]
    return call(
        functools.partial(analyse_kernel, bins, cut),
        [shape((cut, frames), bf16), shape((bins - cut, frames), bf16), shape((comps, frames), bf16)],
        [
            pltpu.VMEM((frames + 16, HOP), f32),
            pltpu.VMEM((frames, 2 * HOP), bf16),
            pltpu.VMEM((comps, bins), bf16),
        ],
        2 * bins * frames * (4 * HOP + 2 * comps),
        audio, halo, kernel, weights, acts,
    )


def template_numerator(power, weights, acts, with_totals):
    bins, comps = weights.shape
    outs = [shape((bins, comps), f32)] + ([shape((8, comps), f32)] if with_totals else [])
    return call(template_kernel, outs, [], 4 * power.size * comps, power, weights, acts)


def activation_numerator(power, weights, acts):
    bins, comps = weights.shape
    return call(
        functools.partial(activation_kernel, True),
        [shape(acts.shape, f32), shape((comps, 128), f32)],
        [pltpu.VMEM((comps, bins), bf16)],
        4 * power.size * comps, power, weights, acts,
    )


def new_activations(power, weights, acts, numer, colsum):
    bins, comps = weights.shape
    return call(
        functools.partial(activation_kernel, False),
        [shape(acts.shape, bf16)],
        [pltpu.VMEM((comps, bins), bf16)],
        4 * power.size * comps, power, weights, acts, numer, colsum,
    )[0]


def halo_rows(audio, peers):
    me = lax.axis_index("tm")
    odd = me % 2 == 1
    head, tail = audio[:HALF], audio[audio.shape[0] - HALF :]
    inner = [(i, i ^ 1) for i in range(peers)]
    outer = [(i, (i + 1) % peers if i % 2 else (i - 1) % peers) for i in range(peers)]
    one = lax.ppermute(jnp.where(odd, head, tail), "tm", inner)
    two = lax.ppermute(jnp.where(odd, tail, head), "tm", outer)
    zero = jnp.zeros_like(two)
    two = jnp.where((me == 0) | (me == peers - 1), zero, two)
    left = jnp.where(odd, one, two)
    right = jnp.where(odd, two, one)
    return jnp.stack([left, right]).astype(f32)


def exchanges(peers):
    me = lax.axis_index("tm")
    even = [1 << b for b in range(peers.bit_length() - 1)]
    odd = even[:]
    if len(even) > 2:
        odd[1], odd[2] = even[2], even[1]
    steps = []
    for e, o in zip(even, odd):
        bit = jnp.where(me % 2 == 0, (me // e) % 2, (me // o) % 2)
        steps.append((bit, [(i, i ^ (e if i % 2 == 0 else o)) for i in range(peers)]))
    return steps


def scatter_sum(cur, totals, steps, scattered):
    for number, (bit, perm) in enumerate(steps):
        if number < scattered:
            rows = cur.shape[0] // 2
            send = lax.dynamic_slice_in_dim(cur, (1 - bit) * rows, rows, 0).astype(bf16)
            cur = lax.dynamic_slice_in_dim(cur, bit * rows, rows, 0)
        else:
            rows = cur.shape[0]
            send = cur.astype(bf16)
            cur = send.astype(f32)
        if totals is not None:
            hi = totals.astype(bf16)
            lo = (totals - hi.astype(f32)).astype(bf16)
            pad = jnp.zeros((6, hi.shape[0]), bf16)
            send = jnp.concatenate([send, hi[None], lo[None], pad], axis=0)
        got = lax.ppermute(send, "tm", perm)
        cur = cur + got[:rows].astype(f32)
        if totals is not None:
            totals = (hi.astype(f32) + lo.astype(f32)) + (
                got[rows].astype(f32) + got[rows + 1].astype(f32)
            )
    return cur, totals


def gather(part, steps, scattered):
    for bit, perm in reversed(steps[:scattered]):
        got = lax.ppermute(part, "tm", perm)
        part = jnp.where(
            bit == 0,
            jnp.concatenate([part, got], axis=0),
            jnp.concatenate([got, part], axis=0),
        )
    return part


def on_device(audio, kernel, templates, activations):
    peers = lax.axis_size("tm")
    frames = activations.shape[1]
    bins = templates.shape[0]
    cut = bins // 2 // 128 * 128 + 128
    halo = halo_rows(audio, peers)
    *powers, acts = analyse(
        audio.reshape(frames, HOP), halo, kernel, templates, activations, cut
    )
    weights = [templates[:cut], templates[cut:]]
    steps = exchanges(peers)
    scattered = min(3, len(steps))
    for step in range(ITERS):
        if step:
            numer, colsum = activation_numerator(powers[0], weights[0], acts)
            acts = new_activations(powers[1], weights[1], acts, numer, colsum)
        news = []
        for i, (w, p) in enumerate(zip(weights, powers)):
            numw, *totals = template_numerator(p, w, acts, i == 0)
            numw, sums = scatter_sum(numw, totals[0][0] if totals else None, steps, scattered)
            if i == 0:
                rowsum = sums
            own = w
            for bit, _ in steps[:scattered]:
                rows = own.shape[0] // 2
                own = lax.dynamic_slice_in_dim(own, bit * rows, rows, 0)
            own = (own.astype(f32) * numw / rowsum[None, :]).astype(bf16)
            news.append(gather(own, steps, scattered))
        weights = news
    return (acts, jnp.concatenate(weights, axis=0))


def solution(mesh):
    in_specs = (P(("groups", "tm")), P(), P(), P(None, ("groups", "tm")))
    out_specs = (P(None, ("groups", "tm")), P("groups", None))
    return jax.shard_map(
        on_device, mesh=mesh, in_specs=in_specs, out_specs=out_specs, check_vma=False
    )
```

time: 150 us -> 112 us (0.75)
  matrix products: 50.1 us -> 0 us
  Pallas kernels: 0 us -> 25.4 us
  other arithmetic: 10.7 us -> 4.33 us
  starting transfers between devices: 34.3 us -> 28 us
    dot_general x10 -> x0, matrix products: 50.1 us -> none  [the longest x4 21.2 us: on_device(): lax.dot_general(ratio, acts, (((1,), (1,)), ((), ())), preferred_element_...]
    pallas_call x0 -> x7, Pallas kernels: none -> 25.4 us  [call(): pl.pallas_call(kernel, out_shape=tuple(outs), in_specs=[VMEM] * len(args)...]
    ppermute x16, starting transfers between devices: 22.6 us -> 14.4 us  [scatter_sum(): got = lax.ppermute(send, 'tm', perm)]
    convert_element_type x17 -> x15, other arithmetic: 2.73 us -> 0.11 us  [the longest x6 0.05 us: scatter_sum(): hi = totals.astype(bf16)]
    ppermute x12, waiting for transfers between devices: 19 us -> 16.6 us  [gather(): got = lax.ppermute(part, 'tm', perm)]
    convert_element_type x12, local copies, waits for them, and re-layouts: 2.64 us -> 0.4 us  [scatter_sum(): send = lax.dynamic_slice_in_dim(cur, (1 - bit) * rows, rows, 0).astype(bf16)]
    unnamed x18 -> x24, local copies, waits for them, and re-layouts: 2.67 us -> 4.83 us
    ppermute x16, waiting for transfers between devices: 25.2 us -> 27.3 us  [scatter_sum(): got = lax.ppermute(send, 'tm', perm)]
  transfers between devices with their start and end apart: 30 -> 30, of which waited for: 19 -> 23; matrix products, arithmetic and copies ran while one was open for 8% -> 5% of each run, Pallas kernels for 0% -> 2%
where the time goes in v2:
time: 112 us
  waiting for transfers between devices  43.9 us (39%)
  starting transfers between devices  28 us (25%)
  Pallas kernels  25.4 us (23%)
  local copies, waits for them, and re-layouts  8.67 us (8%)
  other arithmetic  4.33 us (4%)
  between operations  1.37 us (1%)
    ppermute x16, waiting for transfers between devices, scatter_sum(): got = lax.ppermute(send, 'tm', perm)  27.3 us
    pallas_call x7, Pallas kernels, call(): pl.pallas_call(kernel, out_shape=tuple(outs), in_specs=[VMEM] * len(args)...  25.4 us
    ppermute x12, waiting for transfers between devices, gather(): got = lax.ppermute(part, 'tm', perm)  16.6 us
    ppermute x16, starting transfers between devices, scatter_sum(): got = lax.ppermute(send, 'tm', perm)  14.4 us
    ppermute x12, starting transfers between devices, gather(): got = lax.ppermute(part, 'tm', perm)  8.23 us
    ppermute x1, starting transfers between devices, halo_rows(): two = lax.ppermute(jnp.where(odd, tail, head), 'tm', outer)  5.44 us
    unnamed x24, local copies, waits for them, and re-layouts  4.83 us
    slice x2, local copies, waits for them, and re-layouts, on_device(): weights = [templates[:cut], templates[cut:]]  2.74 us
  transfers between devices with their start and end apart: 30, of which 23 were waited for; matrix products, arithmetic and copies ran while one was open for 5% of the time, Pallas kernels for 2%

profile of v2, /device:TPU:0, one launch (start us, length us, event | category | flops | bytes accessed | tf_op | source)
XLA Modules:
  0.0 111.7 jit_solution(10010978870567878208)
XLA Ops:
  1.5 5.4 %collective-permute-start.1 = (bf16[256]{0:T(256)(128)(2,1)S(1)}, bf16[256]{0:T(256)(128)(2,1)S(1)}, u32[]{:S(2)}, u32[]{:S(2)}) collective-permute-start(bf16[256]{0:T(256)(128)(2,1)S(1)} %get-tuple-element.32), channel_id=1, source_target_pairs={{0,15},{1,2},{2,1},{3,4},{4,3},{5,6},{6,5},{7,8},{8,7},{9,10},{10,... | collective-permute-start | bytes 1544 | tf_op jit(solution)/shard_map/ppermute | solution.py:186
  10.6 2.3 %copy-done.7 = bf16[2304,1024]{1,0:T(8,128)(2,1)S(1)} copy-done((bf16[2304,1024]{1,0:T(8,128)(2,1)S(1)}, bf16[2304,1024]{1,0:T(8,128)(2,1)}, u32[]{:S(2)}) %copy-start.7) | copy-done | bytes 4718616
  14.1 11.5 %shard_map.59 = (bf16[640,1024]{1,0:T(8,128)(2,1)S(1)}, bf16[512,1024]{1,0:T(8,128)(2,1)S(1)}, bf16[512,1024]{1,0:T(8,128)(2,1)S(1)}) custom-call(bf16[1024,512]{1,0:T(8,128)(2,1)S(1)} %reshape.7.a_ref, f32[2,256]{1,0:T(2,128)S(1)} %maximum_convert_fusion.halo_ref, bf16[2304,1024]{1,0:T(8,128)(2,1)S(1)} %copy-done.7, bf16[1152,512]{1,0:T(8,128)(2,1)S(1)} %copy-done, ...), custom_call_target="tpu_custom_call" | custom-call | flops 7247757312 | bytes 11405312 | tf_op jit(solution)/shard_map/pallas_call | solution.py:122
  25.7 2.1 %shard_map.60 = f32[512,512]{1,0:T(8,128)S(1)} custom-call(bf16[512,1024]{1,0:T(8,128)(2,1)S(1)} %get-tuple-element.11.p_ref, bf16[512,512]{1,0:T(8,128)(2,1)S(1)} %copy-done.6, bf16[512,1024]{1,0:T(8,128)(2,1)S(1)} %get-tuple-element.12.h_ref), custom_call_target="tpu_custom_call" | custom-call | flops 1073741824 | bytes 3670016 | tf_op jit(solution)/shard_map/pallas_call | solution.py:122
  28.4 2.6 %shard_map.61 = (f32[640,512]{1,0:T(8,128)S(1)}, f32[8,512]{1,0:T(8,128)S(1)}) custom-call(bf16[640,1024]{1,0:T(8,128)(2,1)S(1)} %get-tuple-element.13.p_ref, bf16[640,512]{1,0:T(8,128)(2,1)S(1)} %copy-done.5, bf16[512,1024]{1,0:T(8,128)(2,1)S(1)} %get-tuple-element.12.h_ref), custom_call_target="tpu_custom_call" | custom-call | flops 1342177280 | bytes 4341760 | tf_op jit(solution)/shard_map/pallas_call | solution.py:122
  33.7 2.7 %collective-permute-done.3 = bf16[128,512]{1,0:T(8,128)(2,1)S(1)} collective-permute-done((bf16[128,512]{1,0:T(8,128)(2,1)S(1)}, bf16[128,512]{1,0:T(8,128)(2,1)S(1)}, u32[]{:S(2)}, u32[]{:S(2)}) %collective-permute-start.3) | collective-permute-done | bytes 131104 | tf_op jit(solution)/shard_map/ppermute | solution.py:222
  36.4 2.1 %collective-permute-done.7 = bf16[168,512]{1,0:T(8,128)(2,1)S(1)} collective-permute-done((bf16[168,512]{1,0:T(8,128)(2,1)S(1)}, bf16[168,512]{1,0:T(8,128)(2,1)S(1)}, u32[]{:S(2)}, u32[]{:S(2)}) %collective-permute-start.7) | collective-permute-done | bytes 172064 | tf_op jit(solution)/shard_map/ppermute | solution.py:222
  38.7 2.1 %collective-permute-start.4 = (bf16[64,512]{1,0:T(8,128)(2,1)S(1)}, bf16[64,512]{1,0:T(8,128)(2,1)S(1)}, u32[]{:S(2)}, u32[]{:S(2)}) collective-permute-start(bf16[64,512]{1,0:T(8,128)(2,1)S(1)} %dynamic-slice_convert_fusion.11), channel_id=1, source_target_pairs={{0,4},{1,3},{2,6},{3,1},{4,0},{5,7},{6,2},{7,5},{8,12},{9,11},{10,... | collective-permute-start | bytes 196616 | tf_op jit(solution)/shard_map/ppermute | solution.py:222
  40.8 2.4 %collective-permute-done.8 = bf16[88,512]{1,0:T(8,128)(2,1)S(1)} collective-permute-done((bf16[88,512]{1,0:T(8,128)(2,1)S(1)}, bf16[88,512]{1,0:T(8,128)(2,1)S(1)}, u32[]{:S(2)}, u32[]{:S(2)}) %collective-permute-start.8) | collective-permute-done | bytes 90144 | tf_op jit(solution)/shard_map/ppermute | solution.py:222
  43.9 2.4 %collective-permute-start.5 = (bf16[64,512]{1,0:T(8,128)(2,1)S(1)}, bf16[64,512]{1,0:T(8,128)(2,1)S(1)}, u32[]{:S(2)}, u32[]{:S(2)}) collective-permute-start(bf16[64,512]{1,0:T(8,128)(2,1)S(1)} %add_convert_fusion.3), channel_id=1, source_target_pairs={{0,8},{1,9},{2,10},{3,11},{4,12},{5,13},{6,14},{7,15},{8,0},{9,1},... | collective-permute-start | bytes 196616 | tf_op jit(solution)/shard_map/ppermute | solution.py:222
  46.4 4.4 %collective-permute-done.9 = bf16[88,512]{1,0:T(8,128)(2,1)S(1)} collective-permute-done((bf16[88,512]{1,0:T(8,128)(2,1)S(1)}, bf16[88,512]{1,0:T(8,128)(2,1)S(1)}, u32[]{:S(2)}, u32[]{:S(2)}) %collective-permute-start.9) | collective-permute-done | bytes 90144 | tf_op jit(solution)/shard_map/ppermute | solution.py:222
  51.7 2.1 %collective-permute-start.13 = (bf16[80,512]{1,0:T(8,128)(2,1)S(1)}, bf16[80,512]{1,0:T(8,128)(2,1)S(1)}, u32[]{:S(2)}, u32[]{:S(2)}) collective-permute-start(bf16[80,512]{1,0:T(8,128)(2,1)S(1)} %divide_convert_fusion.1), channel_id=1, source_target_pairs={{0,4},{1,3},{2,6},{3,1},{4,0},{5,7},{6,2},{7,5},{8,12},{9,11},{10,... | collective-permute-start | bytes 245768 | tf_op jit(solution)/shard_map/ppermute | solution.py:233
  53.7 2.1 %collective-permute-done.10 = bf16[64,512]{1,0:T(8,128)(2,1)S(1)} collective-permute-done((bf16[64,512]{1,0:T(8,128)(2,1)S(1)}, bf16[64,512]{1,0:T(8,128)(2,1)S(1)}, u32[]{:S(2)}, u32[]{:S(2)}) %collective-permute-start.10) | collective-permute-done | bytes 65568 | tf_op jit(solution)/shard_map/ppermute | solution.py:233
  58.1 2.8 %collective-permute-done.11 = bf16[128,512]{1,0:T(8,128)(2,1)S(1)} collective-permute-done((bf16[128,512]{1,0:T(8,128)(2,1)S(1)}, bf16[128,512]{1,0:T(8,128)(2,1)S(1)}, u32[]{:S(2)}, u32[]{:S(2)}) %collective-permute-start.11) | collective-permute-done | bytes 131104 | tf_op jit(solution)/shard_map/ppermute | solution.py:233
  66.7 2.6 %shard_map.63.h_ref = bf16[512,1024]{1,0:T(8,128)(2,1)} custom-call(bf16[512,1024]{1,0:T(8,128)(2,1)S(1)} %get-tuple-element.11.p_ref, bf16[512,512]{1,0:T(8,128)(2,1)S(1)} %maximum_select_fusion.2.w_ref, bf16[512,1024]{1,0:T(8,128)(2,1)S(1)} %copy-done.4, f32[512,1024]{1,0:T(8,128)S(1)} %get-tuple-element.16.refs_0_, f32[512,128]{1,0:T(8,128)S(1)} %get-tuple-element.17.refs_1_), custom_call_target="tpu_custom_call" | custom-call | flops 1073741824 | bytes 6029312 | tf_op jit(solution)/shard_map/pallas_call | solution.py:122
  70.6 2.1 %shard_map.65 = f32[512,512]{1,0:T(8,128)S(1)} custom-call(bf16[512,1024]{1,0:T(8,128)(2,1)S(1)} %get-tuple-element.11.p_ref, bf16[512,512]{1,0:T(8,128)(2,1)S(1)} %maximum_select_fusion.2.w_ref, bf16[512,1024]{1,0:T(8,128)(2,1)S(1)} %copy-done.1), custom_call_target="tpu_custom_call" | custom-call | flops 1073741824 | bytes 3670016 | tf_op jit(solution)/shard_map/pallas_call | solution.py:122
  72.7 2.5 %shard_map.64 = (f32[640,512]{1,0:T(8,128)S(1)}, f32[8,512]{1,0:T(8,128)S(1)}) custom-call(bf16[640,1024]{1,0:T(8,128)(2,1)S(1)} %copy-done.10, bf16[640,512]{1,0:T(8,128)(2,1)S(1)} %maximum_select_fusion.w_ref, bf16[512,1024]{1,0:T(8,128)(2,1)S(1)} %copy-done.2), custom_call_target="tpu_custom_call" | custom-call | flops 1342177280 | bytes 4341760 | tf_op jit(solution)/shard_map/pallas_call | solution.py:122
  79.3 2.7 %collective-permute-done.24 = bf16[128,512]{1,0:T(8,128)(2,1)S(1)} collective-permute-done((bf16[128,512]{1,0:T(8,128)(2,1)S(1)}, bf16[128,512]{1,0:T(8,128)(2,1)S(1)}, u32[]{:S(2)}, u32[]{:S(2)}) %collective-permute-start.24) | collective-permute-done | bytes 131104 | tf_op jit(solution)/shard_map/ppermute | solution.py:222
  86.1 2.4 %collective-permute-done.18 = bf16[88,512]{1,0:T(8,128)(2,1)S(1)} collective-permute-done((bf16[88,512]{1,0:T(8,128)(2,1)S(1)}, bf16[88,512]{1,0:T(8,128)(2,1)S(1)}, u32[]{:S(2)}, u32[]{:S(2)}) %collective-permute-start.18) | collective-permute-done | bytes 90144 | tf_op jit(solution)/shard_map/ppermute | solution.py:222
  88.6 2.1 %collective-permute-start.19 = (bf16[88,512]{1,0:T(8,128)(2,1)S(1)}, bf16[88,512]{1,0:T(8,128)(2,1)S(1)}, u32[]{:S(2)}, u32[]{:S(2)}) collective-permute-start(bf16[88,512]{1,0:T(8,128)(2,1)S(1)} %pad_maximum_fusion.5), channel_id=1, source_target_pairs={{0,8},{1,9},{2,10},{3,11},{4,12},{5,13},{6,14},{7,15},{8,0},{9,1},... | collective-permute-start | bytes 270344 | tf_op jit(solution)/shard_map/ppermute | solution.py:222
  91.7 4.9 %collective-permute-done.19 = bf16[88,512]{1,0:T(8,128)(2,1)S(1)} collective-permute-done((bf16[88,512]{1,0:T(8,128)(2,1)S(1)}, bf16[88,512]{1,0:T(8,128)(2,1)S(1)}, u32[]{:S(2)}, u32[]{:S(2)}) %collective-permute-start.19) | collective-permute-done | bytes 90144 | tf_op jit(solution)/shard_map/ppermute | solution.py:222
  97.5 2.1 %collective-permute-start.20 = (bf16[80,512]{1,0:T(8,128)(2,1)S(1)}, bf16[80,512]{1,0:T(8,128)(2,1)S(1)}, u32[]{:S(2)}, u32[]{:S(2)}) collective-permute-start(bf16[80,512]{1,0:T(8,128)(2,1)S(1)} %divide_convert_fusion), channel_id=1, source_target_pairs={{0,4},{1,3},{2,6},{3,1},{4,0},{5,7},{6,2},{7,5},{8,12},{9,11},{10,... | collective-permute-start | bytes 245768 | tf_op jit(solution)/shard_map/ppermute | solution.py:233
  99.6 2.1 %collective-permute-done.27 = bf16[64,512]{1,0:T(8,128)(2,1)S(1)} collective-permute-done((bf16[64,512]{1,0:T(8,128)(2,1)S(1)}, bf16[64,512]{1,0:T(8,128)(2,1)S(1)}, u32[]{:S(2)}, u32[]{:S(2)}) %collective-permute-start.27) | collective-permute-done | bytes 65568 | tf_op jit(solution)/shard_map/ppermute | solution.py:233
  104.1 2.7 %collective-permute-done.28 = bf16[128,512]{1,0:T(8,128)(2,1)S(1)} collective-permute-done((bf16[128,512]{1,0:T(8,128)(2,1)S(1)}, bf16[128,512]{1,0:T(8,128)(2,1)S(1)}, u32[]{:S(2)}, u32[]{:S(2)}) %collective-permute-start.28) | collective-permute-done | bytes 131104 | tf_op jit(solution)/shard_map/ppermute | solution.py:233
  (143 shorter events, 37.1 us)
Async XLA Ops:
  1.5 9.0 %collective-permute-start.1 = (bf16[256]{0:T(256)(128)(2,1)S(1)}, bf16[256]{0:T(256)(128)(2,1)S(1)}, u32[]{:S(2)}, u32[]{:S(2)}) collective-permute-start(bf16[256]{0:T(256)(128)(2,1)S(1)} %get-tuple-element.32), channel_id=1, source_target_pairs={{0,15},{1,2},{2,1},{3,4},{4,3},{5,6},{6,5},{7,8},{8,7},{9,10},{10,... | collective-permute-start | bytes 1544 | tf_op jit(solution)/shard_map/ppermute | solution.py:186
  7.0 3.5 %collective-permute-start = (bf16[256]{0:T(256)(128)(2,1)S(1)}, bf16[256]{0:T(256)(128)(2,1)S(1)}, u32[]{:S(2)}, u32[]{:S(2)}) collective-permute-start(bf16[256]{0:T(256)(128)(2,1)S(1)} %get-tuple-element.33), channel_id=1, source_target_pairs={{0,1},{1,0},{2,3},{3,2},{4,5},{5,4},{6,7},{7,6},{8,9},{9,8},{10,11... | collective-permute-start | bytes 1544 | tf_op jit(solution)/shard_map/ppermute | solution.py:185
  27.9 3.4 %collective-permute-start.2 = (bf16[256,512]{1,0:T(8,128)(2,1)S(1)}, bf16[256,512]{1,0:T(8,128)(2,1)S(1)}, u32[]{:S(2)}, u32[]{:S(2)}) collective-permute-start(bf16[256,512]{1,0:T(8,128)(2,1)S(1)} %dynamic-slice_convert_fusion.3), channel_id=1, source_target_pairs={{0,1},{1,0},{2,3},{3,2},{4,5},{5,4},{6,7},{7,6},{8,9},{9,8},{10,11... | collective-permute-start | bytes 786440 | tf_op jit(solution)/shard_map/ppermute | solution.py:222
  31.4 5.0 %collective-permute-start.3 = (bf16[128,512]{1,0:T(8,128)(2,1)S(1)}, bf16[128,512]{1,0:T(8,128)(2,1)S(1)}, u32[]{:S(2)}, u32[]{:S(2)}) collective-permute-start(bf16[128,512]{1,0:T(8,128)(2,1)S(1)} %dynamic-slice_convert_fusion.7), channel_id=1, source_target_pairs={{0,2},{1,5},{2,0},{3,7},{4,6},{5,1},{6,4},{7,3},{8,10},{9,13},{10,... | collective-permute-start | bytes 393224 | tf_op jit(solution)/shard_map/ppermute | solution.py:222
  33.0 5.5 %collective-permute-start.7 = (bf16[168,512]{1,0:T(8,128)(2,1)S(1)}, bf16[168,512]{1,0:T(8,128)(2,1)S(1)}, u32[]{:S(2)}, u32[]{:S(2)}) collective-permute-start(bf16[168,512]{1,0:T(8,128)(2,1)S(1)} %pad_maximum_fusion.4), channel_id=1, source_target_pairs={{0,2},{1,5},{2,0},{3,7},{4,6},{5,1},{6,4},{7,3},{8,10},{9,13},{10,... | collective-permute-start | bytes 516104 | tf_op jit(solution)/shard_map/ppermute | solution.py:222
  38.6 4.6 %collective-permute-start.8 = (bf16[88,512]{1,0:T(8,128)(2,1)S(1)}, bf16[88,512]{1,0:T(8,128)(2,1)S(1)}, u32[]{:S(2)}, u32[]{:S(2)}) collective-permute-start(bf16[88,512]{1,0:T(8,128)(2,1)S(1)} %pad_maximum_fusion.8), channel_id=1, source_target_pairs={{0,4},{1,3},{2,6},{3,1},{4,0},{5,7},{6,2},{7,5},{8,12},{9,11},{10,... | collective-permute-start | bytes 270344 | tf_op jit(solution)/shard_map/ppermute | solution.py:222
  38.7 5.2 %collective-permute-start.4 = (bf16[64,512]{1,0:T(8,128)(2,1)S(1)}, bf16[64,512]{1,0:T(8,128)(2,1)S(1)}, u32[]{:S(2)}, u32[]{:S(2)}) collective-permute-start(bf16[64,512]{1,0:T(8,128)(2,1)S(1)} %dynamic-slice_convert_fusion.11), channel_id=1, source_target_pairs={{0,4},{1,3},{2,6},{3,1},{4,0},{5,7},{6,2},{7,5},{8,12},{9,11},{10,... | collective-permute-start | bytes 196616 | tf_op jit(solution)/shard_map/ppermute | solution.py:222
  43.3 7.5 %collective-permute-start.9 = (bf16[88,512]{1,0:T(8,128)(2,1)S(1)}, bf16[88,512]{1,0:T(8,128)(2,1)S(1)}, u32[]{:S(2)}, u32[]{:S(2)}) collective-permute-start(bf16[88,512]{1,0:T(8,128)(2,1)S(1)} %pad_maximum_fusion.7), channel_id=1, source_target_pairs={{0,8},{1,9},{2,10},{3,11},{4,12},{5,13},{6,14},{7,15},{8,0},{9,1},... | collective-permute-start | bytes 270344 | tf_op jit(solution)/shard_map/ppermute | solution.py:222
  43.9 7.5 %collective-permute-start.5 = (bf16[64,512]{1,0:T(8,128)(2,1)S(1)}, bf16[64,512]{1,0:T(8,128)(2,1)S(1)}, u32[]{:S(2)}, u32[]{:S(2)}) collective-permute-start(bf16[64,512]{1,0:T(8,128)(2,1)S(1)} %add_convert_fusion.3), channel_id=1, source_target_pairs={{0,8},{1,9},{2,10},{3,11},{4,12},{5,13},{6,14},{7,15},{8,0},{9,1},... | collective-permute-start | bytes 196616 | tf_op jit(solution)/shard_map/ppermute | solution.py:222
  51.5 4.3 %collective-permute-start.10 = (bf16[64,512]{1,0:T(8,128)(2,1)S(1)}, bf16[64,512]{1,0:T(8,128)(2,1)S(1)}, u32[]{:S(2)}, u32[]{:S(2)}) collective-permute-start(bf16[64,512]{1,0:T(8,128)(2,1)S(1)} %divide_convert_fusion.3), channel_id=1, source_target_pairs={{0,4},{1,3},{2,6},{3,1},{4,0},{5,7},{6,2},{7,5},{8,12},{9,11},{10,... | collective-permute-start | bytes 196616 | tf_op jit(solution)/shard_map/ppermute | solution.py:233
  51.7 5.2 %collective-permute-start.13 = (bf16[80,512]{1,0:T(8,128)(2,1)S(1)}, bf16[80,512]{1,0:T(8,128)(2,1)S(1)}, u32[]{:S(2)}, u32[]{:S(2)}) collective-permute-start(bf16[80,512]{1,0:T(8,128)(2,1)S(1)} %divide_convert_fusion.1), channel_id=1, source_target_pairs={{0,4},{1,3},{2,6},{3,1},{4,0},{5,7},{6,2},{7,5},{8,12},{9,11},{10,... | collective-permute-start | bytes 245768 | tf_op jit(solution)/shard_map/ppermute | solution.py:233
  55.9 5.0 %collective-permute-start.11 = (bf16[128,512]{1,0:T(8,128)(2,1)S(1)}, bf16[128,512]{1,0:T(8,128)(2,1)S(1)}, u32[]{:S(2)}, u32[]{:S(2)}) collective-permute-start(bf16[128,512]{1,0:T(8,128)(2,1)S(1)} %maximum_select_fusion.10), channel_id=1, source_target_pairs={{0,2},{1,5},{2,0},{3,7},{4,6},{5,1},{6,4},{7,3},{8,10},{9,13},{10,... | collective-permute-start | bytes 393224 | tf_op jit(solution)/shard_map/ppermute | solution.py:233
  56.9 5.8 %collective-permute-start.14 = (bf16[160,512]{1,0:T(8,128)(2,1)S(1)}, bf16[160,512]{1,0:T(8,128)(2,1)S(1)}, u32[]{:S(2)}, u32[]{:S(2)}) collective-permute-start(bf16[160,512]{1,0:T(8,128)(2,1)S(1)} %maximum_select_fusion.8), channel_id=1, source_target_pairs={{0,2},{1,5},{2,0},{3,7},{4,6},{5,1},{6,4},{7,3},{8,10},{9,13},{10,... | collective-permute-start | bytes 491528 | tf_op jit(solution)/shard_map/ppermute | solution.py:233
  75.6 2.2 %collective-permute-start.16 = (bf16[328,512]{1,0:T(8,128)(2,1)S(1)}, bf16[328,512]{1,0:T(8,128)(2,1)S(1)}, u32[]{:S(2)}, u32[]{:S(2)}) collective-permute-start(bf16[328,512]{1,0:T(8,128)(2,1)S(1)} %pad_maximum_fusion.1), channel_id=1, source_target_pairs={{0,1},{1,0},{2,3},{3,2},{4,5},{5,4},{6,7},{7,6},{8,9},{9,8},{10,11... | collective-permute-start | bytes 1007624 | tf_op jit(solution)/shard_map/ppermute | solution.py:222
  77.0 5.0 %collective-permute-start.24 = (bf16[128,512]{1,0:T(8,128)(2,1)S(1)}, bf16[128,512]{1,0:T(8,128)(2,1)S(1)}, u32[]{:S(2)}, u32[]{:S(2)}) collective-permute-start(bf16[128,512]{1,0:T(8,128)(2,1)S(1)} %dynamic-slice_convert_fusion.6), channel_id=1, source_target_pairs={{0,2},{1,5},{2,0},{3,7},{4,6},{5,1},{6,4},{7,3},{8,10},{9,13},{10,... | collective-permute-start | bytes 393224 | tf_op jit(solution)/shard_map/ppermute | solution.py:222
  78.0 5.9 %collective-permute-start.17 = (bf16[168,512]{1,0:T(8,128)(2,1)S(1)}, bf16[168,512]{1,0:T(8,128)(2,1)S(1)}, u32[]{:S(2)}, u32[]{:S(2)}) collective-permute-start(bf16[168,512]{1,0:T(8,128)(2,1)S(1)} %pad_maximum_fusion.3), channel_id=1, source_target_pairs={{0,2},{1,5},{2,0},{3,7},{4,6},{5,1},{6,4},{7,3},{8,10},{9,13},{10,... | collective-permute-start | bytes 516104 | tf_op jit(solution)/shard_map/ppermute | solution.py:222
  84.0 4.6 %collective-permute-start.18 = (bf16[88,512]{1,0:T(8,128)(2,1)S(1)}, bf16[88,512]{1,0:T(8,128)(2,1)S(1)}, u32[]{:S(2)}, u32[]{:S(2)}) collective-permute-start(bf16[88,512]{1,0:T(8,128)(2,1)S(1)} %pad_maximum_fusion.6), channel_id=1, source_target_pairs={{0,4},{1,3},{2,6},{3,1},{4,0},{5,7},{6,2},{7,5},{8,12},{9,11},{10,... | collective-permute-start | bytes 270344 | tf_op jit(solution)/shard_map/ppermute | solution.py:222
  85.8 4.9 %collective-permute-start.25 = (bf16[64,512]{1,0:T(8,128)(2,1)S(1)}, bf16[64,512]{1,0:T(8,128)(2,1)S(1)}, u32[]{:S(2)}, u32[]{:S(2)}) collective-permute-start(bf16[64,512]{1,0:T(8,128)(2,1)S(1)} %dynamic-slice_convert_fusion.10), channel_id=1, source_target_pairs={{0,4},{1,3},{2,6},{3,1},{4,0},{5,7},{6,2},{7,5},{8,12},{9,11},{10,... | collective-permute-start | bytes 196616 | tf_op jit(solution)/shard_map/ppermute | solution.py:222
  88.6 8.0 %collective-permute-start.19 = (bf16[88,512]{1,0:T(8,128)(2,1)S(1)}, bf16[88,512]{1,0:T(8,128)(2,1)S(1)}, u32[]{:S(2)}, u32[]{:S(2)}) collective-permute-start(bf16[88,512]{1,0:T(8,128)(2,1)S(1)} %pad_maximum_fusion.5), channel_id=1, source_target_pairs={{0,8},{1,9},{2,10},{3,11},{4,12},{5,13},{6,14},{7,15},{8,0},{9,1},... | collective-permute-start | bytes 270344 | tf_op jit(solution)/shard_map/ppermute | solution.py:222
  90.7 6.6 %collective-permute-start.26 = (bf16[64,512]{1,0:T(8,128)(2,1)S(1)}, bf16[64,512]{1,0:T(8,128)(2,1)S(1)}, u32[]{:S(2)}, u32[]{:S(2)}) collective-permute-start(bf16[64,512]{1,0:T(8,128)(2,1)S(1)} %add_convert_fusion.2), channel_id=1, source_target_pairs={{0,8},{1,9},{2,10},{3,11},{4,12},{5,13},{6,14},{7,15},{8,0},{9,1},... | collective-permute-start | bytes 196616 | tf_op jit(solution)/shard_map/ppermute | solution.py:222
  97.4 4.3 %collective-permute-start.27 = (bf16[64,512]{1,0:T(8,128)(2,1)S(1)}, bf16[64,512]{1,0:T(8,128)(2,1)S(1)}, u32[]{:S(2)}, u32[]{:S(2)}) collective-permute-start(bf16[64,512]{1,0:T(8,128)(2,1)S(1)} %divide_convert_fusion.2), channel_id=1, source_target_pairs={{0,4},{1,3},{2,6},{3,1},{4,0},{5,7},{6,2},{7,5},{8,12},{9,11},{10,... | collective-permute-start | bytes 196616 | tf_op jit(solution)/shard_map/ppermute | solution.py:233
  97.5 5.3 %collective-permute-start.20 = (bf16[80,512]{1,0:T(8,128)(2,1)S(1)}, bf16[80,512]{1,0:T(8,128)(2,1)S(1)}, u32[]{:S(2)}, u32[]{:S(2)}) collective-permute-start(bf16[80,512]{1,0:T(8,128)(2,1)S(1)} %divide_convert_fusion), channel_id=1, source_target_pairs={{0,4},{1,3},{2,6},{3,1},{4,0},{5,7},{6,2},{7,5},{8,12},{9,11},{10,... | collective-permute-start | bytes 245768 | tf_op jit(solution)/shard_map/ppermute | solution.py:233
  101.7 5.0 %collective-permute-start.28 = (bf16[128,512]{1,0:T(8,128)(2,1)S(1)}, bf16[128,512]{1,0:T(8,128)(2,1)S(1)}, u32[]{:S(2)}, u32[]{:S(2)}) collective-permute-start(bf16[128,512]{1,0:T(8,128)(2,1)S(1)} %maximum_select_fusion.11), channel_id=1, source_target_pairs={{0,2},{1,5},{2,0},{3,7},{4,6},{5,1},{6,4},{7,3},{8,10},{9,13},{10,... | collective-permute-start | bytes 393224 | tf_op jit(solution)/shard_map/ppermute | solution.py:233
  102.8 5.7 %collective-permute-start.21 = (bf16[160,512]{1,0:T(8,128)(2,1)S(1)}, bf16[160,512]{1,0:T(8,128)(2,1)S(1)}, u32[]{:S(2)}, u32[]{:S(2)}) collective-permute-start(bf16[160,512]{1,0:T(8,128)(2,1)S(1)} %maximum_select_fusion.9), channel_id=1, source_target_pairs={{0,2},{1,5},{2,0},{3,7},{4,6},{5,1},{6,4},{7,3},{8,10},{9,13},{10,... | collective-permute-start | bytes 491528 | tf_op jit(solution)/shard_map/ppermute | solution.py:233
  (18 other events, 58.4 us)

commit v3 on v2

v3 whole, which is shorter than its diff:
```python
import functools

import jax
import jax.numpy as jnp
from jax import lax
from jax.experimental import pallas as pl
from jax.experimental.pallas import tpu as pltpu
from jax.sharding import PartitionSpec as P

HOP = 512
ITERS = 2
HALF = 256
TILE = 256
LANES = 128
bf16 = jnp.bfloat16
f32 = jnp.float32
NT = (((1,), (1,)), ((), ()))


def inverse(x):
    r = pl.reciprocal(x, approx=True)
    return r * (2.0 - x * r)


def dot(a, b):
    return jnp.dot(a, b, preferred_element_type=f32)


def dot_nt(a, b):
    return lax.dot_general(a, b, NT, preferred_element_type=f32)


def row_blocks(rows):
    first = rows % TILE
    cuts = [0] + list(range(first + TILE if first else TILE, rows + 1, TILE))
    return list(zip(cuts[:-1], cuts[1:]))


def analyse_kernel(cut, halo_ref, a_hbm, k_hbm, w_hbm, h_hbm, pa_ref, pb_ref, new_ref,
                   a_ref, k_ref, w_ref, h_ref, wide, frame, wt, a_sem, k_sem, w_sem, h_sem):
    bins = w_ref.shape[0]
    frames = h_ref.shape[1]
    blocks = row_blocks(bins)
    a_copy = pltpu.make_async_copy(a_hbm, a_ref, a_sem)
    a_copy.start()
    k_copies = []
    for n, (lo, hi) in enumerate(blocks):
        pair = []
        for m, base in enumerate((0, bins)):
            rows = pl.ds(base + lo, hi - lo)
            pair.append(pltpu.make_async_copy(k_hbm.at[rows], k_ref.at[rows], k_sem.at[2 * n + m]))
            pair[-1].start()
        k_copies.append(pair)
    w_copy = pltpu.make_async_copy(w_hbm, w_ref, w_sem)
    h_copy = pltpu.make_async_copy(h_hbm, h_ref, h_sem)
    w_copy.start()
    h_copy.start()

    a_copy.wait()
    wide[8 : 8 + a_ref.shape[0], :] = a_ref[...].astype(f32)
    wide[6:8, :] = halo_ref[0:2, :]
    wide[8 + a_ref.shape[0] : 10 + a_ref.shape[0], :] = halo_ref[2:4, :]
    for j in range(2 * HOP // LANES):
        rows = wide[pl.ds(6 + j, frames, stride=HOP // LANES), :]
        frame[:, j * LANES : (j + 1) * LANES] = rows.astype(bf16)

    for (lo, hi), pair in zip(blocks, k_copies):
        for copy in pair:
            copy.wait()
        for t in range(0, frames, TILE):
            f = frame[t : t + TILE, :]
            re = dot_nt(k_ref[lo:hi, :], f)
            im = dot_nt(k_ref[bins + lo : bins + hi, :], f)
            p = (re * re + im * im).astype(bf16)
            if hi <= cut:
                pa_ref[lo:hi, t : t + TILE] = p
            else:
                pb_ref[lo - cut : hi - cut, t : t + TILE] = p

    w_copy.wait()
    h_copy.wait()
    wt[...] = w_ref[...].T
    inv = inverse(jnp.sum(wt[...].astype(f32), axis=1, keepdims=True))
    for t in range(0, frames, TILE):
        tile = slice(t, t + TILE)
        h = h_ref[:, tile]
        numer = None
        for lo, hi in blocks:
            p = pa_ref[lo:hi, tile] if hi <= cut else pb_ref[lo - cut : hi - cut, tile]
            model = dot(w_ref[lo:hi, :], h)
            ratio = (p.astype(f32) * inverse(model)).astype(bf16)
            part = dot(wt[:, lo:hi], ratio)
            numer = part if numer is None else numer + part
        new_ref[:, tile] = (h.astype(f32) * numer * inv).astype(bf16)


def template_kernel(send, base, extras, at_ref, p_ref, w_ref, h_ref, *outs):
    frames = h_ref.shape[1]
    outs = list(outs)
    numw_ref = outs.pop(0)
    rows = p_ref.shape[0] // 2
    own = pl.multiple_of(at_ref[0] * rows, 16)
    w = w_ref[pl.ds(base + own, rows), :]
    for lo, hi in row_blocks(rows):
        acc = None
        for t in range(0, frames, TILE):
            h = h_ref[:, t : t + TILE]
            model = dot(w[lo:hi, :], h)
            p = p_ref[pl.ds(own + lo, hi - lo), t : t + TILE]
            ratio = (p.astype(f32) * inverse(model)).astype(bf16)
            part = dot_nt(ratio, h)
            acc = part if acc is None else acc + part
        numw_ref[lo:hi, :] = acc.astype(numw_ref.dtype)
    if "totals" in extras:
        total = dot_nt(jnp.ones((16, frames), bf16), h_ref[...])
        high = total.astype(bf16).astype(f32)
        low = (total - high).astype(bf16).astype(f32)
        if send:
            row = lax.broadcasted_iota(jnp.int32, total.shape, 0)
            both = jnp.where(row == 0, high, jnp.where(row == 1, low, 0.0))
            numw_ref[rows : rows + 16, :] = both.astype(bf16)
        else:
            outs.pop(0)[...] = (high + low)[:8]
    if not send:
        outs.pop(0)[...] = w
    if "copy" in extras:
        outs.pop(0)[...] = h_ref[...]


def activation_kernel(first, p_ref, w_ref, h_ref, *refs):
    if first:
        numer_ref, col_ref, wt = refs
    else:
        old_ref, oldcol_ref, new_ref, wt = refs
    frames = h_ref.shape[1]
    wt[...] = w_ref[...].T
    col = jnp.sum(wt[...].astype(f32), axis=1, keepdims=True)
    if first:
        col_ref[...] = jnp.broadcast_to(col, col_ref.shape)
    else:
        inv = inverse(col + oldcol_ref[:, :1])
    for t in range(0, frames, TILE):
        tile = slice(t, t + TILE)
        h = h_ref[:, tile]
        numer = None if first else old_ref[:, tile]
        for lo, hi in row_blocks(p_ref.shape[0]):
            model = dot(w_ref[lo:hi, :], h)
            ratio = (p_ref[lo:hi, tile].astype(f32) * inverse(model)).astype(bf16)
            part = dot(wt[:, lo:hi], ratio)
            numer = part if numer is None else numer + part
        if first:
            numer_ref[:, tile] = numer
        else:
            new_ref[:, tile] = (h.astype(f32) * numer * inv).astype(bf16)


VMEM = pl.BlockSpec(memory_space=pltpu.VMEM)
HBM = pl.BlockSpec(memory_space=pltpu.HBM)


def call(kernel, outs, scratch, flops, *args, specs=None, mib=16):
    size = sum(a.size * a.dtype.itemsize for a in args)
    size += sum(o.size * o.dtype.itemsize for o in outs)
    return pl.pallas_call(
        kernel,
        out_shape=tuple(outs),
        in_specs=specs or [VMEM] * len(args),
        out_specs=tuple([VMEM] * len(outs)),
        scratch_shapes=scratch,
        cost_estimate=pl.CostEstimate(flops=flops*100, bytes_accessed=size*100, transcendentals=0),
        compiler_params=pltpu.CompilerParams(vmem_limit_bytes=mib * 1024 * 1024),
    )(*args)


def shape(dims, dtype):
    return jax.ShapeDtypeStruct(dims, dtype)


def analyse(audio, halo, kernel, weights, acts, cut):
    bins, comps = weights.shape
    frames = acts.shape[1]
    blocks = len(row_blocks(bins))
    return call(
        functools.partial(analyse_kernel, cut),
        [shape((cut, frames), bf16), shape((bins - cut, frames), bf16), shape((comps, frames), bf16)],
        [
            pltpu.VMEM(audio.shape, bf16),
            pltpu.VMEM(kernel.shape, bf16),
            pltpu.VMEM(weights.shape, bf16),
            pltpu.VMEM(acts.shape, bf16),
            pltpu.VMEM((audio.shape[0] + 16, LANES), f32),
            pltpu.VMEM((frames, 2 * HOP), bf16),
            pltpu.VMEM((comps, bins), bf16),
            pltpu.SemaphoreType.DMA,
            pltpu.SemaphoreType.DMA((2 * blocks,)),
            pltpu.SemaphoreType.DMA,
            pltpu.SemaphoreType.DMA,
        ],
        2 * bins * frames * (4 * HOP + 2 * comps),
        halo, *[pltpu.with_memory_space_constraint(x, pltpu.HBM) for x in (audio, kernel, weights, acts)],
        specs=[VMEM, HBM, HBM, HBM, HBM],
        mib=32,
    )


def template_numerator(send, at, power, weights, base, acts, extras=()):
    rows, comps = power.shape[0] // 2, acts.shape[0]
    if send:
        outs = [shape((rows + (16 if "totals" in extras else 0), comps), bf16)]
    else:
        outs = [shape((rows, comps), f32)]
        if "totals" in extras:
            outs.append(shape((8, comps), f32))
        outs.append(shape((rows, comps), bf16))
    if "copy" in extras:
        outs.append(shape(acts.shape, bf16))
    kernel = functools.partial(template_kernel, send, base, extras)
    at = jnp.reshape(1 - at if send else at, (1,)).astype(jnp.int32)
    return call(
        kernel, outs, [], 2 * power.size * comps, at, power, weights, acts,
        specs=[pl.BlockSpec(memory_space=pltpu.SMEM)] + [VMEM] * 3,
    )


def activation_numerator(power, weights, acts):
    bins, comps = weights.shape
    return call(
        functools.partial(activation_kernel, True),
        [shape(acts.shape, f32), shape((comps, 128), f32)],
        [pltpu.VMEM((comps, bins), bf16)],
        4 * power.size * comps, power, weights, acts,
    )


def new_activations(power, weights, acts, numer, colsum):
    bins, comps = weights.shape
    return call(
        functools.partial(activation_kernel, False),
        [shape(acts.shape, bf16)],
        [pltpu.VMEM((comps, bins), bf16)],
        4 * power.size * comps, power, weights, acts, numer, colsum,
    )[0]


def halo_rows(audio, peers):
    me = lax.axis_index("tm")
    odd = me % 2 == 1
    rows = HALF // LANES
    head, tail = audio[:rows], audio[audio.shape[0] - rows :]
    inner = [(i, i ^ 1) for i in range(peers)]
    outer = [(i, (i + 1) % peers if i % 2 else (i - 1) % peers) for i in range(peers)]
    one = lax.ppermute(jnp.where(odd, head, tail), "tm", inner)
    two = lax.ppermute(jnp.where(odd, tail, head), "tm", outer)
    two = jnp.where((me == 0) | (me == peers - 1), jnp.zeros_like(two), two)
    left = jnp.where(odd, one, two)
    right = jnp.where(odd, two, one)
    return jnp.concatenate([left, right], axis=0).astype(f32)


class Group:
    def __init__(self, bits, peers):
        me = lax.axis_index("tm")
        self.size = 1 << len(bits)
        self.me = sum(((me // b) % 2) << j for j, b in enumerate(bits))
        self.others = []
        for code in range(1, self.size):
            mask = sum(b for j, b in enumerate(bits) if code >> j & 1)
            self.others.append((code, [(i, i ^ mask) for i in range(peers)]))


def groups_of(peers):
    bits = [1 << b for b in range(peers.bit_length() - 1)]
    shared = [Group(g, peers) for g in (bits[:1], bits[1:3]) if g]
    return shared, [Group([b], peers) for b in bits[3:]]


def block_of(x, index, rows):
    return lax.dynamic_slice_in_dim(x, index * rows, rows, 0)


def swap(send, totals, perm):
    rows = send.shape[0]
    if totals is None:
        return lax.ppermute(send, "tm", perm).astype(f32), None
    hi, lo = totals
    pad = jnp.zeros((6, hi.shape[0]), bf16)
    got = lax.ppermute(jnp.concatenate([send, hi[None], lo[None], pad], axis=0), "tm", perm)
    return got[:rows].astype(f32), got[rows].astype(f32) + got[rows + 1].astype(f32)


def share_out(cur, totals, group):
    rows = cur.shape[0] // group.size
    halves = None
    if totals is not None:
        hi = totals.astype(bf16)
        halves = (hi, (totals - hi.astype(f32)).astype(bf16))
        totals = halves[0].astype(f32) + halves[1].astype(f32)
    own = block_of(cur, group.me, rows)
    for code, perm in group.others:
        got, more = swap(block_of(cur, group.me ^ code, rows).astype(bf16), halves, perm)
        own = own + got
        if totals is not None:
            totals = totals + more
    return own, totals


def sum_pair(cur, totals, group):
    halves = None
    send = cur.astype(bf16)
    if totals is not None:
        hi = totals.astype(bf16)
        halves = (hi, (totals - hi.astype(f32)).astype(bf16))
        totals = halves[0].astype(f32) + halves[1].astype(f32)
    got, more = swap(send, halves, group.others[0][1])
    return send.astype(f32) + got, None if totals is None else totals + more


def gather(part, group):
    rows = part.shape[0]
    out = jnp.zeros((rows * group.size,) + part.shape[1:], part.dtype)
    out = lax.dynamic_update_slice_in_dim(out, part, group.me * rows, 0)
    for code, perm in group.others:
        got = lax.ppermute(part, "tm", perm)
        out = lax.dynamic_update_slice_in_dim(out, got, (group.me ^ code) * rows, 0)
    return out


def on_device(audio, kernel, templates, activations):
    peers = lax.axis_size("tm")
    frames = activations.shape[1]
    bins = templates.shape[0]
    cut = bins // 2 // 128 * 128 + 128
    audio = audio.reshape(audio.shape[0] // LANES, LANES)
    halo = halo_rows(audio, peers)
    *powers, acts = analyse(audio, halo, kernel, templates, activations, cut)
    weights = [(templates, 0), (templates, cut)]
    shared, pairs = groups_of(peers)
    core, rest = shared[0], shared[1:]
    for step in range(ITERS):
        last = step == ITERS - 1
        totals, parts = None, []
        for i, ((w, base), p) in enumerate(zip(weights, powers)):
            with_totals = ("totals",) if i == 0 else ()
            (send,) = template_numerator(True, core.me, p, w, base, acts, with_totals)
            got = lax.ppermute(send, "tm", core.others[0][1])
            extras = with_totals + (("copy",) if i == 1 and last else ())
            own, *more = template_numerator(False, core.me, p, w, base, acts, extras)
            rows = own.shape[0]
            own = own + got[:rows].astype(f32)
            tot = None
            if i == 0:
                tot = more.pop(0)[0] + (got[rows].astype(f32) + got[rows + 1].astype(f32))
            mine = more.pop(0)
            if more:
                final_acts = more.pop(0)
            for group in rest:
                own, tot = share_out(own, tot, group)
                mine = block_of(mine, group.me, mine.shape[0] // group.size)
            for group in pairs:
                own, tot = sum_pair(own, tot, group)
            if i == 0:
                totals = tot
            part = (mine.astype(f32) * own / totals[None, :]).astype(bf16)
            for group in reversed(rest):
                part = gather(part, group)
            parts.append(part)
        first, second = [gather(part, core) for part in parts]
        if last:
            return (final_acts, jnp.concatenate([first, second], axis=0))
        numer, colsum = activation_numerator(powers[0], first, acts)
        acts = new_activations(powers[1], second, acts, numer, colsum)
        weights = [(first, 0), (second, 0)]


def solution(mesh):
    in_specs = (P(("groups", "tm")), P(), P(), P(None, ("groups", "tm")))
    out_specs = (P(None, ("groups", "tm")), P("groups", None))
    return jax.shard_map(
        on_device, mesh=mesh, in_specs=in_specs, out_specs=out_specs, check_vma=False
    )
```

time: 112 us -> 103 us (0.920)
  waiting for transfers between devices: 43.9 us -> 21.3 us
  starting transfers between devices: 28 us -> 46.8 us
  local copies, waits for them, and re-layouts: 8.67 us -> 2.37 us
  Pallas kernels: 25.4 us -> 28 us
  other arithmetic: 4.33 us -> 2.96 us
    ppermute x16 -> x20, waiting for transfers between devices: 27.3 us -> 11.6 us  [the longest x8 8.69 us: swap(): lax.ppermute(jnp.concatenate([send, hi[None], lo[None], pad], axis=0), 't...]
    ppermute x16 -> x20, starting transfers between devices: 14.4 us -> 25.6 us  [the longest x8 14.3 us: swap(): lax.ppermute(jnp.concatenate([send, hi[None], lo[None], pad], axis=0), 't...]
    ppermute x12 -> x16, waiting for transfers between devices: 16.6 us -> 9.06 us  [gather(): got = lax.ppermute(part, 'tm', perm)]
    ppermute x12 -> x16, starting transfers between devices: 8.23 us -> 15 us  [gather(): got = lax.ppermute(part, 'tm', perm)]
    unnamed x24 -> x6, local copies, waits for them, and re-layouts: 4.83 us -> 0.98 us
    slice x4 -> x0, local copies, waits for them, and re-layouts: 2.78 us -> none  [the longest x2 2.74 us: on_device(): weights = [templates[:cut], templates[cut:]]]
    pallas_call x7 -> x11, Pallas kernels: 25.4 us -> 28 us  [call(): pl.pallas_call(kernel, out_shape=tuple(outs), in_specs=specs or [VMEM] *...]
    select_n x12 -> x0, other arithmetic: 1.34 us -> none  [gather(): jnp.where(bit == 0, jnp.concatenate([part, got], axis=0), jnp.concatenate...]
  transfers between devices with their start and end apart: 30 -> 38, of which waited for: 23 -> 18; matrix products, arithmetic and copies ran while one was open for 5% -> 2% of each run, Pallas kernels for 2% -> 4%
where the time goes in v3:
time: 103 us
  starting transfers between devices  46.8 us (45%)
  Pallas kernels  28 us (27%)
  waiting for transfers between devices  21.3 us (21%)
  other arithmetic  2.96 us (3%)
  local copies, waits for them, and re-layouts  2.37 us (2%)
  between operations  1.15 us (1%)
    pallas_call x11, Pallas kernels, call(): pl.pallas_call(kernel, out_shape=tuple(outs), in_specs=specs or [VMEM] *...  28 us
    ppermute x16, starting transfers between devices, gather(): got = lax.ppermute(part, 'tm', perm)  15 us
    ppermute x8, starting transfers between devices, swap(): lax.ppermute(jnp.concatenate([send, hi[None], lo[None], pad], axis=0), 't...  14.3 us
    ppermute x8, starting transfers between devices, swap(): return (lax.ppermute(send, 'tm', perm).astype(f32), None)  10.2 us
    ppermute x16, waiting for transfers between devices, gather(): got = lax.ppermute(part, 'tm', perm)  9.06 us
    ppermute x8, waiting for transfers between devices, swap(): lax.ppermute(jnp.concatenate([send, hi[None], lo[None], pad], axis=0), 't...  8.69 us
    ppermute x1, starting transfers between devices, halo_rows(): two = lax.ppermute(jnp.where(odd, tail, head), 'tm', outer)  5.67 us
    ppermute x8, waiting for transfers between devices, swap(): return (lax.ppermute(send, 'tm', perm).astype(f32), None)  2.88 us
  transfers between devices with their start and end apart: 38, of which 18 were waited for; matrix products, arithmetic and copies ran while one was open for 2% of the time, Pallas kernels for 4%

profile of v3, /device:TPU:0, one launch (start us, length us, event | category | flops | bytes accessed | tf_op | source)
XLA Modules:
  0.0 102.5 jit_solution(2533183083798107701)
XLA Ops:
  1.8 5.7 %collective-permute-start.1 = (bf16[2,128]{1,0:T(2,128)(2,1)S(1)}, bf16[2,128]{1,0:T(2,128)(2,1)S(1)}, u32[]{:S(2)}, u32[]{:S(2)}) collective-permute-start(bf16[2,128]{1,0:T(2,128)(2,1)S(1)} %get-tuple-element.50), channel_id=1, source_target_pairs={{0,15},{1,2},{2,1},{3,4},{4,3},{5,6},{6,5},{7,8},{8,7},{9,10},{10,... | collective-permute-start | bytes 1544 | tf_op jit(solution)/shard_map/ppermute | solution.py:253
  8.8 12.6 %shard_map.59 = (bf16[640,1024]{1,0:T(8,128)(2,1)S(1)}, bf16[512,1024]{1,0:T(8,128)(2,1)S(1)}, bf16[512,1024]{1,0:T(8,128)(2,1)S(1)}) custom-call(f32[4,128]{1,0:T(4,128)S(1)} %maximum_convert_fusion.halo_ref, bf16[4096,128]{1,0:T(8,128)(2,1)} %bitcast.13, bf16[2304,1024]{1,0:T(8,128)(2,1)} %k_hbm.1, bf16[1152,512]{1,0:T(8,128)(2,1)} %w_ref.7, ...), custom_call_target="tpu_custom_call" | custom-call | flops 724775731200 | bytes 1140531200 | tf_op jit(solution)/shard_map/pallas_call | solution.py:164
  22.9 1.5 %shard_map.63 = bf16[336,512]{1,0:T(8,128)(2,1)S(1)} custom-call(s32[1]{0:T(128)} %bitcast.4.at_ref, bf16[640,1024]{1,0:T(8,128)(2,1)S(1)} %get-tuple-element.22.p_ref, bf16[1152,512]{1,0:T(8,128)(2,1)S(1)} %copy-done, bf16[512,1024]{1,0:T(8,128)(2,1)S(1)} %get-tuple-element.19.h_ref), custom_call_target="tpu_custom_call" | custom-call | flops 67108864000 | bytes 388301184 | tf_op jit(solution)/shard_map/pallas_call | solution.py:164
  29.3 2.5 %collective-permute-start.9 = (bf16[88,512]{1,0:T(8,128)(2,1)S(1)}, bf16[88,512]{1,0:T(8,128)(2,1)S(1)}, u32[]{:S(2)}, u32[]{:S(2)}) collective-permute-start(bf16[88,512]{1,0:T(8,128)(2,1)S(1)} %get-tuple-element.69), channel_id=1, source_target_pairs={{0,4},{1,5},{2,6},{3,7},{4,0},{5,1},{6,2},{7,3},{8,12},{9,13},{10,... | collective-permute-start | bytes 270344 | tf_op jit(solution)/shard_map/ppermute | solution.py:287
  36.3 3.8 %collective-permute-start.11 = (bf16[88,512]{1,0:T(8,128)(2,1)S(1)}, bf16[88,512]{1,0:T(8,128)(2,1)S(1)}, u32[]{:S(2)}, u32[]{:S(2)}) collective-permute-start(bf16[88,512]{1,0:T(8,128)(2,1)S(1)} %maximum_maximum_fusion), channel_id=1, source_target_pairs={{0,8},{1,9},{2,10},{3,11},{4,12},{5,13},{6,14},{7,15},{8,0},{9,1},... | collective-permute-start | bytes 270344 | tf_op jit(solution)/shard_map/ppermute | solution.py:287
  40.8 2.1 %collective-permute-start.6 = (bf16[64,512]{1,0:T(8,128)(2,1)S(1)}, bf16[64,512]{1,0:T(8,128)(2,1)S(1)}, u32[]{:S(2)}, u32[]{:S(2)}) collective-permute-start(bf16[64,512]{1,0:T(8,128)(2,1)S(1)} %add_convert_fusion.3), channel_id=1, source_target_pairs={{0,8},{1,9},{2,10},{3,11},{4,12},{5,13},{6,14},{7,15},{8,0},{9,1},... | collective-permute-start | bytes 196616 | tf_op jit(solution)/shard_map/ppermute | solution.py:284
  42.9 2.1 %collective-permute-done.11 = bf16[88,512]{1,0:T(8,128)(2,1)S(1)} collective-permute-done((bf16[88,512]{1,0:T(8,128)(2,1)S(1)}, bf16[88,512]{1,0:T(8,128)(2,1)S(1)}, u32[]{:S(2)}, u32[]{:S(2)}) %collective-permute-start.11) | collective-permute-done | bytes 90144 | tf_op jit(solution)/shard_map/ppermute | solution.py:287
  46.7 2.1 %collective-permute-start.16 = (bf16[80,512]{1,0:T(8,128)(2,1)S(1)}, bf16[80,512]{1,0:T(8,128)(2,1)S(1)}, u32[]{:S(2)}, u32[]{:S(2)}) collective-permute-start(bf16[80,512]{1,0:T(8,128)(2,1)S(1)} %get-tuple-element.43), channel_id=1, source_target_pairs={{0,2},{1,3},{2,0},{3,1},{4,6},{5,7},{6,4},{7,5},{8,10},{9,11},{10,... | collective-permute-start | bytes 245768 | tf_op jit(solution)/shard_map/ppermute | solution.py:323
  48.8 1.5 %collective-permute-start.18 = (bf16[80,512]{1,0:T(8,128)(2,1)S(1)}, bf16[80,512]{1,0:T(8,128)(2,1)S(1)}, u32[]{:S(2)}, u32[]{:S(2)}) collective-permute-start(bf16[80,512]{1,0:T(8,128)(2,1)S(1)} %get-tuple-element.43), channel_id=1, source_target_pairs={{0,6},{1,7},{2,4},{3,5},{4,2},{5,3},{6,0},{7,1},{8,14},{9,15},{10,... | collective-permute-start | bytes 245768 | tf_op jit(solution)/shard_map/ppermute | solution.py:323
  51.7 2.0 %collective-permute-start.14 = (bf16[64,512]{1,0:T(8,128)(2,1)S(1)}, bf16[64,512]{1,0:T(8,128)(2,1)S(1)}, u32[]{:S(2)}, u32[]{:S(2)}) collective-permute-start(bf16[64,512]{1,0:T(8,128)(2,1)S(1)} %get-tuple-element.45), channel_id=1, source_target_pairs={{0,6},{1,7},{2,4},{3,5},{4,2},{5,3},{6,0},{7,1},{8,14},{9,15},{10,... | collective-permute-start | bytes 196616 | tf_op jit(solution)/shard_map/ppermute | solution.py:323
  55.1 1.8 %collective-permute-done.14 = bf16[64,512]{1,0:T(8,128)(2,1)S(1)} collective-permute-done((bf16[64,512]{1,0:T(8,128)(2,1)S(1)}, bf16[64,512]{1,0:T(8,128)(2,1)S(1)}, u32[]{:S(2)}, u32[]{:S(2)}) %collective-permute-start.14) | collective-permute-done | bytes 65568 | tf_op jit(solution)/shard_map/ppermute | solution.py:323
  59.0 2.1 %shard_map.64 = (f32[512,1024]{1,0:T(8,128)S(1)}, f32[512,128]{1,0:T(8,128)S(1)}) custom-call(bf16[640,1024]{1,0:T(8,128)(2,1)S(1)} %get-tuple-element.22.p_ref, bf16[640,512]{1,0:T(8,128)(2,1)S(1)} %constant_dynamic-update-slice_fusion.12.w_ref, bf16[512,1024]{1,0:T(8,128)(2,1)S(1)} %get-tuple-element.19.h_ref), custom_call_target="tpu_custom_call" | custom-call | flops 134217728000 | bytes 537395200 | tf_op jit(solution)/shard_map/pallas_call | solution.py:164
  61.1 1.7 %shard_map.65.h_ref = bf16[512,1024]{1,0:T(8,128)(2,1)S(1)} custom-call(bf16[512,1024]{1,0:T(8,128)(2,1)S(1)} %get-tuple-element.18.p_ref, bf16[512,512]{1,0:T(8,128)(2,1)S(1)} %constant_dynamic-update-slice_fusion.18.w_ref, bf16[512,1024]{1,0:T(8,128)(2,1)S(1)} %get-tuple-element.19.h_ref, f32[512,1024]{1,0:T(8,128)S(1)} %get-tuple-element.26.refs_0_, ...), custom_call_target="tpu_custom_call" | custom-call | flops 107374182400 | bytes 602931200 | tf_op jit(solution)/shard_map/pallas_call | solution.py:164
  64.3 1.5 %shard_map.68 = bf16[336,512]{1,0:T(8,128)(2,1)S(1)} custom-call(s32[1]{0:T(128)} %bitcast.4.at_ref, bf16[640,1024]{1,0:T(8,128)(2,1)S(1)} %get-tuple-element.22.p_ref, bf16[640,512]{1,0:T(8,128)(2,1)S(1)} %constant_dynamic-update-slice_fusion.12.w_ref, bf16[512,1024]{1,0:T(8,128)(2,1)S(1)} %shard_map.65.h_ref), custom_call_target="tpu_custom_call" | custom-call | flops 67108864000 | bytes 335872384 | tf_op jit(solution)/shard_map/pallas_call | solution.py:164
  67.6 2.1 %shard_map.66 = (f32[256,512]{1,0:T(8,128)S(1)}, bf16[256,512]{1,0:T(8,128)(2,1)S(1)}, bf16[512,1024]{1,0:T(8,128)(2,1)}) custom-call(s32[1]{0:T(128)} %bitcast.at_ref, bf16[512,1024]{1,0:T(8,128)(2,1)S(1)} %get-tuple-element.18.p_ref, bf16[512,512]{1,0:T(8,128)(2,1)S(1)} %constant_dynamic-update-slice_fusion.18.w_ref, bf16[512,1024]{1,0:T(8,128)(2,1)S(1)} %shard_map.65.h_ref), custom_call_target="tpu_custom_call" | custom-call | flops 53687091200 | bytes 445645184 | tf_op jit(solution)/shard_map/pallas_call | solution.py:164
  71.1 2.0 %collective-permute-start.22 = (bf16[88,512]{1,0:T(8,128)(2,1)S(1)}, bf16[88,512]{1,0:T(8,128)(2,1)S(1)}, u32[]{:S(2)}, u32[]{:S(2)}) collective-permute-start(bf16[88,512]{1,0:T(8,128)(2,1)S(1)} %get-tuple-element.66), channel_id=1, source_target_pairs={{0,4},{1,5},{2,6},{3,7},{4,0},{5,1},{6,2},{7,3},{8,12},{9,13},{10,... | collective-permute-start | bytes 270344 | tf_op jit(solution)/shard_map/ppermute | solution.py:287
  74.7 2.0 %collective-permute-start.31 = (bf16[64,512]{1,0:T(8,128)(2,1)S(1)}, bf16[64,512]{1,0:T(8,128)(2,1)S(1)}, u32[]{:S(2)}, u32[]{:S(2)}) collective-permute-start(bf16[64,512]{1,0:T(8,128)(2,1)S(1)} %get-tuple-element.60), channel_id=1, source_target_pairs={{0,4},{1,5},{2,6},{3,7},{4,0},{5,1},{6,2},{7,3},{8,12},{9,13},{10,... | collective-permute-start | bytes 196616 | tf_op jit(solution)/shard_map/ppermute | solution.py:284
  77.7 1.6 %collective-permute-done.23 = bf16[88,512]{1,0:T(8,128)(2,1)S(1)} collective-permute-done((bf16[88,512]{1,0:T(8,128)(2,1)S(1)}, bf16[88,512]{1,0:T(8,128)(2,1)S(1)}, u32[]{:S(2)}, u32[]{:S(2)}) %collective-permute-start.23) | collective-permute-done | bytes 90144 | tf_op jit(solution)/shard_map/ppermute | solution.py:287
  79.5 3.3 %collective-permute-start.24 = (bf16[88,512]{1,0:T(8,128)(2,1)S(1)}, bf16[88,512]{1,0:T(8,128)(2,1)S(1)}, u32[]{:S(2)}, u32[]{:S(2)}) collective-permute-start(bf16[88,512]{1,0:T(8,128)(2,1)S(1)} %maximum_maximum_fusion.1), channel_id=1, source_target_pairs={{0,8},{1,9},{2,10},{3,11},{4,12},{5,13},{6,14},{7,15},{8,0},{9,1},... | collective-permute-start | bytes 270344 | tf_op jit(solution)/shard_map/ppermute | solution.py:287
  82.9 2.5 %collective-permute-start.33 = (bf16[64,512]{1,0:T(8,128)(2,1)S(1)}, bf16[64,512]{1,0:T(8,128)(2,1)S(1)}, u32[]{:S(2)}, u32[]{:S(2)}) collective-permute-start(bf16[64,512]{1,0:T(8,128)(2,1)S(1)} %add_convert_fusion.2), channel_id=1, source_target_pairs={{0,8},{1,9},{2,10},{3,11},{4,12},{5,13},{6,14},{7,15},{8,0},{9,1},... | collective-permute-start | bytes 196616 | tf_op jit(solution)/shard_map/ppermute | solution.py:284
  85.4 2.8 %collective-permute-done.24 = bf16[88,512]{1,0:T(8,128)(2,1)S(1)} collective-permute-done((bf16[88,512]{1,0:T(8,128)(2,1)S(1)}, bf16[88,512]{1,0:T(8,128)(2,1)S(1)}, u32[]{:S(2)}, u32[]{:S(2)}) %collective-permute-start.24) | collective-permute-done | bytes 90144 | tf_op jit(solution)/shard_map/ppermute | solution.py:287
  91.2 2.6 %collective-permute-start.27 = (bf16[80,512]{1,0:T(8,128)(2,1)S(1)}, bf16[80,512]{1,0:T(8,128)(2,1)S(1)}, u32[]{:S(2)}, u32[]{:S(2)}) collective-permute-start(bf16[80,512]{1,0:T(8,128)(2,1)S(1)} %get-tuple-element.35), channel_id=1, source_target_pairs={{0,6},{1,7},{2,4},{3,5},{4,2},{5,3},{6,0},{7,1},{8,14},{9,15},{10,... | collective-permute-start | bytes 245768 | tf_op jit(solution)/shard_map/ppermute | solution.py:323
  94.2 2.0 %collective-permute-start.36 = (bf16[64,512]{1,0:T(8,128)(2,1)S(1)}, bf16[64,512]{1,0:T(8,128)(2,1)S(1)}, u32[]{:S(2)}, u32[]{:S(2)}) collective-permute-start(bf16[64,512]{1,0:T(8,128)(2,1)S(1)} %get-tuple-element.37), channel_id=1, source_target_pairs={{0,6},{1,7},{2,4},{3,5},{4,2},{5,3},{6,0},{7,1},{8,14},{9,15},{10,... | collective-permute-start | bytes 196616 | tf_op jit(solution)/shard_map/ppermute | solution.py:323
  96.1 1.9 %collective-permute-done.35 = bf16[64,512]{1,0:T(8,128)(2,1)S(1)} collective-permute-done((bf16[64,512]{1,0:T(8,128)(2,1)S(1)}, bf16[64,512]{1,0:T(8,128)(2,1)S(1)}, u32[]{:S(2)}, u32[]{:S(2)}) %collective-permute-start.35) | collective-permute-done | bytes 65568 | tf_op jit(solution)/shard_map/ppermute | solution.py:323
  (133 shorter events, 35.6 us)
Async XLA Ops:
  1.4 6.8 %collective-permute-start = (bf16[2,128]{1,0:T(2,128)(2,1)S(1)}, bf16[2,128]{1,0:T(2,128)(2,1)S(1)}, u32[]{:S(2)}, u32[]{:S(2)}) collective-permute-start(bf16[2,128]{1,0:T(2,128)(2,1)S(1)} %get-tuple-element.51), channel_id=1, source_target_pairs={{0,1},{1,0},{2,3},{3,2},{4,5},{5,4},{6,7},{7,6},{8,9},{9,8},{10,11... | collective-permute-start | bytes 1544 | tf_op jit(solution)/shard_map/ppermute | solution.py:252
  1.8 7.0 %collective-permute-start.1 = (bf16[2,128]{1,0:T(2,128)(2,1)S(1)}, bf16[2,128]{1,0:T(2,128)(2,1)S(1)}, u32[]{:S(2)}, u32[]{:S(2)}) collective-permute-start(bf16[2,128]{1,0:T(2,128)(2,1)S(1)} %get-tuple-element.50), channel_id=1, source_target_pairs={{0,15},{1,2},{2,1},{3,4},{4,3},{5,6},{6,5},{7,8},{8,7},{9,10},{10,... | collective-permute-start | bytes 1544 | tf_op jit(solution)/shard_map/ppermute | solution.py:253
  28.2 6.5 %collective-permute-start.10 = (bf16[88,512]{1,0:T(8,128)(2,1)S(1)}, bf16[88,512]{1,0:T(8,128)(2,1)S(1)}, u32[]{:S(2)}, u32[]{:S(2)}) collective-permute-start(bf16[88,512]{1,0:T(8,128)(2,1)S(1)} %get-tuple-element.68), channel_id=1, source_target_pairs={{0,6},{1,7},{2,4},{3,5},{4,2},{5,3},{6,0},{7,1},{8,14},{9,15},{10,... | collective-permute-start | bytes 270344 | tf_op jit(solution)/shard_map/ppermute | solution.py:287
  29.1 7.0 %collective-permute-start.8 = (bf16[88,512]{1,0:T(8,128)(2,1)S(1)}, bf16[88,512]{1,0:T(8,128)(2,1)S(1)}, u32[]{:S(2)}, u32[]{:S(2)}) collective-permute-start(bf16[88,512]{1,0:T(8,128)(2,1)S(1)} %get-tuple-element.67), channel_id=1, source_target_pairs={{0,2},{1,3},{2,0},{3,1},{4,6},{5,7},{6,4},{7,5},{8,10},{9,11},{10,... | collective-permute-start | bytes 270344 | tf_op jit(solution)/shard_map/ppermute | solution.py:287
  29.3 6.8 %collective-permute-start.9 = (bf16[88,512]{1,0:T(8,128)(2,1)S(1)}, bf16[88,512]{1,0:T(8,128)(2,1)S(1)}, u32[]{:S(2)}, u32[]{:S(2)}) collective-permute-start(bf16[88,512]{1,0:T(8,128)(2,1)S(1)} %get-tuple-element.69), channel_id=1, source_target_pairs={{0,4},{1,5},{2,6},{3,7},{4,0},{5,1},{6,2},{7,3},{8,12},{9,13},{10,... | collective-permute-start | bytes 270344 | tf_op jit(solution)/shard_map/ppermute | solution.py:287
  31.8 8.3 %collective-permute-start.3 = (bf16[64,512]{1,0:T(8,128)(2,1)S(1)}, bf16[64,512]{1,0:T(8,128)(2,1)S(1)}, u32[]{:S(2)}, u32[]{:S(2)}) collective-permute-start(bf16[64,512]{1,0:T(8,128)(2,1)S(1)} %get-tuple-element.61), channel_id=1, source_target_pairs={{0,2},{1,3},{2,0},{3,1},{4,6},{5,7},{6,4},{7,5},{8,10},{9,11},{10,... | collective-permute-start | bytes 196616 | tf_op jit(solution)/shard_map/ppermute | solution.py:284
  31.9 8.2 %collective-permute-start.4 = (bf16[64,512]{1,0:T(8,128)(2,1)S(1)}, bf16[64,512]{1,0:T(8,128)(2,1)S(1)}, u32[]{:S(2)}, u32[]{:S(2)}) collective-permute-start(bf16[64,512]{1,0:T(8,128)(2,1)S(1)} %get-tuple-element.63), channel_id=1, source_target_pairs={{0,4},{1,5},{2,6},{3,7},{4,0},{5,1},{6,2},{7,3},{8,12},{9,13},{10,... | collective-permute-start | bytes 196616 | tf_op jit(solution)/shard_map/ppermute | solution.py:284
  34.7 6.1 %collective-permute-start.5 = (bf16[64,512]{1,0:T(8,128)(2,1)S(1)}, bf16[64,512]{1,0:T(8,128)(2,1)S(1)}, u32[]{:S(2)}, u32[]{:S(2)}) collective-permute-start(bf16[64,512]{1,0:T(8,128)(2,1)S(1)} %get-tuple-element.62), channel_id=1, source_target_pairs={{0,6},{1,7},{2,4},{3,5},{4,2},{5,3},{6,0},{7,1},{8,14},{9,15},{10,... | collective-permute-start | bytes 196616 | tf_op jit(solution)/shard_map/ppermute | solution.py:284
  36.3 8.7 %collective-permute-start.11 = (bf16[88,512]{1,0:T(8,128)(2,1)S(1)}, bf16[88,512]{1,0:T(8,128)(2,1)S(1)}, u32[]{:S(2)}, u32[]{:S(2)}) collective-permute-start(bf16[88,512]{1,0:T(8,128)(2,1)S(1)} %maximum_maximum_fusion), channel_id=1, source_target_pairs={{0,8},{1,9},{2,10},{3,11},{4,12},{5,13},{6,14},{7,15},{8,0},{9,1},... | collective-permute-start | bytes 270344 | tf_op jit(solution)/shard_map/ppermute | solution.py:287
  40.8 5.6 %collective-permute-start.6 = (bf16[64,512]{1,0:T(8,128)(2,1)S(1)}, bf16[64,512]{1,0:T(8,128)(2,1)S(1)}, u32[]{:S(2)}, u32[]{:S(2)}) collective-permute-start(bf16[64,512]{1,0:T(8,128)(2,1)S(1)} %add_convert_fusion.3), channel_id=1, source_target_pairs={{0,8},{1,9},{2,10},{3,11},{4,12},{5,13},{6,14},{7,15},{8,0},{9,1},... | collective-permute-start | bytes 196616 | tf_op jit(solution)/shard_map/ppermute | solution.py:284
  46.7 10.3 %collective-permute-start.16 = (bf16[80,512]{1,0:T(8,128)(2,1)S(1)}, bf16[80,512]{1,0:T(8,128)(2,1)S(1)}, u32[]{:S(2)}, u32[]{:S(2)}) collective-permute-start(bf16[80,512]{1,0:T(8,128)(2,1)S(1)} %get-tuple-element.43), channel_id=1, source_target_pairs={{0,2},{1,3},{2,0},{3,1},{4,6},{5,7},{6,4},{7,5},{8,10},{9,11},{10,... | collective-permute-start | bytes 245768 | tf_op jit(solution)/shard_map/ppermute | solution.py:323
  48.8 8.3 %collective-permute-start.17 = (bf16[80,512]{1,0:T(8,128)(2,1)S(1)}, bf16[80,512]{1,0:T(8,128)(2,1)S(1)}, u32[]{:S(2)}, u32[]{:S(2)}) collective-permute-start(bf16[80,512]{1,0:T(8,128)(2,1)S(1)} %get-tuple-element.43), channel_id=1, source_target_pairs={{0,4},{1,5},{2,6},{3,7},{4,0},{5,1},{6,2},{7,3},{8,12},{9,13},{10,... | collective-permute-start | bytes 245768 | tf_op jit(solution)/shard_map/ppermute | solution.py:323
  48.8 8.3 %collective-permute-start.18 = (bf16[80,512]{1,0:T(8,128)(2,1)S(1)}, bf16[80,512]{1,0:T(8,128)(2,1)S(1)}, u32[]{:S(2)}, u32[]{:S(2)}) collective-permute-start(bf16[80,512]{1,0:T(8,128)(2,1)S(1)} %get-tuple-element.43), channel_id=1, source_target_pairs={{0,6},{1,7},{2,4},{3,5},{4,2},{5,3},{6,0},{7,1},{8,14},{9,15},{10,... | collective-permute-start | bytes 245768 | tf_op jit(solution)/shard_map/ppermute | solution.py:323
  70.6 6.2 %collective-permute-start.21 = (bf16[88,512]{1,0:T(8,128)(2,1)S(1)}, bf16[88,512]{1,0:T(8,128)(2,1)S(1)}, u32[]{:S(2)}, u32[]{:S(2)}) collective-permute-start(bf16[88,512]{1,0:T(8,128)(2,1)S(1)} %get-tuple-element.64), channel_id=1, source_target_pairs={{0,2},{1,3},{2,0},{3,1},{4,6},{5,7},{6,4},{7,5},{8,10},{9,11},{10,... | collective-permute-start | bytes 270344 | tf_op jit(solution)/shard_map/ppermute | solution.py:287
  71.1 6.6 %collective-permute-start.22 = (bf16[88,512]{1,0:T(8,128)(2,1)S(1)}, bf16[88,512]{1,0:T(8,128)(2,1)S(1)}, u32[]{:S(2)}, u32[]{:S(2)}) collective-permute-start(bf16[88,512]{1,0:T(8,128)(2,1)S(1)} %get-tuple-element.66), channel_id=1, source_target_pairs={{0,4},{1,5},{2,6},{3,7},{4,0},{5,1},{6,2},{7,3},{8,12},{9,13},{10,... | collective-permute-start | bytes 270344 | tf_op jit(solution)/shard_map/ppermute | solution.py:287
  73.2 6.2 %collective-permute-start.23 = (bf16[88,512]{1,0:T(8,128)(2,1)S(1)}, bf16[88,512]{1,0:T(8,128)(2,1)S(1)}, u32[]{:S(2)}, u32[]{:S(2)}) collective-permute-start(bf16[88,512]{1,0:T(8,128)(2,1)S(1)} %get-tuple-element.65), channel_id=1, source_target_pairs={{0,6},{1,7},{2,4},{3,5},{4,2},{5,3},{6,0},{7,1},{8,14},{9,15},{10,... | collective-permute-start | bytes 270344 | tf_op jit(solution)/shard_map/ppermute | solution.py:287
  74.1 8.7 %collective-permute-start.30 = (bf16[64,512]{1,0:T(8,128)(2,1)S(1)}, bf16[64,512]{1,0:T(8,128)(2,1)S(1)}, u32[]{:S(2)}, u32[]{:S(2)}) collective-permute-start(bf16[64,512]{1,0:T(8,128)(2,1)S(1)} %get-tuple-element.58), channel_id=1, source_target_pairs={{0,2},{1,3},{2,0},{3,1},{4,6},{5,7},{6,4},{7,5},{8,10},{9,11},{10,... | collective-permute-start | bytes 196616 | tf_op jit(solution)/shard_map/ppermute | solution.py:284
  74.7 8.1 %collective-permute-start.31 = (bf16[64,512]{1,0:T(8,128)(2,1)S(1)}, bf16[64,512]{1,0:T(8,128)(2,1)S(1)}, u32[]{:S(2)}, u32[]{:S(2)}) collective-permute-start(bf16[64,512]{1,0:T(8,128)(2,1)S(1)} %get-tuple-element.60), channel_id=1, source_target_pairs={{0,4},{1,5},{2,6},{3,7},{4,0},{5,1},{6,2},{7,3},{8,12},{9,13},{10,... | collective-permute-start | bytes 196616 | tf_op jit(solution)/shard_map/ppermute | solution.py:284
  76.8 6.1 %collective-permute-start.32 = (bf16[64,512]{1,0:T(8,128)(2,1)S(1)}, bf16[64,512]{1,0:T(8,128)(2,1)S(1)}, u32[]{:S(2)}, u32[]{:S(2)}) collective-permute-start(bf16[64,512]{1,0:T(8,128)(2,1)S(1)} %get-tuple-element.59), channel_id=1, source_target_pairs={{0,6},{1,7},{2,4},{3,5},{4,2},{5,3},{6,0},{7,1},{8,14},{9,15},{10,... | collective-permute-start | bytes 196616 | tf_op jit(solution)/shard_map/ppermute | solution.py:284
  79.5 8.6 %collective-permute-start.24 = (bf16[88,512]{1,0:T(8,128)(2,1)S(1)}, bf16[88,512]{1,0:T(8,128)(2,1)S(1)}, u32[]{:S(2)}, u32[]{:S(2)}) collective-permute-start(bf16[88,512]{1,0:T(8,128)(2,1)S(1)} %maximum_maximum_fusion.1), channel_id=1, source_target_pairs={{0,8},{1,9},{2,10},{3,11},{4,12},{5,13},{6,14},{7,15},{8,0},{9,1},... | collective-permute-start | bytes 270344 | tf_op jit(solution)/shard_map/ppermute | solution.py:287
  82.9 6.0 %collective-permute-start.33 = (bf16[64,512]{1,0:T(8,128)(2,1)S(1)}, bf16[64,512]{1,0:T(8,128)(2,1)S(1)}, u32[]{:S(2)}, u32[]{:S(2)}) collective-permute-start(bf16[64,512]{1,0:T(8,128)(2,1)S(1)} %add_convert_fusion.2), channel_id=1, source_target_pairs={{0,8},{1,9},{2,10},{3,11},{4,12},{5,13},{6,14},{7,15},{8,0},{9,1},... | collective-permute-start | bytes 196616 | tf_op jit(solution)/shard_map/ppermute | solution.py:284
  90.2 9.2 %collective-permute-start.25 = (bf16[80,512]{1,0:T(8,128)(2,1)S(1)}, bf16[80,512]{1,0:T(8,128)(2,1)S(1)}, u32[]{:S(2)}, u32[]{:S(2)}) collective-permute-start(bf16[80,512]{1,0:T(8,128)(2,1)S(1)} %get-tuple-element.35), channel_id=1, source_target_pairs={{0,2},{1,3},{2,0},{3,1},{4,6},{5,7},{6,4},{7,5},{8,10},{9,11},{10,... | collective-permute-start | bytes 245768 | tf_op jit(solution)/shard_map/ppermute | solution.py:323
  91.2 8.3 %collective-permute-start.26 = (bf16[80,512]{1,0:T(8,128)(2,1)S(1)}, bf16[80,512]{1,0:T(8,128)(2,1)S(1)}, u32[]{:S(2)}, u32[]{:S(2)}) collective-permute-start(bf16[80,512]{1,0:T(8,128)(2,1)S(1)} %get-tuple-element.35), channel_id=1, source_target_pairs={{0,4},{1,5},{2,6},{3,7},{4,0},{5,1},{6,2},{7,3},{8,12},{9,13},{10,... | collective-permute-start | bytes 245768 | tf_op jit(solution)/shard_map/ppermute | solution.py:323
  91.2 8.3 %collective-permute-start.27 = (bf16[80,512]{1,0:T(8,128)(2,1)S(1)}, bf16[80,512]{1,0:T(8,128)(2,1)S(1)}, u32[]{:S(2)}, u32[]{:S(2)}) collective-permute-start(bf16[80,512]{1,0:T(8,128)(2,1)S(1)} %get-tuple-element.35), channel_id=1, source_target_pairs={{0,6},{1,7},{2,4},{3,5},{4,2},{5,3},{6,0},{7,1},{8,14},{9,15},{10,... | collective-permute-start | bytes 245768 | tf_op jit(solution)/shard_map/ppermute | solution.py:323
  (17 other events, 60.5 us)

commit v4 on v3

v4 whole, which is shorter than its diff:
```python
import functools

import jax
import jax.numpy as jnp
from jax import lax
from jax.experimental import pallas as pl
from jax.experimental.pallas import tpu as pltpu
from jax.sharding import PartitionSpec as P

HOP = 512
ITERS = 2
HALF = 256
TILE = 256
LANES = 128
bf16 = jnp.bfloat16
f32 = jnp.float32
DIRECT = ((False, True), (True, False))
NT = (((1,), (1,)), ((), ()))


def inverse(x):
    r = pl.reciprocal(x, approx=True)
    return r * (2.0 - x * r)


def dot(a, b):
    return jnp.dot(a, b, preferred_element_type=f32)


def dot_nt(a, b):
    return lax.dot_general(a, b, NT, preferred_element_type=f32)


def row_blocks(rows):
    if rows < TILE:
        return [(0, rows)]
    first = rows % TILE
    cuts = [0] + list(range(first + TILE if first else TILE, rows + 1, TILE))
    return list(zip(cuts[:-1], cuts[1:]))


def analyse_kernel(rows, at_ref, halo_ref, a_hbm, k_hbm, w_hbm, h_hbm, p_ref, new_ref, w_ref,
                   a_ref, k_ref, h_ref, wide, frame, wt, a_sem, k_sem, w_sem, h_sem):
    bins = w_ref.shape[0]
    frames = h_ref.shape[1]
    blocks = row_blocks(bins)
    a_copy = pltpu.make_async_copy(a_hbm, a_ref, a_sem)
    a_copy.start()
    k_copies, w_copies = [], []
    for n in range(bins // rows):
        start = pl.multiple_of(at_ref[n] * rows, 16)
        here = pl.ds(n * rows, rows)
        for m in range(2):
            k_copies.append(
                pltpu.make_async_copy(
                    k_hbm.at[pl.ds(m * bins + start, rows)],
                    k_ref.at[pl.ds(m * bins + n * rows, rows)],
                    k_sem.at[2 * n + m],
                )
            )
        w_copies.append(pltpu.make_async_copy(w_hbm.at[pl.ds(start, rows)], w_ref.at[here], w_sem.at[n]))
    h_copy = pltpu.make_async_copy(h_hbm, h_ref, h_sem)
    for copy in k_copies + w_copies + [h_copy]:
        copy.start()

    a_copy.wait()
    wide[8 : 8 + a_ref.shape[0], :] = a_ref[...].astype(f32)
    wide[6:8, :] = halo_ref[0:2, :]
    wide[8 + a_ref.shape[0] : 10 + a_ref.shape[0], :] = halo_ref[2:4, :]
    for j in range(2 * HOP // LANES):
        strip = wide[pl.ds(6 + j, frames, stride=HOP // LANES), :]
        frame[:, j * LANES : (j + 1) * LANES] = strip.astype(bf16)

    waited = 0
    for lo, hi in blocks:
        while waited < -(-hi // rows):
            k_copies[2 * waited].wait()
            k_copies[2 * waited + 1].wait()
            waited += 1
        for t in range(0, frames, TILE):
            f = frame[t : t + TILE, :]
            re = dot_nt(k_ref[lo:hi, :], f)
            im = dot_nt(k_ref[bins + lo : bins + hi, :], f)
            p_ref[lo:hi, t : t + TILE] = (re * re + im * im).astype(bf16)

    for copy in w_copies + [h_copy]:
        copy.wait()
    wt[...] = w_ref[...].T
    inv = inverse(jnp.sum(wt[...].astype(f32), axis=1, keepdims=True))
    for t in range(0, frames, TILE):
        tile = slice(t, t + TILE)
        h = h_ref[:, tile]
        numer = None
        for lo, hi in blocks:
            model = dot(w_ref[lo:hi, :], h)
            ratio = (p_ref[lo:hi, tile].astype(f32) * inverse(model)).astype(bf16)
            part = dot(wt[:, lo:hi], ratio)
            numer = part if numer is None else numer + part
        new_ref[:, tile] = (h.astype(f32) * numer * inv).astype(bf16)


def template_kernel(size, p_base, w_base, extras, p_ref, w_ref, h_ref, *outs):
    frames = h_ref.shape[1]
    outs = list(outs)
    numw_ref = outs.pop(0)
    for lo, hi in row_blocks(size):
        w = w_ref[w_base + lo : w_base + hi, :]
        acc = None
        for t in range(0, frames, TILE):
            h = h_ref[:, t : t + TILE]
            model = dot(w, h)
            p = p_ref[p_base + lo : p_base + hi, t : t + TILE]
            ratio = (p.astype(f32) * inverse(model)).astype(bf16)
            part = dot_nt(ratio, h)
            acc = part if acc is None else acc + part
        numw_ref[lo:hi, :] = acc.astype(numw_ref.dtype)
    if "send" in extras or "totals" in extras:
        total = dot_nt(jnp.ones((16, frames), bf16), h_ref[...])
        high = total.astype(bf16).astype(f32)
        low = (total - high).astype(bf16).astype(f32)
        if "send" in extras:
            row = lax.broadcasted_iota(jnp.int32, total.shape, 0)
            both = jnp.where(row == 0, high, jnp.where(row == 1, low, 0.0))
            numw_ref[size : size + 16, :] = both.astype(bf16)
        else:
            outs.pop(0)[...] = (high + low)[:8]
    if "templates" in extras:
        outs.pop(0)[...] = w_ref[w_base : w_base + size, :]
    if "copy" in extras:
        outs.pop(0)[...] = h_ref[...]


def activation_kernel(first, base, p_ref, w_ref, h_ref, *refs):
    if first:
        numer_ref, col_ref, wt = refs
    else:
        old_ref, oldcol_ref, new_ref, wt = refs
    frames = h_ref.shape[1]
    wt[...] = w_ref[...].T
    col = jnp.sum(wt[...].astype(f32), axis=1, keepdims=True)
    if first:
        col_ref[...] = jnp.broadcast_to(col, col_ref.shape)
    else:
        inv = inverse(col + oldcol_ref[:, :1])
    for t in range(0, frames, TILE):
        tile = slice(t, t + TILE)
        h = h_ref[:, tile]
        numer = None if first else old_ref[:, tile]
        for lo, hi in row_blocks(w_ref.shape[0]):
            model = dot(w_ref[lo:hi, :], h)
            p = p_ref[base + lo : base + hi, tile]
            ratio = (p.astype(f32) * inverse(model)).astype(bf16)
            part = dot(wt[:, lo:hi], ratio)
            numer = part if numer is None else numer + part
        if first:
            numer_ref[:, tile] = numer
        else:
            new_ref[:, tile] = (h.astype(f32) * numer * inv).astype(bf16)


def place_kernel(rows, at_ref, own_ref, other_ref, out_ref, sems):
    blocks = own_ref.shape[0] // rows
    copies = []
    for n in range(2 * blocks):
        ref, m = (own_ref, n) if n < blocks else (other_ref, n - blocks)
        start = pl.multiple_of(at_ref[n] * rows, 16)
        source = ref.at[pl.ds(m * rows, rows)]
        copies.append(pltpu.make_async_copy(source, out_ref.at[pl.ds(start, rows)], sems.at[n]))
        copies[-1].start()
    for copy in copies:
        copy.wait()


VMEM = pl.BlockSpec(memory_space=pltpu.VMEM)
HBM = pl.BlockSpec(memory_space=pltpu.HBM)
SMEM = pl.BlockSpec(memory_space=pltpu.SMEM)
ANY = pl.BlockSpec(memory_space=pl.ANY)


def call(kernel, outs, scratch, flops, *args, specs=None, out_spec=None, mib=16):
    size = sum(a.size * a.dtype.itemsize for a in args)
    size += sum(o.size * o.dtype.itemsize for o in outs)
    return pl.pallas_call(
        kernel,
        out_shape=tuple(outs),
        in_specs=specs or [VMEM] * len(args),
        out_specs=tuple([out_spec or VMEM] * len(outs)),
        scratch_shapes=scratch,
        cost_estimate=pl.CostEstimate(flops=flops, bytes_accessed=size, transcendentals=0),
        compiler_params=pltpu.CompilerParams(vmem_limit_bytes=mib * 1024 * 1024),
    )(*args)


def shape(dims, dtype):
    return jax.ShapeDtypeStruct(dims, dtype)


def analyse(at, audio, halo, kernel, weights, acts):
    bins, comps = weights.shape
    frames = acts.shape[1]
    blocks = at.shape[0]
    return call(
        functools.partial(analyse_kernel, bins // blocks),
        [shape((bins, frames), bf16), shape((comps, frames), bf16), shape((bins, comps), bf16)],
        [
            pltpu.VMEM(audio.shape, bf16),
            pltpu.VMEM(kernel.shape, bf16),
            pltpu.VMEM(acts.shape, bf16),
            pltpu.VMEM((audio.shape[0] + 16, LANES), f32),
            pltpu.VMEM((frames, 2 * HOP), bf16),
            pltpu.VMEM((comps, bins), bf16),
            pltpu.SemaphoreType.DMA,
            pltpu.SemaphoreType.DMA((2 * blocks,)),
            pltpu.SemaphoreType.DMA((blocks,)),
            pltpu.SemaphoreType.DMA,
        ],
        2 * bins * frames * (4 * HOP + 2 * comps),
        at, halo, *[pltpu.with_memory_space_constraint(x, pltpu.HBM) for x in (audio, kernel, weights, acts)],
        specs=[SMEM, VMEM, HBM, HBM, HBM, HBM],
        mib=32,
    )


def template_numerator(size, power, p_base, weights, w_base, acts, extras):
    comps = acts.shape[0]
    outs = [shape((size + 16, comps), bf16) if "send" in extras else shape((size, comps), f32)]
    if "totals" in extras:
        outs.append(shape((8, comps), f32))
    if "templates" in extras:
        outs.append(shape((size, comps), bf16))
    if "copy" in extras:
        outs.append(shape(acts.shape, bf16))
    kernel = functools.partial(template_kernel, size, p_base, w_base, extras)
    return call(kernel, outs, [], 4 * size * acts.size, power, weights, acts)


def activation_numerator(power, base, weights, acts):
    size, comps = weights.shape
    return call(
        functools.partial(activation_kernel, True, base),
        [shape(acts.shape, f32), shape((comps, 128), f32)],
        [pltpu.VMEM((comps, size), bf16)],
        4 * size * acts.size, power, weights, acts,
    )


def new_activations(power, base, weights, acts, numer, colsum):
    size, comps = weights.shape
    return call(
        functools.partial(activation_kernel, False, base),
        [shape(acts.shape, bf16)],
        [pltpu.VMEM((comps, size), bf16)],
        4 * size * acts.size, power, weights, acts, numer, colsum,
    )[0]


def halo_rows(audio, peers):
    me = lax.axis_index("tm")
    odd = me % 2 == 1
    rows = HALF // LANES
    head, tail = audio[:rows], audio[audio.shape[0] - rows :]
    inner = [(i, i ^ 1) for i in range(peers)]
    outer = [(i, (i + 1) % peers if i % 2 else (i - 1) % peers) for i in range(peers)]
    one = lax.ppermute(jnp.where(odd, head, tail), "tm", inner)
    two = lax.ppermute(jnp.where(odd, tail, head), "tm", outer)
    two = jnp.where((me == 0) | (me == peers - 1), jnp.zeros_like(two), two)
    left = jnp.where(odd, one, two)
    right = jnp.where(odd, two, one)
    return jnp.concatenate([left, right], axis=0).astype(f32)


class Group:
    def __init__(self, bits, peers):
        me = lax.axis_index("tm")
        self.size = 1 << len(bits)
        self.me = sum(((me // b) % 2) << j for j, b in enumerate(bits))
        self.others = []
        for code in range(1, self.size):
            mask = sum(b for j, b in enumerate(bits) if code >> j & 1)
            self.others.append((code, [(i, i ^ mask) for i in range(peers)]))


def groups_of(peers):
    bits = [1 << b for b in range(peers.bit_length() - 1)]
    return Group(bits[:1], peers), Group(bits[1:3], peers), [Group([b], peers) for b in bits[3:]]


def halves_of(totals):
    hi = totals.astype(bf16)
    lo = (totals - hi.astype(f32)).astype(bf16)
    return (hi, lo), hi.astype(f32) + lo.astype(f32)


def swap(send, halves, perm):
    if halves is None:
        return lax.ppermute(send, "tm", perm), None
    rows = send.shape[0]
    pad = jnp.zeros((14, send.shape[1]), bf16)
    got = lax.ppermute(jnp.concatenate([send, halves[0][None], halves[1][None], pad], axis=0), "tm", perm)
    return got[:rows], got[rows].astype(f32) + got[rows + 1].astype(f32)


def sum_chips(mine, others, total, quad, pairs, direct):
    halves = None
    if total is not None:
        halves, total = halves_of(total)
    perms = [perm for _, perm in quad.others]
    if direct:
        for other, perm in zip(others, perms):
            more, part = swap(other.astype(bf16), halves, perm)
            mine = mine + more.astype(f32)
            total = None if total is None else total + part
    else:
        rows = mine.shape[0]
        more = lax.ppermute(jnp.concatenate([others[0], others[2]]).astype(bf16), "tm", perms[0])
        far = (others[1] + more[rows:].astype(f32)).astype(bf16)
        mine = mine + more[:rows].astype(f32)
        mine = mine + lax.ppermute(far, "tm", perms[1]).astype(f32)
    for group in pairs:
        if total is not None:
            halves, total = halves_of(total)
        mine = mine.astype(bf16)
        more, part = swap(mine, halves, group.others[0][1])
        mine = mine.astype(f32) + more.astype(f32)
        total = None if total is None else total + part
    return mine, total


def spread(part, quad, direct):
    perms = [perm for _, perm in quad.others]
    if direct:
        return [part] + [lax.ppermute(part, "tm", perm) for perm in perms]
    rows = part.shape[0]
    far = lax.ppermute(part, "tm", perms[1])
    got = lax.ppermute(jnp.concatenate([part, far]), "tm", perms[0])
    return [part, got[:rows], far, got[rows:]]


def on_device(audio, kernel, templates, activations):
    peers = lax.axis_size("tm")
    bins = templates.shape[0]
    size = bins // 2
    audio = audio.reshape(audio.shape[0] // LANES, LANES)
    halo = halo_rows(audio, peers)
    core, quad, pairs = groups_of(peers)
    rows = size // quad.size
    cuts = [0, (rows // 2 + 15) // 16 * 16, rows]
    order = [quad.me] + [quad.me ^ code for code, _ in quad.others]
    at = [core.me * quad.size + q for q in order] + [(1 - core.me) * quad.size + q for q in order]
    at = jnp.stack(at).astype(jnp.int32)
    power, acts, weights = analyse(at, audio, halo, kernel, templates, activations)
    own_w, other_w, base = weights, weights, size
    for step in range(ITERS):
        last = step == ITERS - 1
        (send,) = template_numerator(size, power, size, other_w, base, acts, ("send",))
        got = lax.ppermute(send, "tm", core.others[0][1])
        rest, total = template_numerator(size - rows, power, rows, own_w, rows, acts, ("totals",))
        extras = ("templates",) + (("copy",) if last else ())
        mine, weights, *copied = template_numerator(rows, power, 0, own_w, 0, acts, extras)
        rest = rest + got[rows:size].astype(f32)
        mine = mine + got[:rows].astype(f32)
        total = total[0] + (got[size].astype(f32) + got[size + 1].astype(f32))
        pieces, rowsum = [], None
        for lo, hi in zip(cuts[:-1], cuts[1:]):
            others = [rest[n * rows + lo : n * rows + hi] for n in range(quad.size - 1)]
            part, tot = sum_chips(
                mine[lo:hi], others, total if lo == 0 else None, quad, pairs, DIRECT[0][lo == 0]
            )
            rowsum = tot if lo == 0 else rowsum
            part = (weights[lo:hi].astype(f32) * part / rowsum[None, :]).astype(bf16)
            pieces.append(spread(part, quad, DIRECT[1][lo == 0]))
        own_w = jnp.concatenate([piece[n] for n in range(quad.size) for piece in pieces], axis=0)
        other_w, base = lax.ppermute(own_w, "tm", core.others[0][1]), 0
        if not last:
            numer, colsum = activation_numerator(power, 0, own_w, acts)
            acts = new_activations(power, size, other_w, acts, numer, colsum)
    kernel = functools.partial(place_kernel, rows)
    out = call(
        kernel, [shape(templates.shape, bf16)], [pltpu.SemaphoreType.DMA((at.shape[0],))], 0,
        at, own_w, other_w, specs=[SMEM, ANY, ANY], out_spec=ANY,
    )
    return (copied[0], out[0])


def solution(mesh):
    in_specs = (P(("groups", "tm")), P(), P(), P(None, ("groups", "tm")))
    out_specs = (P(None, ("groups", "tm")), P("groups", None))
    return jax.shard_map(
        on_device, mesh=mesh, in_specs=in_specs, out_specs=out_specs, check_vma=False
    )
```

time: 103 us -> 100 us (0.971)
  starting transfers between devices: 46.8 us -> 37.5 us
  waiting for transfers between devices: 21.3 us -> 28.5 us
  Pallas kernels: 28 us -> 30.4 us
  local copies, waits for them, and re-layouts: 2.37 us -> 0.3 us
  other arithmetic: 2.96 us -> 1.93 us
    ppermute x32 -> x26, starting transfers between devices: 39.5 us -> 31.5 us  [the longest x8 12.2 us: swap(): lax.ppermute(jnp.concatenate([send, halves[0][None], halves[1][None], pad...]
    ppermute x32 -> x26, waiting for transfers between devices: 20.6 us -> 27.2 us  [the longest x8 14.9 us: swap(): lax.ppermute(jnp.concatenate([send, halves[0][None], halves[1][None], pad...]
    pallas_call x11 -> x10, Pallas kernels: 28 us -> 30.4 us  [call(): pl.pallas_call(kernel, out_shape=tuple(outs), in_specs=specs or [VMEM] *...]
    concatenate x5 -> x8, other arithmetic: 1.48 us -> 0.45 us  [the longest x4 0.4 us: swap(): jnp.concatenate([send, halves[0][None], halves[1][None], pad], axis=0)]
  transfers between devices with their start and end apart: 38 -> 30, of which waited for: 18 -> 17; matrix products, arithmetic and copies ran while one was open for 2% -> 1% of each run, Pallas kernels for 4% -> 8%
where the time goes in v4:
time: 100 us; the launch traced here: 99.8 us
  starting transfers between devices  37.5 us (38%)
  Pallas kernels  30.4 us (30%)
  waiting for transfers between devices  28.5 us (28%)
  other arithmetic  1.93 us (2%)
  between operations  1.18 us (1%)
    pallas_call x10, Pallas kernels, call(): pl.pallas_call(kernel, out_shape=tuple(outs), in_specs=specs or [VMEM] *...  30.4 us
    ppermute x8, waiting for transfers between devices, swap(): lax.ppermute(jnp.concatenate([send, halves[0][None], halves[1][None], pad...  14.9 us
    ppermute x8, starting transfers between devices, swap(): lax.ppermute(jnp.concatenate([send, halves[0][None], halves[1][None], pad...  12.2 us
    ppermute x6, starting transfers between devices, spread(): return [part] + [lax.ppermute(part, 'tm', perm) for perm in perms]  7.11 us
    ppermute x2, starting transfers between devices, swap(): return (lax.ppermute(send, 'tm', perm), None)  6.29 us
    ppermute x1, starting transfers between devices, halo_rows(): two = lax.ppermute(jnp.where(odd, tail, head), 'tm', outer)  5.44 us
    ppermute x6, waiting for transfers between devices, spread(): return [part] + [lax.ppermute(part, 'tm', perm) for perm in perms]  3.72 us
    ppermute x2, waiting for transfers between devices, spread(): got = lax.ppermute(jnp.concatenate([part, far]), 'tm', perms[0])  2.51 us
  transfers between devices with their start and end apart: 30, of which 17 were waited for; matrix products, arithmetic and copies ran while one was open for 1% of the time, Pallas kernels for 8%

profile of v4, /device:TPU:0, one launch (start us, length us, event | category | flops | bytes accessed | tf_op | source)
XLA Modules:
  0.0 99.8 jit_solution(8147792617592987813)
XLA Ops:
  1.4 5.4 %collective-permute-start.1 = (bf16[2,128]{1,0:T(2,128)(2,1)S(1)}, bf16[2,128]{1,0:T(2,128)(2,1)S(1)}, u32[]{:S(2)}, u32[]{:S(2)}) collective-permute-start(bf16[2,128]{1,0:T(2,128)(2,1)S(1)} %get-tuple-element.50), channel_id=1, source_target_pairs={{0,15},{1,2},{2,1},{3,4},{4,3},{5,6},{6,5},{7,8},{8,7},{9,10},{10,... | collective-permute-start | bytes 1544 | tf_op jit(solution)/shard_map/ppermute | solution.py:265
  8.1 13.4 %shard_map.59 = (bf16[1152,1024]{1,0:T(8,128)(2,1)S(1)}, bf16[512,1024]{1,0:T(8,128)(2,1)S(1)}, bf16[1152,512]{1,0:T(8,128)(2,1)S(1)}) custom-call(s32[8]{0:T(128)S(1)} %stack.35.at_ref, f32[4,128]{1,0:T(4,128)S(1)} %maximum_convert_fusion.halo_ref, bf16[4096,128]{1,0:T(8,128)(2,1)} %bitcast.19, bf16[2304,1024]{1,0:T(8,128)(2,1)} %k_hbm.1, ...), custom_call_target="tpu_custom_call" | custom-call | flops 7247757312 | bytes 12584992 | tf_op jit(solution)/shard_map/pallas_call | solution.py:183
  21.6 2.4 %shard_map.61 = bf16[592,512]{1,0:T(8,128)(2,1)S(1)} custom-call(bf16[1152,1024]{1,0:T(8,128)(2,1)S(1)} %get-tuple-element.16.p_ref, bf16[1152,512]{1,0:T(8,128)(2,1)S(1)} %get-tuple-element.17.w_ref, bf16[512,1024]{1,0:T(8,128)(2,1)S(1)} %get-tuple-element.18.h_ref), custom_call_target="tpu_custom_call" | custom-call | flops 1207959552 | bytes 5193728 | tf_op jit(solution)/shard_map/pallas_call | solution.py:183
  25.1 1.7 %shard_map.62 = (f32[432,512]{1,0:T(8,128)S(1)}, f32[8,512]{1,0:T(8,128)S(1)}) custom-call(bf16[1152,1024]{1,0:T(8,128)(2,1)S(1)} %get-tuple-element.16.p_ref, bf16[1152,512]{1,0:T(8,128)(2,1)S(1)} %get-tuple-element.17.w_ref, bf16[512,1024]{1,0:T(8,128)(2,1)S(1)} %get-tuple-element.18.h_ref), custom_call_target="tpu_custom_call" | custom-call | flops 905969664 | bytes 5488640 | tf_op jit(solution)/shard_map/pallas_call | solution.py:183
  28.8 1.9 %collective-permute-start.4 = (bf16[96,512]{1,0:T(8,128)(2,1)S(1)}, bf16[96,512]{1,0:T(8,128)(2,1)S(1)}, u32[]{:S(2)}, u32[]{:S(2)}) collective-permute-start(bf16[96,512]{1,0:T(8,128)(2,1)S(1)} %get-tuple-element.67), channel_id=1, source_target_pairs={{0,4},{1,5},{2,6},{3,7},{4,0},{5,1},{6,2},{7,3},{8,12},{9,13},{10,... | collective-permute-start | bytes 294920 | tf_op jit(solution)/shard_map/ppermute | solution.py:299
  30.9 4.0 %collective-permute-done.3 = bf16[96,512]{1,0:T(8,128)(2,1)S(1)} collective-permute-done((bf16[96,512]{1,0:T(8,128)(2,1)S(1)}, bf16[96,512]{1,0:T(8,128)(2,1)S(1)}, u32[]{:S(2)}, u32[]{:S(2)}) %collective-permute-start.3) | collective-permute-done | bytes 98336 | tf_op jit(solution)/shard_map/ppermute | solution.py:299
  35.8 2.3 %collective-permute-start.6 = (bf16[96,512]{1,0:T(8,128)(2,1)S(1)}, bf16[96,512]{1,0:T(8,128)(2,1)S(1)}, u32[]{:S(2)}, u32[]{:S(2)}) collective-permute-start(bf16[96,512]{1,0:T(8,128)(2,1)S(1)} %maximum_maximum_fusion), channel_id=1, source_target_pairs={{0,8},{1,9},{2,10},{3,11},{4,12},{5,13},{6,14},{7,15},{8,0},{9,1},... | collective-permute-start | bytes 294920 | tf_op jit(solution)/shard_map/ppermute | solution.py:299
  38.1 1.7 %collective-permute-start.8 = (bf16[64,512]{1,0:T(8,128)(2,1)S(1)}, bf16[64,512]{1,0:T(8,128)(2,1)S(1)}, u32[]{:S(2)}, u32[]{:S(2)}) collective-permute-start(bf16[64,512]{1,0:T(8,128)(2,1)S(1)} %fusion.9), channel_id=1, source_target_pairs={{0,4},{1,5},{2,6},{3,7},{4,0},{5,1},{6,2},{7,3},{8,12},{9,13},{10,... | collective-permute-start | bytes 196616 | tf_op jit(solution)/shard_map/ppermute | solution.py:318
  39.8 3.3 %collective-permute-done.6 = bf16[96,512]{1,0:T(8,128)(2,1)S(1)} collective-permute-done((bf16[96,512]{1,0:T(8,128)(2,1)S(1)}, bf16[96,512]{1,0:T(8,128)(2,1)S(1)}, u32[]{:S(2)}, u32[]{:S(2)}) %collective-permute-start.6) | collective-permute-done | bytes 98336 | tf_op jit(solution)/shard_map/ppermute | solution.py:299
  43.3 3.5 %collective-permute-start.9 = (bf16[64,512]{1,0:T(8,128)(2,1)S(1)}, bf16[64,512]{1,0:T(8,128)(2,1)S(1)}, u32[]{:S(2)}, u32[]{:S(2)}) collective-permute-start(bf16[64,512]{1,0:T(8,128)(2,1)S(1)} %fusion.11), channel_id=1, source_target_pairs={{0,8},{1,9},{2,10},{3,11},{4,12},{5,13},{6,14},{7,15},{8,0},{9,1},... | collective-permute-start | bytes 196616 | tf_op jit(solution)/shard_map/ppermute | solution.py:296
  49.1 1.9 %collective-permute-start.14 = (bf16[64,512]{1,0:T(8,128)(2,1)S(1)}, bf16[64,512]{1,0:T(8,128)(2,1)S(1)}, u32[]{:S(2)}, u32[]{:S(2)}) collective-permute-start(bf16[64,512]{1,0:T(8,128)(2,1)S(1)} %get-tuple-element.41), channel_id=1, source_target_pairs={{0,6},{1,7},{2,4},{3,5},{4,2},{5,3},{6,0},{7,1},{8,14},{9,15},{10,... | collective-permute-start | bytes 196616 | tf_op jit(solution)/shard_map/ppermute | solution.py:332
  52.7 2.0 %collective-permute-done.11 = bf16[160,512]{1,0:T(8,128)(2,1)S(1)} collective-permute-done((bf16[160,512]{1,0:T(8,128)(2,1)S(1)}, bf16[160,512]{1,0:T(8,128)(2,1)S(1)}, u32[]{:S(2)}, u32[]{:S(2)}) %collective-permute-start.11) | collective-permute-done | bytes 163872 | tf_op jit(solution)/shard_map/ppermute | solution.py:335
  56.3 2.0 %shard_map.63 = (f32[512,1024]{1,0:T(8,128)S(1)}, f32[512,128]{1,0:T(8,128)S(1)}) custom-call(bf16[1152,1024]{1,0:T(8,128)(2,1)S(1)} %get-tuple-element.16.p_ref, bf16[576,512]{1,0:T(8,128)(2,1)S(1)} %constant_dynamic-update-slice_fusion.w_ref, bf16[512,1024]{1,0:T(8,128)(2,1)S(1)} %get-tuple-element.18.h_ref), custom_call_target="tpu_custom_call" | custom-call | flops 1207959552 | bytes 6356992 | tf_op jit(solution)/shard_map/pallas_call | solution.py:183
  58.3 2.4 %shard_map.64.h_ref = bf16[512,1024]{1,0:T(8,128)(2,1)S(1)} custom-call(bf16[1152,1024]{1,0:T(8,128)(2,1)S(1)} %get-tuple-element.16.p_ref, bf16[576,512]{1,0:T(8,128)(2,1)S(1)} %collective-permute-done.15.w_ref, bf16[512,1024]{1,0:T(8,128)(2,1)S(1)} %get-tuple-element.18.h_ref, f32[512,1024]{1,0:T(8,128)S(1)} %get-tuple-element.23.refs_0_, ...), custom_call_target="tpu_custom_call" | custom-call | flops 1207959552 | bytes 7405568 | tf_op jit(solution)/shard_map/pallas_call | solution.py:183
  60.7 2.4 %shard_map.66 = bf16[592,512]{1,0:T(8,128)(2,1)S(1)} custom-call(bf16[1152,1024]{1,0:T(8,128)(2,1)S(1)} %get-tuple-element.16.p_ref, bf16[576,512]{1,0:T(8,128)(2,1)S(1)} %collective-permute-done.15.w_ref, bf16[512,1024]{1,0:T(8,128)(2,1)S(1)} %shard_map.64.h_ref), custom_call_target="tpu_custom_call" | custom-call | flops 1207959552 | bytes 4603904 | tf_op jit(solution)/shard_map/pallas_call | solution.py:183
  63.7 1.8 %shard_map.65 = (f32[144,512]{1,0:T(8,128)S(1)}, bf16[144,512]{1,0:T(8,128)(2,1)S(1)}, bf16[512,1024]{1,0:T(8,128)(2,1)}) custom-call(bf16[1152,1024]{1,0:T(8,128)(2,1)S(1)} %get-tuple-element.16.p_ref, bf16[576,512]{1,0:T(8,128)(2,1)S(1)} %constant_dynamic-update-slice_fusion.w_ref, bf16[512,1024]{1,0:T(8,128)(2,1)S(1)} %shard_map.64.h_ref), custom_call_target="tpu_custom_call" | custom-call | flops 301989888 | bytes 5488640 | tf_op jit(solution)/shard_map/pallas_call | solution.py:183
  65.5 1.7 %shard_map.67 = (f32[432,512]{1,0:T(8,128)S(1)}, f32[8,512]{1,0:T(8,128)S(1)}) custom-call(bf16[1152,1024]{1,0:T(8,128)(2,1)S(1)} %get-tuple-element.16.p_ref, bf16[576,512]{1,0:T(8,128)(2,1)S(1)} %constant_dynamic-update-slice_fusion.w_ref, bf16[512,1024]{1,0:T(8,128)(2,1)S(1)} %shard_map.64.h_ref), custom_call_target="tpu_custom_call" | custom-call | flops 905969664 | bytes 4898816 | tf_op jit(solution)/shard_map/pallas_call | solution.py:183
  68.4 1.9 %collective-permute-start.19 = (bf16[96,512]{1,0:T(8,128)(2,1)S(1)}, bf16[96,512]{1,0:T(8,128)(2,1)S(1)}, u32[]{:S(2)}, u32[]{:S(2)}) collective-permute-start(bf16[96,512]{1,0:T(8,128)(2,1)S(1)} %get-tuple-element.63), channel_id=1, source_target_pairs={{0,6},{1,7},{2,4},{3,5},{4,2},{5,3},{6,0},{7,1},{8,14},{9,15},{10,... | collective-permute-start | bytes 294920 | tf_op jit(solution)/shard_map/ppermute | solution.py:299
  72.1 2.6 %collective-permute-done.17 = bf16[96,512]{1,0:T(8,128)(2,1)S(1)} collective-permute-done((bf16[96,512]{1,0:T(8,128)(2,1)S(1)}, bf16[96,512]{1,0:T(8,128)(2,1)S(1)}, u32[]{:S(2)}, u32[]{:S(2)}) %collective-permute-start.17) | collective-permute-done | bytes 98336 | tf_op jit(solution)/shard_map/ppermute | solution.py:299
  75.9 2.8 %collective-permute-start.20 = (bf16[96,512]{1,0:T(8,128)(2,1)S(1)}, bf16[96,512]{1,0:T(8,128)(2,1)S(1)}, u32[]{:S(2)}, u32[]{:S(2)}) collective-permute-start(bf16[96,512]{1,0:T(8,128)(2,1)S(1)} %maximum_maximum_fusion.1), channel_id=1, source_target_pairs={{0,8},{1,9},{2,10},{3,11},{4,12},{5,13},{6,14},{7,15},{8,0},{9,1},... | collective-permute-start | bytes 294920 | tf_op jit(solution)/shard_map/ppermute | solution.py:299
  79.1 3.2 %collective-permute-done.20 = bf16[96,512]{1,0:T(8,128)(2,1)S(1)} collective-permute-done((bf16[96,512]{1,0:T(8,128)(2,1)S(1)}, bf16[96,512]{1,0:T(8,128)(2,1)S(1)}, u32[]{:S(2)}, u32[]{:S(2)}) %collective-permute-start.20) | collective-permute-done | bytes 98336 | tf_op jit(solution)/shard_map/ppermute | solution.py:299
  83.5 2.8 %collective-permute-start.23 = (bf16[64,512]{1,0:T(8,128)(2,1)S(1)}, bf16[64,512]{1,0:T(8,128)(2,1)S(1)}, u32[]{:S(2)}, u32[]{:S(2)}) collective-permute-start(bf16[64,512]{1,0:T(8,128)(2,1)S(1)} %fusion.8), channel_id=1, source_target_pairs={{0,8},{1,9},{2,10},{3,11},{4,12},{5,13},{6,14},{7,15},{8,0},{9,1},... | collective-permute-start | bytes 196616 | tf_op jit(solution)/shard_map/ppermute | solution.py:296
  93.6 2.2 %collective-permute-done.26 = bf16[64,512]{1,0:T(8,128)(2,1)S(1)} collective-permute-done((bf16[64,512]{1,0:T(8,128)(2,1)S(1)}, bf16[64,512]{1,0:T(8,128)(2,1)S(1)}, u32[]{:S(2)}, u32[]{:S(2)}) %collective-permute-start.26) | collective-permute-done | bytes 65568 | tf_op jit(solution)/shard_map/ppermute | solution.py:332
  96.0 2.0 %collective-permute-done.29.other_ref = bf16[576,512]{1,0:T(8,128)(2,1)S(1)} collective-permute-done((bf16[576,512]{1,0:T(8,128)(2,1)S(1)}, bf16[576,512]{1,0:T(8,128)(2,1)S(1)}, u32[]{:S(2)}, u32[]{:S(2)}) %collective-permute-start.29) | collective-permute-done | bytes 589856 | tf_op jit(solution)/shard_map/ppermute | solution.py:373
  (100 shorter events, 27.3 us)
Async XLA Ops:
  1.4 6.7 %collective-permute-start.1 = (bf16[2,128]{1,0:T(2,128)(2,1)S(1)}, bf16[2,128]{1,0:T(2,128)(2,1)S(1)}, u32[]{:S(2)}, u32[]{:S(2)}) collective-permute-start(bf16[2,128]{1,0:T(2,128)(2,1)S(1)} %get-tuple-element.50), channel_id=1, source_target_pairs={{0,15},{1,2},{2,1},{3,4},{4,3},{5,6},{6,5},{7,8},{8,7},{9,10},{10,... | collective-permute-start | bytes 1544 | tf_op jit(solution)/shard_map/ppermute | solution.py:265
  27.1 7.8 %collective-permute-start.3 = (bf16[96,512]{1,0:T(8,128)(2,1)S(1)}, bf16[96,512]{1,0:T(8,128)(2,1)S(1)}, u32[]{:S(2)}, u32[]{:S(2)}) collective-permute-start(bf16[96,512]{1,0:T(8,128)(2,1)S(1)} %get-tuple-element.65), channel_id=1, source_target_pairs={{0,2},{1,3},{2,0},{3,1},{4,6},{5,7},{6,4},{7,5},{8,10},{9,11},{10,... | collective-permute-start | bytes 294920 | tf_op jit(solution)/shard_map/ppermute | solution.py:299
  27.2 7.7 %collective-permute-start.5 = (bf16[96,512]{1,0:T(8,128)(2,1)S(1)}, bf16[96,512]{1,0:T(8,128)(2,1)S(1)}, u32[]{:S(2)}, u32[]{:S(2)}) collective-permute-start(bf16[96,512]{1,0:T(8,128)(2,1)S(1)} %get-tuple-element.66), channel_id=1, source_target_pairs={{0,6},{1,7},{2,4},{3,5},{4,2},{5,3},{6,0},{7,1},{8,14},{9,15},{10,... | collective-permute-start | bytes 294920 | tf_op jit(solution)/shard_map/ppermute | solution.py:299
  28.8 6.9 %collective-permute-start.4 = (bf16[96,512]{1,0:T(8,128)(2,1)S(1)}, bf16[96,512]{1,0:T(8,128)(2,1)S(1)}, u32[]{:S(2)}, u32[]{:S(2)}) collective-permute-start(bf16[96,512]{1,0:T(8,128)(2,1)S(1)} %get-tuple-element.67), channel_id=1, source_target_pairs={{0,4},{1,5},{2,6},{3,7},{4,0},{5,1},{6,2},{7,3},{8,12},{9,13},{10,... | collective-permute-start | bytes 294920 | tf_op jit(solution)/shard_map/ppermute | solution.py:299
  30.7 7.4 %collective-permute-start.7 = (bf16[128,512]{1,0:T(8,128)(2,1)S(1)}, bf16[128,512]{1,0:T(8,128)(2,1)S(1)}, u32[]{:S(2)}, u32[]{:S(2)}) collective-permute-start(bf16[128,512]{1,0:T(8,128)(2,1)S(1)} %pad_maximum_fusion.14), channel_id=1, source_target_pairs={{0,2},{1,3},{2,0},{3,1},{4,6},{5,7},{6,4},{7,5},{8,10},{9,11},{10,... | collective-permute-start | bytes 393224 | tf_op jit(solution)/shard_map/ppermute | solution.py:315
  35.8 7.2 %collective-permute-start.6 = (bf16[96,512]{1,0:T(8,128)(2,1)S(1)}, bf16[96,512]{1,0:T(8,128)(2,1)S(1)}, u32[]{:S(2)}, u32[]{:S(2)}) collective-permute-start(bf16[96,512]{1,0:T(8,128)(2,1)S(1)} %maximum_maximum_fusion), channel_id=1, source_target_pairs={{0,8},{1,9},{2,10},{3,11},{4,12},{5,13},{6,14},{7,15},{8,0},{9,1},... | collective-permute-start | bytes 294920 | tf_op jit(solution)/shard_map/ppermute | solution.py:299
  38.1 5.2 %collective-permute-start.8 = (bf16[64,512]{1,0:T(8,128)(2,1)S(1)}, bf16[64,512]{1,0:T(8,128)(2,1)S(1)}, u32[]{:S(2)}, u32[]{:S(2)}) collective-permute-start(bf16[64,512]{1,0:T(8,128)(2,1)S(1)} %fusion.9), channel_id=1, source_target_pairs={{0,4},{1,5},{2,6},{3,7},{4,0},{5,1},{6,2},{7,3},{8,12},{9,13},{10,... | collective-permute-start | bytes 196616 | tf_op jit(solution)/shard_map/ppermute | solution.py:318
  43.1 5.1 %collective-permute-start.10 = (bf16[80,512]{1,0:T(8,128)(2,1)S(1)}, bf16[80,512]{1,0:T(8,128)(2,1)S(1)}, u32[]{:S(2)}, u32[]{:S(2)}) collective-permute-start(bf16[80,512]{1,0:T(8,128)(2,1)S(1)} %get-tuple-element.43), channel_id=1, source_target_pairs={{0,4},{1,5},{2,6},{3,7},{4,0},{5,1},{6,2},{7,3},{8,12},{9,13},{10,... | collective-permute-start | bytes 245768 | tf_op jit(solution)/shard_map/ppermute | solution.py:334
  43.3 5.8 %collective-permute-start.9 = (bf16[64,512]{1,0:T(8,128)(2,1)S(1)}, bf16[64,512]{1,0:T(8,128)(2,1)S(1)}, u32[]{:S(2)}, u32[]{:S(2)}) collective-permute-start(bf16[64,512]{1,0:T(8,128)(2,1)S(1)} %fusion.11), channel_id=1, source_target_pairs={{0,8},{1,9},{2,10},{3,11},{4,12},{5,13},{6,14},{7,15},{8,0},{9,1},... | collective-permute-start | bytes 196616 | tf_op jit(solution)/shard_map/ppermute | solution.py:296
  48.2 6.4 %collective-permute-start.11 = (bf16[160,512]{1,0:T(8,128)(2,1)S(1)}, bf16[160,512]{1,0:T(8,128)(2,1)S(1)}, u32[]{:S(2)}, u32[]{:S(2)}) collective-permute-start(bf16[160,512]{1,0:T(8,128)(2,1)S(1)} %pad_maximum_fusion.12), channel_id=1, source_target_pairs={{0,2},{1,3},{2,0},{3,1},{4,6},{5,7},{6,4},{7,5},{8,10},{9,11},{10,... | collective-permute-start | bytes 491528 | tf_op jit(solution)/shard_map/ppermute | solution.py:335
  49.1 7.1 %collective-permute-start.14 = (bf16[64,512]{1,0:T(8,128)(2,1)S(1)}, bf16[64,512]{1,0:T(8,128)(2,1)S(1)}, u32[]{:S(2)}, u32[]{:S(2)}) collective-permute-start(bf16[64,512]{1,0:T(8,128)(2,1)S(1)} %get-tuple-element.41), channel_id=1, source_target_pairs={{0,6},{1,7},{2,4},{3,5},{4,2},{5,3},{6,0},{7,1},{8,14},{9,15},{10,... | collective-permute-start | bytes 196616 | tf_op jit(solution)/shard_map/ppermute | solution.py:332
  51.1 5.1 %collective-permute-start.13 = (bf16[64,512]{1,0:T(8,128)(2,1)S(1)}, bf16[64,512]{1,0:T(8,128)(2,1)S(1)}, u32[]{:S(2)}, u32[]{:S(2)}) collective-permute-start(bf16[64,512]{1,0:T(8,128)(2,1)S(1)} %get-tuple-element.41), channel_id=1, source_target_pairs={{0,4},{1,5},{2,6},{3,7},{4,0},{5,1},{6,2},{7,3},{8,12},{9,13},{10,... | collective-permute-start | bytes 196616 | tf_op jit(solution)/shard_map/ppermute | solution.py:332
  51.9 4.3 %collective-permute-start.12 = (bf16[64,512]{1,0:T(8,128)(2,1)S(1)}, bf16[64,512]{1,0:T(8,128)(2,1)S(1)}, u32[]{:S(2)}, u32[]{:S(2)}) collective-permute-start(bf16[64,512]{1,0:T(8,128)(2,1)S(1)} %get-tuple-element.41), channel_id=1, source_target_pairs={{0,2},{1,3},{2,0},{3,1},{4,6},{5,7},{6,4},{7,5},{8,10},{9,11},{10,... | collective-permute-start | bytes 196616 | tf_op jit(solution)/shard_map/ppermute | solution.py:332
  67.6 7.1 %collective-permute-start.17 = (bf16[96,512]{1,0:T(8,128)(2,1)S(1)}, bf16[96,512]{1,0:T(8,128)(2,1)S(1)}, u32[]{:S(2)}, u32[]{:S(2)}) collective-permute-start(bf16[96,512]{1,0:T(8,128)(2,1)S(1)} %get-tuple-element.62), channel_id=1, source_target_pairs={{0,2},{1,3},{2,0},{3,1},{4,6},{5,7},{6,4},{7,5},{8,10},{9,11},{10,... | collective-permute-start | bytes 294920 | tf_op jit(solution)/shard_map/ppermute | solution.py:299
  68.4 6.5 %collective-permute-start.19 = (bf16[96,512]{1,0:T(8,128)(2,1)S(1)}, bf16[96,512]{1,0:T(8,128)(2,1)S(1)}, u32[]{:S(2)}, u32[]{:S(2)}) collective-permute-start(bf16[96,512]{1,0:T(8,128)(2,1)S(1)} %get-tuple-element.63), channel_id=1, source_target_pairs={{0,6},{1,7},{2,4},{3,5},{4,2},{5,3},{6,0},{7,1},{8,14},{9,15},{10,... | collective-permute-start | bytes 294920 | tf_op jit(solution)/shard_map/ppermute | solution.py:299
  70.3 5.4 %collective-permute-start.18 = (bf16[96,512]{1,0:T(8,128)(2,1)S(1)}, bf16[96,512]{1,0:T(8,128)(2,1)S(1)}, u32[]{:S(2)}, u32[]{:S(2)}) collective-permute-start(bf16[96,512]{1,0:T(8,128)(2,1)S(1)} %get-tuple-element.64), channel_id=1, source_target_pairs={{0,4},{1,5},{2,6},{3,7},{4,0},{5,1},{6,2},{7,3},{8,12},{9,13},{10,... | collective-permute-start | bytes 294920 | tf_op jit(solution)/shard_map/ppermute | solution.py:299
  71.1 7.5 %collective-permute-start.21 = (bf16[128,512]{1,0:T(8,128)(2,1)S(1)}, bf16[128,512]{1,0:T(8,128)(2,1)S(1)}, u32[]{:S(2)}, u32[]{:S(2)}) collective-permute-start(bf16[128,512]{1,0:T(8,128)(2,1)S(1)} %pad_maximum_fusion.15), channel_id=1, source_target_pairs={{0,2},{1,3},{2,0},{3,1},{4,6},{5,7},{6,4},{7,5},{8,10},{9,11},{10,... | collective-permute-start | bytes 393224 | tf_op jit(solution)/shard_map/ppermute | solution.py:315
  75.9 6.5 %collective-permute-start.20 = (bf16[96,512]{1,0:T(8,128)(2,1)S(1)}, bf16[96,512]{1,0:T(8,128)(2,1)S(1)}, u32[]{:S(2)}, u32[]{:S(2)}) collective-permute-start(bf16[96,512]{1,0:T(8,128)(2,1)S(1)} %maximum_maximum_fusion.1), channel_id=1, source_target_pairs={{0,8},{1,9},{2,10},{3,11},{4,12},{5,13},{6,14},{7,15},{8,0},{9,1},... | collective-permute-start | bytes 294920 | tf_op jit(solution)/shard_map/ppermute | solution.py:299
  78.7 4.8 %collective-permute-start.22 = (bf16[64,512]{1,0:T(8,128)(2,1)S(1)}, bf16[64,512]{1,0:T(8,128)(2,1)S(1)}, u32[]{:S(2)}, u32[]{:S(2)}) collective-permute-start(bf16[64,512]{1,0:T(8,128)(2,1)S(1)} %fusion.6), channel_id=1, source_target_pairs={{0,4},{1,5},{2,6},{3,7},{4,0},{5,1},{6,2},{7,3},{8,12},{9,13},{10,... | collective-permute-start | bytes 196616 | tf_op jit(solution)/shard_map/ppermute | solution.py:318
  82.4 5.0 %collective-permute-start.24 = (bf16[80,512]{1,0:T(8,128)(2,1)S(1)}, bf16[80,512]{1,0:T(8,128)(2,1)S(1)}, u32[]{:S(2)}, u32[]{:S(2)}) collective-permute-start(bf16[80,512]{1,0:T(8,128)(2,1)S(1)} %get-tuple-element.33), channel_id=1, source_target_pairs={{0,4},{1,5},{2,6},{3,7},{4,0},{5,1},{6,2},{7,3},{8,12},{9,13},{10,... | collective-permute-start | bytes 245768 | tf_op jit(solution)/shard_map/ppermute | solution.py:334
  83.5 5.9 %collective-permute-start.23 = (bf16[64,512]{1,0:T(8,128)(2,1)S(1)}, bf16[64,512]{1,0:T(8,128)(2,1)S(1)}, u32[]{:S(2)}, u32[]{:S(2)}) collective-permute-start(bf16[64,512]{1,0:T(8,128)(2,1)S(1)} %fusion.8), channel_id=1, source_target_pairs={{0,8},{1,9},{2,10},{3,11},{4,12},{5,13},{6,14},{7,15},{8,0},{9,1},... | collective-permute-start | bytes 196616 | tf_op jit(solution)/shard_map/ppermute | solution.py:296
  87.4 6.2 %collective-permute-start.25 = (bf16[160,512]{1,0:T(8,128)(2,1)S(1)}, bf16[160,512]{1,0:T(8,128)(2,1)S(1)}, u32[]{:S(2)}, u32[]{:S(2)}) collective-permute-start(bf16[160,512]{1,0:T(8,128)(2,1)S(1)} %pad_maximum_fusion.13), channel_id=1, source_target_pairs={{0,2},{1,3},{2,0},{3,1},{4,6},{5,7},{6,4},{7,5},{8,10},{9,11},{10,... | collective-permute-start | bytes 491528 | tf_op jit(solution)/shard_map/ppermute | solution.py:335
  89.5 6.4 %collective-permute-start.28 = (bf16[64,512]{1,0:T(8,128)(2,1)S(1)}, bf16[64,512]{1,0:T(8,128)(2,1)S(1)}, u32[]{:S(2)}, u32[]{:S(2)}) collective-permute-start(bf16[64,512]{1,0:T(8,128)(2,1)S(1)} %get-tuple-element.31), channel_id=1, source_target_pairs={{0,6},{1,7},{2,4},{3,5},{4,2},{5,3},{6,0},{7,1},{8,14},{9,15},{10,... | collective-permute-start | bytes 196616 | tf_op jit(solution)/shard_map/ppermute | solution.py:332
  91.0 4.8 %collective-permute-start.27 = (bf16[64,512]{1,0:T(8,128)(2,1)S(1)}, bf16[64,512]{1,0:T(8,128)(2,1)S(1)}, u32[]{:S(2)}, u32[]{:S(2)}) collective-permute-start(bf16[64,512]{1,0:T(8,128)(2,1)S(1)} %get-tuple-element.31), channel_id=1, source_target_pairs={{0,4},{1,5},{2,6},{3,7},{4,0},{5,1},{6,2},{7,3},{8,12},{9,13},{10,... | collective-permute-start | bytes 196616 | tf_op jit(solution)/shard_map/ppermute | solution.py:332
  (6 other events, 16.6 us)

commit v5 on v4

--- a/solution.py
+++ b/solution.py
@@ -11,6 +11,7 @@
 ITERS = 2
 HALF = 256
 TILE = 256
+SPAN = 1024
 LANES = 128
 bf16 = jnp.bfloat16
 f32 = jnp.float32
@@ -77,11 +78,11 @@
             k_copies[2 * waited].wait()
             k_copies[2 * waited + 1].wait()
             waited += 1
-        for t in range(0, frames, TILE):
-            f = frame[t : t + TILE, :]
+        for t in range(0, frames, 512):
+            f = frame[t : t + 512, :]
             re = dot_nt(k_ref[lo:hi, :], f)
             im = dot_nt(k_ref[bins + lo : bins + hi, :], f)
-            p_ref[lo:hi, t : t + TILE] = (re * re + im * im).astype(bf16)
+            p_ref[lo:hi, t : t + 512] = (re * re + im * im).astype(bf16)
 
     for copy in w_copies + [h_copy]:
         copy.wait()
@@ -106,10 +107,10 @@
     for lo, hi in row_blocks(size):
         w = w_ref[w_base + lo : w_base + hi, :]
         acc = None
-        for t in range(0, frames, TILE):
-            h = h_ref[:, t : t + TILE]
+        for t in range(0, frames, SPAN):
+            h = h_ref[:, t : t + SPAN]
             model = dot(w, h)
-            p = p_ref[p_base + lo : p_base + hi, t : t + TILE]
+            p = p_ref[p_base + lo : p_base + hi, t : t + SPAN]
             ratio = (p.astype(f32) * inverse(model)).astype(bf16)
             part = dot_nt(ratio, h)
             acc = part if acc is None else acc + part
@@ -126,8 +127,6 @@
             outs.pop(0)[...] = (high + low)[:8]
     if "templates" in extras:
         outs.pop(0)[...] = w_ref[w_base : w_base + size, :]
-    if "copy" in extras:
-        outs.pop(0)[...] = h_ref[...]
 
 
 def activation_kernel(first, base, p_ref, w_ref, h_ref, *refs):
@@ -158,26 +157,36 @@
             new_ref[:, tile] = (h.astype(f32) * numer * inv).astype(bf16)
 
 
-def place_kernel(rows, at_ref, own_ref, other_ref, out_ref, sems):
-    blocks = own_ref.shape[0] // rows
-    copies = []
-    for n in range(2 * blocks):
-        ref, m = (own_ref, n) if n < blocks else (other_ref, n - blocks)
+def place_kernel(rows, at_ref, own_ref, acts_ref, out_ref, acts_out_ref, sems):
+    copies = [pltpu.make_async_copy(acts_ref, acts_out_ref, sems.at[at_ref.shape[0]])]
+    copies[0].start()
+    for n in range(at_ref.shape[0]):
         start = pl.multiple_of(at_ref[n] * rows, 16)
-        source = ref.at[pl.ds(m * rows, rows)]
+        source = own_ref.at[pl.ds(n * rows, rows)]
         copies.append(pltpu.make_async_copy(source, out_ref.at[pl.ds(start, rows)], sems.at[n]))
         copies[-1].start()
     for copy in copies:
         copy.wait()
 
 
+def place_other_kernel(rows, at_ref, other_ref, half_ref, out_ref, sems):
+    copies = []
+    for n in range(at_ref.shape[0]):
+        start = pl.multiple_of(at_ref[n] * rows, 16)
+        source = other_ref.at[pl.ds(n * rows, rows)]
+        copies.append(pltpu.make_async_copy(source, out_ref.at[pl.ds(start, rows)], sems.at[n]))
+        copies[-1].start()
+    for copy in copies:
+        copy.wait()
+
+
 VMEM = pl.BlockSpec(memory_space=pltpu.VMEM)
 HBM = pl.BlockSpec(memory_space=pltpu.HBM)
 SMEM = pl.BlockSpec(memory_space=pltpu.SMEM)
 ANY = pl.BlockSpec(memory_space=pl.ANY)
 
 
-def call(kernel, outs, scratch, flops, *args, specs=None, out_spec=None, mib=16):
+def call(kernel, outs, scratch, flops, *args, specs=None, out_spec=None, aliases={}, mib=16):
     size = sum(a.size * a.dtype.itemsize for a in args)
     size += sum(o.size * o.dtype.itemsize for o in outs)
     return pl.pallas_call(
@@ -186,6 +195,7 @@
         in_specs=specs or [VMEM] * len(args),
         out_specs=tuple([out_spec or VMEM] * len(outs)),
         scratch_shapes=scratch,
+        input_output_aliases=aliases,
         cost_estimate=pl.CostEstimate(flops=flops, bytes_accessed=size, transcendentals=0),
         compiler_params=pltpu.CompilerParams(vmem_limit_bytes=mib * 1024 * 1024),
     )(*args)
@@ -228,8 +238,6 @@
         outs.append(shape((8, comps), f32))
     if "templates" in extras:
         outs.append(shape((size, comps), bf16))
-    if "copy" in extras:
-        outs.append(shape(acts.shape, bf16))
     kernel = functools.partial(template_kernel, size, p_base, w_base, extras)
     return call(kernel, outs, [], 4 * size * acts.size, power, weights, acts)
 
@@ -355,8 +363,7 @@
         (send,) = template_numerator(size, power, size, other_w, base, acts, ("send",))
         got = lax.ppermute(send, "tm", core.others[0][1])
         rest, total = template_numerator(size - rows, power, rows, own_w, rows, acts, ("totals",))
-        extras = ("templates",) + (("copy",) if last else ())
-        mine, weights, *copied = template_numerator(rows, power, 0, own_w, 0, acts, extras)
+        mine, weights = template_numerator(rows, power, 0, own_w, 0, acts, ("templates",))
         rest = rest + got[rows:size].astype(f32)
         mine = mine + got[:rows].astype(f32)
         total = total[0] + (got[size].astype(f32) + got[size + 1].astype(f32))
@@ -374,12 +381,21 @@
         if not last:
             numer, colsum = activation_numerator(power, 0, own_w, acts)
             acts = new_activations(power, size, other_w, acts, numer, colsum)
-    kernel = functools.partial(place_kernel, rows)
-    out = call(
-        kernel, [shape(templates.shape, bf16)], [pltpu.SemaphoreType.DMA((at.shape[0],))], 0,
-        at, own_w, other_w, specs=[SMEM, ANY, ANY], out_spec=ANY,
+    out, acts = call(
+        functools.partial(place_kernel, rows),
+        [shape(templates.shape, bf16), shape(acts.shape, bf16)],
+        [pltpu.SemaphoreType.DMA((quad.size + 1,))],
+        2 * acts.size * acts.shape[0],
+        at[: quad.size], own_w, acts, specs=[SMEM, ANY, ANY], out_spec=ANY,
     )
-    return (copied[0], out[0])
+    (out,) = call(
+        functools.partial(place_other_kernel, rows),
+        [shape(templates.shape, bf16)],
+        [pltpu.SemaphoreType.DMA((quad.size,))],
+        0,
+        at[quad.size :], other_w, out, specs=[SMEM, ANY, ANY], out_spec=ANY, aliases={2: 0},
+    )
+    return (acts, out)
 
 
 def solution(mesh):

time: 100 us -> 96.3 us (0.963)
  Pallas kernels: 30.4 us -> 28.4 us
  waiting for transfers between devices: 28.5 us -> 26.6 us
    pallas_call x10 -> x11, Pallas kernels: 30.4 us -> 28.4 us  [call(): pl.pallas_call(kernel, out_shape=tuple(outs), in_specs=specs or [VMEM] *...]
    ppermute x2, waiting for transfers between devices: 2 us -> 0.09 us  [on_device(): other_w, base = (lax.ppermute(own_w, 'tm', core.others[0][1]), 0)]
where the time goes in v5:
time: 96.3 us; the launch traced here: 96.1 us
  starting transfers between devices  37.4 us (39%)
  Pallas kernels  28.4 us (29%)
  waiting for transfers between devices  26.6 us (28%)
  other arithmetic  2.08 us (2%)
  between operations  1.23 us (1%)
    pallas_call x11, Pallas kernels, call(): pl.pallas_call(kernel, out_shape=tuple(outs), in_specs=specs or [VMEM] *...  28.4 us
    ppermute x8, waiting for transfers between devices, swap(): lax.ppermute(jnp.concatenate([send, halves[0][None], halves[1][None], pad...  14.9 us
    ppermute x8, starting transfers between devices, swap(): lax.ppermute(jnp.concatenate([send, halves[0][None], halves[1][None], pad...  12.2 us
    ppermute x6, starting transfers between devices, spread(): return [part] + [lax.ppermute(part, 'tm', perm) for perm in perms]  7.11 us
    ppermute x2, starting transfers between devices, swap(): return (lax.ppermute(send, 'tm', perm), None)  6.14 us
    ppermute x1, starting transfers between devices, halo_rows(): two = lax.ppermute(jnp.where(odd, tail, head), 'tm', outer)  5.44 us
    ppermute x6, waiting for transfers between devices, spread(): return [part] + [lax.ppermute(part, 'tm', perm) for perm in perms]  3.65 us
    ppermute x2, waiting for transfers between devices, spread(): far = lax.ppermute(part, 'tm', perms[1])  2.53 us
  transfers between devices with their start and end apart: 30, of which 17 were waited for; matrix products, arithmetic and copies ran while one was open for 1% of the time, Pallas kernels for 8%

profile of v5, /device:TPU:0, one launch (start us, length us, event | category | flops | bytes accessed | tf_op | source)
XLA Modules:
  0.0 96.1 jit_solution(12690929476712938184)
XLA Ops:
  1.4 5.4 %collective-permute-start.1 = (bf16[2,128]{1,0:T(2,128)(2,1)S(1)}, bf16[2,128]{1,0:T(2,128)(2,1)S(1)}, u32[]{:S(2)}, u32[]{:S(2)}) collective-permute-start(bf16[2,128]{1,0:T(2,128)(2,1)S(1)} %get-tuple-element.52), channel_id=1, source_target_pairs={{0,15},{1,2},{2,1},{3,4},{4,3},{5,6},{6,5},{7,8},{8,7},{9,10},{10,... | collective-permute-start | bytes 1544 | tf_op jit(solution)/shard_map/ppermute | solution.py:273
  8.1 13.4 %shard_map.59 = (bf16[1152,1024]{1,0:T(8,128)(2,1)S(1)}, bf16[512,1024]{1,0:T(8,128)(2,1)S(1)}, bf16[1152,512]{1,0:T(8,128)(2,1)S(1)}) custom-call(s32[8]{0:T(128)S(1)} %stack.40.at_ref, f32[4,128]{1,0:T(4,128)S(1)} %maximum_convert_fusion.halo_ref, bf16[4096,128]{1,0:T(8,128)(2,1)} %bitcast.19, bf16[2304,1024]{1,0:T(8,128)(2,1)} %k_hbm.1, ...), custom_call_target="tpu_custom_call" | custom-call | flops 7247757312 | bytes 12584992 | tf_op jit(solution)/shard_map/pallas_call | solution.py:192
  21.6 1.7 %shard_map.61 = bf16[592,512]{1,0:T(8,128)(2,1)S(1)} custom-call(bf16[1152,1024]{1,0:T(8,128)(2,1)S(1)} %get-tuple-element.17.p_ref, bf16[1152,512]{1,0:T(8,128)(2,1)S(1)} %get-tuple-element.18.w_ref, bf16[512,1024]{1,0:T(8,128)(2,1)S(1)} %get-tuple-element.19.h_ref), custom_call_target="tpu_custom_call" | custom-call | flops 1207959552 | bytes 5193728 | tf_op jit(solution)/shard_map/pallas_call | solution.py:192
  26.0 1.6 %collective-permute-start.5 = (bf16[96,512]{1,0:T(8,128)(2,1)S(1)}, bf16[96,512]{1,0:T(8,128)(2,1)S(1)}, u32[]{:S(2)}, u32[]{:S(2)}) collective-permute-start(bf16[96,512]{1,0:T(8,128)(2,1)S(1)} %get-tuple-element.68), channel_id=1, source_target_pairs={{0,6},{1,7},{2,4},{3,5},{4,2},{5,3},{6,0},{7,1},{8,14},{9,15},{10,... | collective-permute-start | bytes 294920 | tf_op jit(solution)/shard_map/ppermute | solution.py:307
  27.6 1.9 %collective-permute-start.4 = (bf16[96,512]{1,0:T(8,128)(2,1)S(1)}, bf16[96,512]{1,0:T(8,128)(2,1)S(1)}, u32[]{:S(2)}, u32[]{:S(2)}) collective-permute-start(bf16[96,512]{1,0:T(8,128)(2,1)S(1)} %get-tuple-element.69), channel_id=1, source_target_pairs={{0,4},{1,5},{2,6},{3,7},{4,0},{5,1},{6,2},{7,3},{8,12},{9,13},{10,... | collective-permute-start | bytes 294920 | tf_op jit(solution)/shard_map/ppermute | solution.py:307
  29.7 4.0 %collective-permute-done.3 = bf16[96,512]{1,0:T(8,128)(2,1)S(1)} collective-permute-done((bf16[96,512]{1,0:T(8,128)(2,1)S(1)}, bf16[96,512]{1,0:T(8,128)(2,1)S(1)}, u32[]{:S(2)}, u32[]{:S(2)}) %collective-permute-start.3) | collective-permute-done | bytes 98336 | tf_op jit(solution)/shard_map/ppermute | solution.py:307
  34.6 2.2 %collective-permute-start.6 = (bf16[96,512]{1,0:T(8,128)(2,1)S(1)}, bf16[96,512]{1,0:T(8,128)(2,1)S(1)}, u32[]{:S(2)}, u32[]{:S(2)}) collective-permute-start(bf16[96,512]{1,0:T(8,128)(2,1)S(1)} %maximum_maximum_fusion), channel_id=1, source_target_pairs={{0,8},{1,9},{2,10},{3,11},{4,12},{5,13},{6,14},{7,15},{8,0},{9,1},... | collective-permute-start | bytes 294920 | tf_op jit(solution)/shard_map/ppermute | solution.py:307
  36.9 1.7 %collective-permute-start.8 = (bf16[64,512]{1,0:T(8,128)(2,1)S(1)}, bf16[64,512]{1,0:T(8,128)(2,1)S(1)}, u32[]{:S(2)}, u32[]{:S(2)}) collective-permute-start(bf16[64,512]{1,0:T(8,128)(2,1)S(1)} %fusion.9), channel_id=1, source_target_pairs={{0,4},{1,5},{2,6},{3,7},{4,0},{5,1},{6,2},{7,3},{8,12},{9,13},{10,... | collective-permute-start | bytes 196616 | tf_op jit(solution)/shard_map/ppermute | solution.py:326
  38.5 3.3 %collective-permute-done.6 = bf16[96,512]{1,0:T(8,128)(2,1)S(1)} collective-permute-done((bf16[96,512]{1,0:T(8,128)(2,1)S(1)}, bf16[96,512]{1,0:T(8,128)(2,1)S(1)}, u32[]{:S(2)}, u32[]{:S(2)}) %collective-permute-start.6) | collective-permute-done | bytes 98336 | tf_op jit(solution)/shard_map/ppermute | solution.py:307
  42.1 3.5 %collective-permute-start.9 = (bf16[64,512]{1,0:T(8,128)(2,1)S(1)}, bf16[64,512]{1,0:T(8,128)(2,1)S(1)}, u32[]{:S(2)}, u32[]{:S(2)}) collective-permute-start(bf16[64,512]{1,0:T(8,128)(2,1)S(1)} %fusion.11), channel_id=1, source_target_pairs={{0,8},{1,9},{2,10},{3,11},{4,12},{5,13},{6,14},{7,15},{8,0},{9,1},... | collective-permute-start | bytes 196616 | tf_op jit(solution)/shard_map/ppermute | solution.py:304
  47.9 2.0 %collective-permute-start.14 = (bf16[64,512]{1,0:T(8,128)(2,1)S(1)}, bf16[64,512]{1,0:T(8,128)(2,1)S(1)}, u32[]{:S(2)}, u32[]{:S(2)}) collective-permute-start(bf16[64,512]{1,0:T(8,128)(2,1)S(1)} %get-tuple-element.43), channel_id=1, source_target_pairs={{0,6},{1,7},{2,4},{3,5},{4,2},{5,3},{6,0},{7,1},{8,14},{9,15},{10,... | collective-permute-start | bytes 196616 | tf_op jit(solution)/shard_map/ppermute | solution.py:340
  51.4 2.0 %collective-permute-done.11 = bf16[160,512]{1,0:T(8,128)(2,1)S(1)} collective-permute-done((bf16[160,512]{1,0:T(8,128)(2,1)S(1)}, bf16[160,512]{1,0:T(8,128)(2,1)S(1)}, u32[]{:S(2)}, u32[]{:S(2)}) %collective-permute-start.11) | collective-permute-done | bytes 163872 | tf_op jit(solution)/shard_map/ppermute | solution.py:343
  53.4 1.5 %collective-permute-done.12 = bf16[64,512]{1,0:T(8,128)(2,1)S(1)} collective-permute-done((bf16[64,512]{1,0:T(8,128)(2,1)S(1)}, bf16[64,512]{1,0:T(8,128)(2,1)S(1)}, u32[]{:S(2)}, u32[]{:S(2)}) %collective-permute-start.12) | collective-permute-done | bytes 65568 | tf_op jit(solution)/shard_map/ppermute | solution.py:340
  55.0 2.0 %shard_map.63 = (f32[512,1024]{1,0:T(8,128)S(1)}, f32[512,128]{1,0:T(8,128)S(1)}) custom-call(bf16[1152,1024]{1,0:T(8,128)(2,1)S(1)} %get-tuple-element.17.p_ref, bf16[576,512]{1,0:T(8,128)(2,1)S(1)} %constant_dynamic-update-slice_fusion.w_ref, bf16[512,1024]{1,0:T(8,128)(2,1)S(1)} %get-tuple-element.19.h_ref), custom_call_target="tpu_custom_call" | custom-call | flops 1207959552 | bytes 6356992 | tf_op jit(solution)/shard_map/pallas_call | solution.py:192
  57.0 2.4 %shard_map.64.h_ref.acts_ref = bf16[512,1024]{1,0:T(8,128)(2,1)S(1)} custom-call(bf16[1152,1024]{1,0:T(8,128)(2,1)S(1)} %get-tuple-element.17.p_ref, bf16[576,512]{1,0:T(8,128)(2,1)S(1)} %collective-permute-done.15.w_ref, bf16[512,1024]{1,0:T(8,128)(2,1)S(1)} %get-tuple-element.19.h_ref, f32[512,1024]{1,0:T(8,128)S(1)} %get-tuple-element.24.refs_0_, ...), custom_call_target="tpu_custom_call" | custom-call | flops 1207959552 | bytes 7405568 | tf_op jit(solution)/shard_map/pallas_call | solution.py:192
  59.4 1.7 %shard_map.66 = bf16[592,512]{1,0:T(8,128)(2,1)S(1)} custom-call(bf16[1152,1024]{1,0:T(8,128)(2,1)S(1)} %get-tuple-element.17.p_ref, bf16[576,512]{1,0:T(8,128)(2,1)S(1)} %collective-permute-done.15.w_ref, bf16[512,1024]{1,0:T(8,128)(2,1)S(1)} %shard_map.64.h_ref.acts_ref), custom_call_target="tpu_custom_call" | custom-call | flops 1207959552 | bytes 4603904 | tf_op jit(solution)/shard_map/pallas_call | solution.py:192
  65.1 1.9 %collective-permute-start.19 = (bf16[96,512]{1,0:T(8,128)(2,1)S(1)}, bf16[96,512]{1,0:T(8,128)(2,1)S(1)}, u32[]{:S(2)}, u32[]{:S(2)}) collective-permute-start(bf16[96,512]{1,0:T(8,128)(2,1)S(1)} %get-tuple-element.65), channel_id=1, source_target_pairs={{0,6},{1,7},{2,4},{3,5},{4,2},{5,3},{6,0},{7,1},{8,14},{9,15},{10,... | collective-permute-start | bytes 294920 | tf_op jit(solution)/shard_map/ppermute | solution.py:307
  68.7 2.5 %collective-permute-done.17 = bf16[96,512]{1,0:T(8,128)(2,1)S(1)} collective-permute-done((bf16[96,512]{1,0:T(8,128)(2,1)S(1)}, bf16[96,512]{1,0:T(8,128)(2,1)S(1)}, u32[]{:S(2)}, u32[]{:S(2)}) %collective-permute-start.17) | collective-permute-done | bytes 98336 | tf_op jit(solution)/shard_map/ppermute | solution.py:307
  72.4 2.9 %collective-permute-start.20 = (bf16[96,512]{1,0:T(8,128)(2,1)S(1)}, bf16[96,512]{1,0:T(8,128)(2,1)S(1)}, u32[]{:S(2)}, u32[]{:S(2)}) collective-permute-start(bf16[96,512]{1,0:T(8,128)(2,1)S(1)} %maximum_maximum_fusion.1), channel_id=1, source_target_pairs={{0,8},{1,9},{2,10},{3,11},{4,12},{5,13},{6,14},{7,15},{8,0},{9,1},... | collective-permute-start | bytes 294920 | tf_op jit(solution)/shard_map/ppermute | solution.py:307
  75.7 3.2 %collective-permute-done.20 = bf16[96,512]{1,0:T(8,128)(2,1)S(1)} collective-permute-done((bf16[96,512]{1,0:T(8,128)(2,1)S(1)}, bf16[96,512]{1,0:T(8,128)(2,1)S(1)}, u32[]{:S(2)}, u32[]{:S(2)}) %collective-permute-start.20) | collective-permute-done | bytes 98336 | tf_op jit(solution)/shard_map/ppermute | solution.py:307
  80.2 2.7 %collective-permute-start.23 = (bf16[64,512]{1,0:T(8,128)(2,1)S(1)}, bf16[64,512]{1,0:T(8,128)(2,1)S(1)}, u32[]{:S(2)}, u32[]{:S(2)}) collective-permute-start(bf16[64,512]{1,0:T(8,128)(2,1)S(1)} %fusion.8), channel_id=1, source_target_pairs={{0,8},{1,9},{2,10},{3,11},{4,12},{5,13},{6,14},{7,15},{8,0},{9,1},... | collective-permute-start | bytes 196616 | tf_op jit(solution)/shard_map/ppermute | solution.py:304
  88.1 1.6 %collective-permute-start.26 = (bf16[64,512]{1,0:T(8,128)(2,1)S(1)}, bf16[64,512]{1,0:T(8,128)(2,1)S(1)}, u32[]{:S(2)}, u32[]{:S(2)}) collective-permute-start(bf16[64,512]{1,0:T(8,128)(2,1)S(1)} %get-tuple-element.33), channel_id=1, source_target_pairs={{0,2},{1,3},{2,0},{3,1},{4,6},{5,7},{6,4},{7,5},{8,10},{9,11},{10,... | collective-permute-start | bytes 196616 | tf_op jit(solution)/shard_map/ppermute | solution.py:340
  90.2 2.2 %collective-permute-done.26 = bf16[64,512]{1,0:T(8,128)(2,1)S(1)} collective-permute-done((bf16[64,512]{1,0:T(8,128)(2,1)S(1)}, bf16[64,512]{1,0:T(8,128)(2,1)S(1)}, u32[]{:S(2)}, u32[]{:S(2)}) %collective-permute-start.26) | collective-permute-done | bytes 65568 | tf_op jit(solution)/shard_map/ppermute | solution.py:340
  92.7 1.7 %shard_map.68 = (bf16[1152,512]{1,0:T(8,128)(2,1)}, bf16[512,1024]{1,0:T(8,128)(2,1)}) custom-call(s32[4]{0:T(128)S(1)} %pad_add_fusion.at_ref, bf16[576,512]{1,0:T(8,128)(2,1)S(1)} %constant_dynamic-update-slice_fusion.6.own_ref, bf16[512,1024]{1,0:T(8,128)(2,1)S(1)} %shard_map.64.h_ref.acts_ref), custom_call_target="tpu_custom_call" | custom-call | flops 536870912 | bytes 3866640 | tf_op jit(solution)/shard_map/pallas_call | solution.py:192
  (103 shorter events, 25.9 us)
Async XLA Ops:
  1.4 6.7 %collective-permute-start.1 = (bf16[2,128]{1,0:T(2,128)(2,1)S(1)}, bf16[2,128]{1,0:T(2,128)(2,1)S(1)}, u32[]{:S(2)}, u32[]{:S(2)}) collective-permute-start(bf16[2,128]{1,0:T(2,128)(2,1)S(1)} %get-tuple-element.52), channel_id=1, source_target_pairs={{0,15},{1,2},{2,1},{3,4},{4,3},{5,6},{6,5},{7,8},{8,7},{9,10},{10,... | collective-permute-start | bytes 1544 | tf_op jit(solution)/shard_map/ppermute | solution.py:273
  25.9 7.8 %collective-permute-start.3 = (bf16[96,512]{1,0:T(8,128)(2,1)S(1)}, bf16[96,512]{1,0:T(8,128)(2,1)S(1)}, u32[]{:S(2)}, u32[]{:S(2)}) collective-permute-start(bf16[96,512]{1,0:T(8,128)(2,1)S(1)} %get-tuple-element.67), channel_id=1, source_target_pairs={{0,2},{1,3},{2,0},{3,1},{4,6},{5,7},{6,4},{7,5},{8,10},{9,11},{10,... | collective-permute-start | bytes 294920 | tf_op jit(solution)/shard_map/ppermute | solution.py:307
  26.0 7.7 %collective-permute-start.5 = (bf16[96,512]{1,0:T(8,128)(2,1)S(1)}, bf16[96,512]{1,0:T(8,128)(2,1)S(1)}, u32[]{:S(2)}, u32[]{:S(2)}) collective-permute-start(bf16[96,512]{1,0:T(8,128)(2,1)S(1)} %get-tuple-element.68), channel_id=1, source_target_pairs={{0,6},{1,7},{2,4},{3,5},{4,2},{5,3},{6,0},{7,1},{8,14},{9,15},{10,... | collective-permute-start | bytes 294920 | tf_op jit(solution)/shard_map/ppermute | solution.py:307
  27.6 6.9 %collective-permute-start.4 = (bf16[96,512]{1,0:T(8,128)(2,1)S(1)}, bf16[96,512]{1,0:T(8,128)(2,1)S(1)}, u32[]{:S(2)}, u32[]{:S(2)}) collective-permute-start(bf16[96,512]{1,0:T(8,128)(2,1)S(1)} %get-tuple-element.69), channel_id=1, source_target_pairs={{0,4},{1,5},{2,6},{3,7},{4,0},{5,1},{6,2},{7,3},{8,12},{9,13},{10,... | collective-permute-start | bytes 294920 | tf_op jit(solution)/shard_map/ppermute | solution.py:307
  29.5 7.4 %collective-permute-start.7 = (bf16[128,512]{1,0:T(8,128)(2,1)S(1)}, bf16[128,512]{1,0:T(8,128)(2,1)S(1)}, u32[]{:S(2)}, u32[]{:S(2)}) collective-permute-start(bf16[128,512]{1,0:T(8,128)(2,1)S(1)} %pad_maximum_fusion.14), channel_id=1, source_target_pairs={{0,2},{1,3},{2,0},{3,1},{4,6},{5,7},{6,4},{7,5},{8,10},{9,11},{10,... | collective-permute-start | bytes 393224 | tf_op jit(solution)/shard_map/ppermute | solution.py:323
  34.6 7.2 %collective-permute-start.6 = (bf16[96,512]{1,0:T(8,128)(2,1)S(1)}, bf16[96,512]{1,0:T(8,128)(2,1)S(1)}, u32[]{:S(2)}, u32[]{:S(2)}) collective-permute-start(bf16[96,512]{1,0:T(8,128)(2,1)S(1)} %maximum_maximum_fusion), channel_id=1, source_target_pairs={{0,8},{1,9},{2,10},{3,11},{4,12},{5,13},{6,14},{7,15},{8,0},{9,1},... | collective-permute-start | bytes 294920 | tf_op jit(solution)/shard_map/ppermute | solution.py:307
  36.9 5.2 %collective-permute-start.8 = (bf16[64,512]{1,0:T(8,128)(2,1)S(1)}, bf16[64,512]{1,0:T(8,128)(2,1)S(1)}, u32[]{:S(2)}, u32[]{:S(2)}) collective-permute-start(bf16[64,512]{1,0:T(8,128)(2,1)S(1)} %fusion.9), channel_id=1, source_target_pairs={{0,4},{1,5},{2,6},{3,7},{4,0},{5,1},{6,2},{7,3},{8,12},{9,13},{10,... | collective-permute-start | bytes 196616 | tf_op jit(solution)/shard_map/ppermute | solution.py:326
  41.9 5.1 %collective-permute-start.10 = (bf16[80,512]{1,0:T(8,128)(2,1)S(1)}, bf16[80,512]{1,0:T(8,128)(2,1)S(1)}, u32[]{:S(2)}, u32[]{:S(2)}) collective-permute-start(bf16[80,512]{1,0:T(8,128)(2,1)S(1)} %get-tuple-element.45), channel_id=1, source_target_pairs={{0,4},{1,5},{2,6},{3,7},{4,0},{5,1},{6,2},{7,3},{8,12},{9,13},{10,... | collective-permute-start | bytes 245768 | tf_op jit(solution)/shard_map/ppermute | solution.py:342
  42.1 5.7 %collective-permute-start.9 = (bf16[64,512]{1,0:T(8,128)(2,1)S(1)}, bf16[64,512]{1,0:T(8,128)(2,1)S(1)}, u32[]{:S(2)}, u32[]{:S(2)}) collective-permute-start(bf16[64,512]{1,0:T(8,128)(2,1)S(1)} %fusion.11), channel_id=1, source_target_pairs={{0,8},{1,9},{2,10},{3,11},{4,12},{5,13},{6,14},{7,15},{8,0},{9,1},... | collective-permute-start | bytes 196616 | tf_op jit(solution)/shard_map/ppermute | solution.py:304
  47.0 6.4 %collective-permute-start.11 = (bf16[160,512]{1,0:T(8,128)(2,1)S(1)}, bf16[160,512]{1,0:T(8,128)(2,1)S(1)}, u32[]{:S(2)}, u32[]{:S(2)}) collective-permute-start(bf16[160,512]{1,0:T(8,128)(2,1)S(1)} %pad_maximum_fusion.12), channel_id=1, source_target_pairs={{0,2},{1,3},{2,0},{3,1},{4,6},{5,7},{6,4},{7,5},{8,10},{9,11},{10,... | collective-permute-start | bytes 491528 | tf_op jit(solution)/shard_map/ppermute | solution.py:343
  47.9 7.1 %collective-permute-start.14 = (bf16[64,512]{1,0:T(8,128)(2,1)S(1)}, bf16[64,512]{1,0:T(8,128)(2,1)S(1)}, u32[]{:S(2)}, u32[]{:S(2)}) collective-permute-start(bf16[64,512]{1,0:T(8,128)(2,1)S(1)} %get-tuple-element.43), channel_id=1, source_target_pairs={{0,6},{1,7},{2,4},{3,5},{4,2},{5,3},{6,0},{7,1},{8,14},{9,15},{10,... | collective-permute-start | bytes 196616 | tf_op jit(solution)/shard_map/ppermute | solution.py:340
  49.9 5.0 %collective-permute-start.13 = (bf16[64,512]{1,0:T(8,128)(2,1)S(1)}, bf16[64,512]{1,0:T(8,128)(2,1)S(1)}, u32[]{:S(2)}, u32[]{:S(2)}) collective-permute-start(bf16[64,512]{1,0:T(8,128)(2,1)S(1)} %get-tuple-element.43), channel_id=1, source_target_pairs={{0,4},{1,5},{2,6},{3,7},{4,0},{5,1},{6,2},{7,3},{8,12},{9,13},{10,... | collective-permute-start | bytes 196616 | tf_op jit(solution)/shard_map/ppermute | solution.py:340
  64.1 7.0 %collective-permute-start.17 = (bf16[96,512]{1,0:T(8,128)(2,1)S(1)}, bf16[96,512]{1,0:T(8,128)(2,1)S(1)}, u32[]{:S(2)}, u32[]{:S(2)}) collective-permute-start(bf16[96,512]{1,0:T(8,128)(2,1)S(1)} %get-tuple-element.64), channel_id=1, source_target_pairs={{0,2},{1,3},{2,0},{3,1},{4,6},{5,7},{6,4},{7,5},{8,10},{9,11},{10,... | collective-permute-start | bytes 294920 | tf_op jit(solution)/shard_map/ppermute | solution.py:307
  65.1 6.4 %collective-permute-start.19 = (bf16[96,512]{1,0:T(8,128)(2,1)S(1)}, bf16[96,512]{1,0:T(8,128)(2,1)S(1)}, u32[]{:S(2)}, u32[]{:S(2)}) collective-permute-start(bf16[96,512]{1,0:T(8,128)(2,1)S(1)} %get-tuple-element.65), channel_id=1, source_target_pairs={{0,6},{1,7},{2,4},{3,5},{4,2},{5,3},{6,0},{7,1},{8,14},{9,15},{10,... | collective-permute-start | bytes 294920 | tf_op jit(solution)/shard_map/ppermute | solution.py:307
  67.0 5.3 %collective-permute-start.18 = (bf16[96,512]{1,0:T(8,128)(2,1)S(1)}, bf16[96,512]{1,0:T(8,128)(2,1)S(1)}, u32[]{:S(2)}, u32[]{:S(2)}) collective-permute-start(bf16[96,512]{1,0:T(8,128)(2,1)S(1)} %get-tuple-element.66), channel_id=1, source_target_pairs={{0,4},{1,5},{2,6},{3,7},{4,0},{5,1},{6,2},{7,3},{8,12},{9,13},{10,... | collective-permute-start | bytes 294920 | tf_op jit(solution)/shard_map/ppermute | solution.py:307
  67.7 7.6 %collective-permute-start.21 = (bf16[128,512]{1,0:T(8,128)(2,1)S(1)}, bf16[128,512]{1,0:T(8,128)(2,1)S(1)}, u32[]{:S(2)}, u32[]{:S(2)}) collective-permute-start(bf16[128,512]{1,0:T(8,128)(2,1)S(1)} %pad_maximum_fusion.15), channel_id=1, source_target_pairs={{0,2},{1,3},{2,0},{3,1},{4,6},{5,7},{6,4},{7,5},{8,10},{9,11},{10,... | collective-permute-start | bytes 393224 | tf_op jit(solution)/shard_map/ppermute | solution.py:323
  72.4 6.5 %collective-permute-start.20 = (bf16[96,512]{1,0:T(8,128)(2,1)S(1)}, bf16[96,512]{1,0:T(8,128)(2,1)S(1)}, u32[]{:S(2)}, u32[]{:S(2)}) collective-permute-start(bf16[96,512]{1,0:T(8,128)(2,1)S(1)} %maximum_maximum_fusion.1), channel_id=1, source_target_pairs={{0,8},{1,9},{2,10},{3,11},{4,12},{5,13},{6,14},{7,15},{8,0},{9,1},... | collective-permute-start | bytes 294920 | tf_op jit(solution)/shard_map/ppermute | solution.py:307
  75.3 4.8 %collective-permute-start.22 = (bf16[64,512]{1,0:T(8,128)(2,1)S(1)}, bf16[64,512]{1,0:T(8,128)(2,1)S(1)}, u32[]{:S(2)}, u32[]{:S(2)}) collective-permute-start(bf16[64,512]{1,0:T(8,128)(2,1)S(1)} %fusion.6), channel_id=1, source_target_pairs={{0,4},{1,5},{2,6},{3,7},{4,0},{5,1},{6,2},{7,3},{8,12},{9,13},{10,... | collective-permute-start | bytes 196616 | tf_op jit(solution)/shard_map/ppermute | solution.py:326
  79.0 5.0 %collective-permute-start.24 = (bf16[80,512]{1,0:T(8,128)(2,1)S(1)}, bf16[80,512]{1,0:T(8,128)(2,1)S(1)}, u32[]{:S(2)}, u32[]{:S(2)}) collective-permute-start(bf16[80,512]{1,0:T(8,128)(2,1)S(1)} %get-tuple-element.35), channel_id=1, source_target_pairs={{0,4},{1,5},{2,6},{3,7},{4,0},{5,1},{6,2},{7,3},{8,12},{9,13},{10,... | collective-permute-start | bytes 245768 | tf_op jit(solution)/shard_map/ppermute | solution.py:342
  80.2 6.0 %collective-permute-start.23 = (bf16[64,512]{1,0:T(8,128)(2,1)S(1)}, bf16[64,512]{1,0:T(8,128)(2,1)S(1)}, u32[]{:S(2)}, u32[]{:S(2)}) collective-permute-start(bf16[64,512]{1,0:T(8,128)(2,1)S(1)} %fusion.8), channel_id=1, source_target_pairs={{0,8},{1,9},{2,10},{3,11},{4,12},{5,13},{6,14},{7,15},{8,0},{9,1},... | collective-permute-start | bytes 196616 | tf_op jit(solution)/shard_map/ppermute | solution.py:304
  84.0 6.2 %collective-permute-start.25 = (bf16[160,512]{1,0:T(8,128)(2,1)S(1)}, bf16[160,512]{1,0:T(8,128)(2,1)S(1)}, u32[]{:S(2)}, u32[]{:S(2)}) collective-permute-start(bf16[160,512]{1,0:T(8,128)(2,1)S(1)} %pad_maximum_fusion.13), channel_id=1, source_target_pairs={{0,2},{1,3},{2,0},{3,1},{4,6},{5,7},{6,4},{7,5},{8,10},{9,11},{10,... | collective-permute-start | bytes 491528 | tf_op jit(solution)/shard_map/ppermute | solution.py:343
  86.2 6.2 %collective-permute-start.28 = (bf16[64,512]{1,0:T(8,128)(2,1)S(1)}, bf16[64,512]{1,0:T(8,128)(2,1)S(1)}, u32[]{:S(2)}, u32[]{:S(2)}) collective-permute-start(bf16[64,512]{1,0:T(8,128)(2,1)S(1)} %get-tuple-element.33), channel_id=1, source_target_pairs={{0,6},{1,7},{2,4},{3,5},{4,2},{5,3},{6,0},{7,1},{8,14},{9,15},{10,... | collective-permute-start | bytes 196616 | tf_op jit(solution)/shard_map/ppermute | solution.py:340
  87.6 4.8 %collective-permute-start.27 = (bf16[64,512]{1,0:T(8,128)(2,1)S(1)}, bf16[64,512]{1,0:T(8,128)(2,1)S(1)}, u32[]{:S(2)}, u32[]{:S(2)}) collective-permute-start(bf16[64,512]{1,0:T(8,128)(2,1)S(1)} %get-tuple-element.33), channel_id=1, source_target_pairs={{0,4},{1,5},{2,6},{3,7},{4,0},{5,1},{6,2},{7,3},{8,12},{9,13},{10,... | collective-permute-start | bytes 196616 | tf_op jit(solution)/shard_map/ppermute | solution.py:340
  88.1 4.3 %collective-permute-start.26 = (bf16[64,512]{1,0:T(8,128)(2,1)S(1)}, bf16[64,512]{1,0:T(8,128)(2,1)S(1)}, u32[]{:S(2)}, u32[]{:S(2)}) collective-permute-start(bf16[64,512]{1,0:T(8,128)(2,1)S(1)} %get-tuple-element.33), channel_id=1, source_target_pairs={{0,2},{1,3},{2,0},{3,1},{4,6},{5,7},{6,4},{7,5},{8,10},{9,11},{10,... | collective-permute-start | bytes 196616 | tf_op jit(solution)/shard_map/ppermute | solution.py:340
  (6 other events, 14.6 us)

commit v6 on v5

--- a/solution.py
+++ b/solution.py
@@ -68,10 +68,14 @@
     wide[8 : 8 + a_ref.shape[0], :] = a_ref[...].astype(f32)
     wide[6:8, :] = halo_ref[0:2, :]
     wide[8 + a_ref.shape[0] : 10 + a_ref.shape[0], :] = halo_ref[2:4, :]
-    for j in range(2 * HOP // LANES):
-        strip = wide[pl.ds(6 + j, frames, stride=HOP // LANES), :]
-        frame[:, j * LANES : (j + 1) * LANES] = strip.astype(bf16)
-
+    stride = HOP // LANES
+
+    def build(t):
+        for j in range(2 * HOP // LANES):
+            strip = wide[pl.ds(6 + j + t * stride, 512, stride=stride), :]
+            frame[t : t + 512, j * LANES : (j + 1) * LANES] = strip.astype(bf16)
+
+    build(0)
     waited = 0
     for lo, hi in blocks:
         while waited < -(-hi // rows):
@@ -79,6 +83,8 @@
             k_copies[2 * waited + 1].wait()
             waited += 1
         for t in range(0, frames, 512):
+            if lo == 0 and t + 512 < frames:
+                build(t + 512)
             f = frame[t : t + 512, :]
             re = dot_nt(k_ref[lo:hi, :], f)
             im = dot_nt(k_ref[bins + lo : bins + hi, :], f)
@@ -352,7 +358,7 @@
     halo = halo_rows(audio, peers)
     core, quad, pairs = groups_of(peers)
     rows = size // quad.size
-    cuts = [0, (rows // 2 + 15) // 16 * 16, rows]
+    cuts = [0, rows // 2 // 16 * 16, rows]
     order = [quad.me] + [quad.me ^ code for code, _ in quad.others]
     at = [core.me * quad.size + q for q in order] + [(1 - core.me) * quad.size + q for q in order]
     at = jnp.stack(at).astype(jnp.int32)

time: 96.3 us -> 95.8 us (level)
  waiting for transfers between devices: 26.6 us -> 25.4 us
  starting transfers between devices: 37.4 us -> 38.5 us
    ppermute x8, waiting for transfers between devices: 14.9 us -> 12.6 us  [swap(): lax.ppermute(jnp.concatenate([send, halves[0][None], halves[1][None], pad...]
    ppermute x2, waiting for transfers between devices: 2.53 us -> 1 us  [spread(): far = lax.ppermute(part, 'tm', perms[1])]
    ppermute x2, starting transfers between devices: 2.08 us -> 3.12 us  [sum_chips(): mine = mine + lax.ppermute(far, 'tm', perms[1]).astype(f32)]
  transfers between devices with their start and end apart: 30 -> 30, of which waited for: 17 -> 18; matrix products, arithmetic and copies ran while one was open for 1% -> 1% of each run, Pallas kernels for 8% -> 8%
where the time goes in v6:
time: 95.8 us; the launch traced here: 95.6 us
  starting transfers between devices  38.5 us (40%)
  Pallas kernels  28.2 us (29%)
  waiting for transfers between devices  25.4 us (27%)
  other arithmetic  2.07 us (2%)
  between operations  1.22 us (1%)
    pallas_call x11, Pallas kernels, call(): pl.pallas_call(kernel, out_shape=tuple(outs), in_specs=specs or [VMEM] *...  28.2 us
    ppermute x8, starting transfers between devices, swap(): lax.ppermute(jnp.concatenate([send, halves[0][None], halves[1][None], pad...  13.1 us
    ppermute x8, waiting for transfers between devices, swap(): lax.ppermute(jnp.concatenate([send, halves[0][None], halves[1][None], pad...  12.6 us
    ppermute x6, starting transfers between devices, spread(): return [part] + [lax.ppermute(part, 'tm', perm) for perm in perms]  7.11 us
    ppermute x2, starting transfers between devices, swap(): return (lax.ppermute(send, 'tm', perm), None)  6.13 us
    ppermute x1, starting transfers between devices, halo_rows(): two = lax.ppermute(jnp.where(odd, tail, head), 'tm', outer)  5.44 us
    ppermute x6, waiting for transfers between devices, spread(): return [part] + [lax.ppermute(part, 'tm', perm) for perm in perms]  3.91 us
    ppermute x2, waiting for transfers between devices, spread(): got = lax.ppermute(jnp.concatenate([part, far]), 'tm', perms[0])  3.22 us
  transfers between devices with their start and end apart: 30, of which 18 were waited for; matrix products, arithmetic and copies ran while one was open for 1% of the time, Pallas kernels for 8%

profile of v6, /device:TPU:0, one launch (start us, length us, event | category | flops | bytes accessed | tf_op | source)
XLA Modules:
  0.0 95.6 jit_solution(4442834232110903222)
XLA Ops:
  1.4 5.4 %collective-permute-start.1 = (bf16[2,128]{1,0:T(2,128)(2,1)S(1)}, bf16[2,128]{1,0:T(2,128)(2,1)S(1)}, u32[]{:S(2)}, u32[]{:S(2)}) collective-permute-start(bf16[2,128]{1,0:T(2,128)(2,1)S(1)} %get-tuple-element.52), channel_id=1, source_target_pairs={{0,15},{1,2},{2,1},{3,4},{4,3},{5,6},{6,5},{7,8},{8,7},{9,10},{10,... | collective-permute-start | bytes 1544 | tf_op jit(solution)/shard_map/ppermute | solution.py:279
  8.1 13.2 %shard_map.59 = (bf16[1152,1024]{1,0:T(8,128)(2,1)S(1)}, bf16[512,1024]{1,0:T(8,128)(2,1)S(1)}, bf16[1152,512]{1,0:T(8,128)(2,1)S(1)}) custom-call(s32[8]{0:T(128)S(1)} %stack.40.at_ref, f32[4,128]{1,0:T(4,128)S(1)} %maximum_convert_fusion.halo_ref, bf16[4096,128]{1,0:T(8,128)(2,1)} %bitcast.19, bf16[2304,1024]{1,0:T(8,128)(2,1)} %k_hbm.1, ...), custom_call_target="tpu_custom_call" | custom-call | flops 7247757312 | bytes 12584992 | tf_op jit(solution)/shard_map/pallas_call | solution.py:198
  21.4 1.7 %shard_map.61 = bf16[592,512]{1,0:T(8,128)(2,1)S(1)} custom-call(bf16[1152,1024]{1,0:T(8,128)(2,1)S(1)} %get-tuple-element.17.p_ref, bf16[1152,512]{1,0:T(8,128)(2,1)S(1)} %get-tuple-element.18.w_ref, bf16[512,1024]{1,0:T(8,128)(2,1)S(1)} %get-tuple-element.19.h_ref), custom_call_target="tpu_custom_call" | custom-call | flops 1207959552 | bytes 5193728 | tf_op jit(solution)/shard_map/pallas_call | solution.py:198
  25.7 1.6 %collective-permute-start.5 = (bf16[80,512]{1,0:T(8,128)(2,1)S(1)}, bf16[80,512]{1,0:T(8,128)(2,1)S(1)}, u32[]{:S(2)}, u32[]{:S(2)}) collective-permute-start(bf16[80,512]{1,0:T(8,128)(2,1)S(1)} %get-tuple-element.68), channel_id=1, source_target_pairs={{0,6},{1,7},{2,4},{3,5},{4,2},{5,3},{6,0},{7,1},{8,14},{9,15},{10,... | collective-permute-start | bytes 245768 | tf_op jit(solution)/shard_map/ppermute | solution.py:313
  27.3 1.9 %collective-permute-start.4 = (bf16[80,512]{1,0:T(8,128)(2,1)S(1)}, bf16[80,512]{1,0:T(8,128)(2,1)S(1)}, u32[]{:S(2)}, u32[]{:S(2)}) collective-permute-start(bf16[80,512]{1,0:T(8,128)(2,1)S(1)} %get-tuple-element.69), channel_id=1, source_target_pairs={{0,4},{1,5},{2,6},{3,7},{4,0},{5,1},{6,2},{7,3},{8,12},{9,13},{10,... | collective-permute-start | bytes 245768 | tf_op jit(solution)/shard_map/ppermute | solution.py:313
  29.4 3.3 %collective-permute-done.3 = bf16[80,512]{1,0:T(8,128)(2,1)S(1)} collective-permute-done((bf16[80,512]{1,0:T(8,128)(2,1)S(1)}, bf16[80,512]{1,0:T(8,128)(2,1)S(1)}, u32[]{:S(2)}, u32[]{:S(2)}) %collective-permute-start.3) | collective-permute-done | bytes 81952 | tf_op jit(solution)/shard_map/ppermute | solution.py:313
  33.7 2.5 %collective-permute-start.6 = (bf16[80,512]{1,0:T(8,128)(2,1)S(1)}, bf16[80,512]{1,0:T(8,128)(2,1)S(1)}, u32[]{:S(2)}, u32[]{:S(2)}) collective-permute-start(bf16[80,512]{1,0:T(8,128)(2,1)S(1)} %maximum_maximum_fusion), channel_id=1, source_target_pairs={{0,8},{1,9},{2,10},{3,11},{4,12},{5,13},{6,14},{7,15},{8,0},{9,1},... | collective-permute-start | bytes 245768 | tf_op jit(solution)/shard_map/ppermute | solution.py:313
  36.2 1.8 %collective-permute-start.8 = (bf16[80,512]{1,0:T(8,128)(2,1)S(1)}, bf16[80,512]{1,0:T(8,128)(2,1)S(1)}, u32[]{:S(2)}, u32[]{:S(2)}) collective-permute-start(bf16[80,512]{1,0:T(8,128)(2,1)S(1)} %fusion.3), channel_id=1, source_target_pairs={{0,4},{1,5},{2,6},{3,7},{4,0},{5,1},{6,2},{7,3},{8,12},{9,13},{10,... | collective-permute-start | bytes 245768 | tf_op jit(solution)/shard_map/ppermute | solution.py:332
  38.0 2.4 %collective-permute-done.6 = bf16[80,512]{1,0:T(8,128)(2,1)S(1)} collective-permute-done((bf16[80,512]{1,0:T(8,128)(2,1)S(1)}, bf16[80,512]{1,0:T(8,128)(2,1)S(1)}, u32[]{:S(2)}, u32[]{:S(2)}) %collective-permute-start.6) | collective-permute-done | bytes 81952 | tf_op jit(solution)/shard_map/ppermute | solution.py:313
  41.2 3.0 %collective-permute-start.9 = (bf16[80,512]{1,0:T(8,128)(2,1)S(1)}, bf16[80,512]{1,0:T(8,128)(2,1)S(1)}, u32[]{:S(2)}, u32[]{:S(2)}) collective-permute-start(bf16[80,512]{1,0:T(8,128)(2,1)S(1)} %fusion.5), channel_id=1, source_target_pairs={{0,8},{1,9},{2,10},{3,11},{4,12},{5,13},{6,14},{7,15},{8,0},{9,1},... | collective-permute-start | bytes 245768 | tf_op jit(solution)/shard_map/ppermute | solution.py:310
  46.7 2.8 %collective-permute-start.14 = (bf16[80,512]{1,0:T(8,128)(2,1)S(1)}, bf16[80,512]{1,0:T(8,128)(2,1)S(1)}, u32[]{:S(2)}, u32[]{:S(2)}) collective-permute-start(bf16[80,512]{1,0:T(8,128)(2,1)S(1)} %get-tuple-element.43), channel_id=1, source_target_pairs={{0,6},{1,7},{2,4},{3,5},{4,2},{5,3},{6,0},{7,1},{8,14},{9,15},{10,... | collective-permute-start | bytes 245768 | tf_op jit(solution)/shard_map/ppermute | solution.py:346
  50.2 2.3 %collective-permute-done.11 = bf16[128,512]{1,0:T(8,128)(2,1)S(1)} collective-permute-done((bf16[128,512]{1,0:T(8,128)(2,1)S(1)}, bf16[128,512]{1,0:T(8,128)(2,1)S(1)}, u32[]{:S(2)}, u32[]{:S(2)}) %collective-permute-start.11) | collective-permute-done | bytes 131104 | tf_op jit(solution)/shard_map/ppermute | solution.py:349
  52.5 2.0 %collective-permute-done.12 = bf16[80,512]{1,0:T(8,128)(2,1)S(1)} collective-permute-done((bf16[80,512]{1,0:T(8,128)(2,1)S(1)}, bf16[80,512]{1,0:T(8,128)(2,1)S(1)}, u32[]{:S(2)}, u32[]{:S(2)}) %collective-permute-start.12) | collective-permute-done | bytes 81952 | tf_op jit(solution)/shard_map/ppermute | solution.py:346
  54.6 2.0 %shard_map.63 = (f32[512,1024]{1,0:T(8,128)S(1)}, f32[512,128]{1,0:T(8,128)S(1)}) custom-call(bf16[1152,1024]{1,0:T(8,128)(2,1)S(1)} %get-tuple-element.17.p_ref, bf16[576,512]{1,0:T(8,128)(2,1)S(1)} %constant_dynamic-update-slice_fusion.w_ref, bf16[512,1024]{1,0:T(8,128)(2,1)S(1)} %get-tuple-element.19.h_ref), custom_call_target="tpu_custom_call" | custom-call | flops 1207959552 | bytes 6356992 | tf_op jit(solution)/shard_map/pallas_call | solution.py:198
  56.6 2.4 %shard_map.64.h_ref.acts_ref = bf16[512,1024]{1,0:T(8,128)(2,1)S(1)} custom-call(bf16[1152,1024]{1,0:T(8,128)(2,1)S(1)} %get-tuple-element.17.p_ref, bf16[576,512]{1,0:T(8,128)(2,1)S(1)} %collective-permute-done.15.w_ref, bf16[512,1024]{1,0:T(8,128)(2,1)S(1)} %get-tuple-element.19.h_ref, f32[512,1024]{1,0:T(8,128)S(1)} %get-tuple-element.24.refs_0_, ...), custom_call_target="tpu_custom_call" | custom-call | flops 1207959552 | bytes 7405568 | tf_op jit(solution)/shard_map/pallas_call | solution.py:198
  59.0 1.7 %shard_map.66 = bf16[592,512]{1,0:T(8,128)(2,1)S(1)} custom-call(bf16[1152,1024]{1,0:T(8,128)(2,1)S(1)} %get-tuple-element.17.p_ref, bf16[576,512]{1,0:T(8,128)(2,1)S(1)} %collective-permute-done.15.w_ref, bf16[512,1024]{1,0:T(8,128)(2,1)S(1)} %shard_map.64.h_ref.acts_ref), custom_call_target="tpu_custom_call" | custom-call | flops 1207959552 | bytes 4603904 | tf_op jit(solution)/shard_map/pallas_call | solution.py:198
  64.1 2.6 %collective-permute-start.19 = (bf16[80,512]{1,0:T(8,128)(2,1)S(1)}, bf16[80,512]{1,0:T(8,128)(2,1)S(1)}, u32[]{:S(2)}, u32[]{:S(2)}) collective-permute-start(bf16[80,512]{1,0:T(8,128)(2,1)S(1)} %get-tuple-element.65), channel_id=1, source_target_pairs={{0,6},{1,7},{2,4},{3,5},{4,2},{5,3},{6,0},{7,1},{8,14},{9,15},{10,... | collective-permute-start | bytes 245768 | tf_op jit(solution)/shard_map/ppermute | solution.py:313
  67.7 2.6 %collective-permute-done.17 = bf16[80,512]{1,0:T(8,128)(2,1)S(1)} collective-permute-done((bf16[80,512]{1,0:T(8,128)(2,1)S(1)}, bf16[80,512]{1,0:T(8,128)(2,1)S(1)}, u32[]{:S(2)}, u32[]{:S(2)}) %collective-permute-start.17) | collective-permute-done | bytes 81952 | tf_op jit(solution)/shard_map/ppermute | solution.py:313
  71.6 3.5 %collective-permute-start.20 = (bf16[80,512]{1,0:T(8,128)(2,1)S(1)}, bf16[80,512]{1,0:T(8,128)(2,1)S(1)}, u32[]{:S(2)}, u32[]{:S(2)}) collective-permute-start(bf16[80,512]{1,0:T(8,128)(2,1)S(1)} %maximum_maximum_fusion.1), channel_id=1, source_target_pairs={{0,8},{1,9},{2,10},{3,11},{4,12},{5,13},{6,14},{7,15},{8,0},{9,1},... | collective-permute-start | bytes 245768 | tf_op jit(solution)/shard_map/ppermute | solution.py:313
  76.4 2.3 %collective-permute-done.20 = bf16[80,512]{1,0:T(8,128)(2,1)S(1)} collective-permute-done((bf16[80,512]{1,0:T(8,128)(2,1)S(1)}, bf16[80,512]{1,0:T(8,128)(2,1)S(1)}, u32[]{:S(2)}, u32[]{:S(2)}) %collective-permute-start.20) | collective-permute-done | bytes 81952 | tf_op jit(solution)/shard_map/ppermute | solution.py:313
  79.7 3.1 %collective-permute-start.23 = (bf16[80,512]{1,0:T(8,128)(2,1)S(1)}, bf16[80,512]{1,0:T(8,128)(2,1)S(1)}, u32[]{:S(2)}, u32[]{:S(2)}) collective-permute-start(bf16[80,512]{1,0:T(8,128)(2,1)S(1)} %fusion.2), channel_id=1, source_target_pairs={{0,8},{1,9},{2,10},{3,11},{4,12},{5,13},{6,14},{7,15},{8,0},{9,1},... | collective-permute-start | bytes 245768 | tf_op jit(solution)/shard_map/ppermute | solution.py:310
  83.7 1.8 %collective-permute-done.23 = bf16[80,512]{1,0:T(8,128)(2,1)S(1)} collective-permute-done((bf16[80,512]{1,0:T(8,128)(2,1)S(1)}, bf16[80,512]{1,0:T(8,128)(2,1)S(1)}, u32[]{:S(2)}, u32[]{:S(2)}) %collective-permute-start.23) | collective-permute-done | bytes 81952 | tf_op jit(solution)/shard_map/ppermute | solution.py:310
  90.0 1.9 %collective-permute-done.26 = bf16[80,512]{1,0:T(8,128)(2,1)S(1)} collective-permute-done((bf16[80,512]{1,0:T(8,128)(2,1)S(1)}, bf16[80,512]{1,0:T(8,128)(2,1)S(1)}, u32[]{:S(2)}, u32[]{:S(2)}) %collective-permute-start.26) | collective-permute-done | bytes 81952 | tf_op jit(solution)/shard_map/ppermute | solution.py:346
  92.3 1.7 %shard_map.68 = (bf16[1152,512]{1,0:T(8,128)(2,1)}, bf16[512,1024]{1,0:T(8,128)(2,1)}) custom-call(s32[4]{0:T(128)S(1)} %pad_add_fusion.at_ref, bf16[576,512]{1,0:T(8,128)(2,1)S(1)} %constant_dynamic-update-slice_fusion.6.own_ref, bf16[512,1024]{1,0:T(8,128)(2,1)S(1)} %shard_map.64.h_ref.acts_ref), custom_call_target="tpu_custom_call" | custom-call | flops 536870912 | bytes 3866640 | tf_op jit(solution)/shard_map/pallas_call | solution.py:198
  (103 shorter events, 24.7 us)
Async XLA Ops:
  1.4 6.7 %collective-permute-start.1 = (bf16[2,128]{1,0:T(2,128)(2,1)S(1)}, bf16[2,128]{1,0:T(2,128)(2,1)S(1)}, u32[]{:S(2)}, u32[]{:S(2)}) collective-permute-start(bf16[2,128]{1,0:T(2,128)(2,1)S(1)} %get-tuple-element.52), channel_id=1, source_target_pairs={{0,15},{1,2},{2,1},{3,4},{4,3},{5,6},{6,5},{7,8},{8,7},{9,10},{10,... | collective-permute-start | bytes 1544 | tf_op jit(solution)/shard_map/ppermute | solution.py:279
  25.7 7.1 %collective-permute-start.3 = (bf16[80,512]{1,0:T(8,128)(2,1)S(1)}, bf16[80,512]{1,0:T(8,128)(2,1)S(1)}, u32[]{:S(2)}, u32[]{:S(2)}) collective-permute-start(bf16[80,512]{1,0:T(8,128)(2,1)S(1)} %get-tuple-element.67), channel_id=1, source_target_pairs={{0,2},{1,3},{2,0},{3,1},{4,6},{5,7},{6,4},{7,5},{8,10},{9,11},{10,... | collective-permute-start | bytes 245768 | tf_op jit(solution)/shard_map/ppermute | solution.py:313
  25.7 7.0 %collective-permute-start.5 = (bf16[80,512]{1,0:T(8,128)(2,1)S(1)}, bf16[80,512]{1,0:T(8,128)(2,1)S(1)}, u32[]{:S(2)}, u32[]{:S(2)}) collective-permute-start(bf16[80,512]{1,0:T(8,128)(2,1)S(1)} %get-tuple-element.68), channel_id=1, source_target_pairs={{0,6},{1,7},{2,4},{3,5},{4,2},{5,3},{6,0},{7,1},{8,14},{9,15},{10,... | collective-permute-start | bytes 245768 | tf_op jit(solution)/shard_map/ppermute | solution.py:313
  27.3 6.2 %collective-permute-start.4 = (bf16[80,512]{1,0:T(8,128)(2,1)S(1)}, bf16[80,512]{1,0:T(8,128)(2,1)S(1)}, u32[]{:S(2)}, u32[]{:S(2)}) collective-permute-start(bf16[80,512]{1,0:T(8,128)(2,1)S(1)} %get-tuple-element.69), channel_id=1, source_target_pairs={{0,4},{1,5},{2,6},{3,7},{4,0},{5,1},{6,2},{7,3},{8,12},{9,13},{10,... | collective-permute-start | bytes 245768 | tf_op jit(solution)/shard_map/ppermute | solution.py:313
  29.2 7.0 %collective-permute-start.7 = (bf16[160,512]{1,0:T(8,128)(2,1)S(1)}, bf16[160,512]{1,0:T(8,128)(2,1)S(1)}, u32[]{:S(2)}, u32[]{:S(2)}) collective-permute-start(bf16[160,512]{1,0:T(8,128)(2,1)S(1)} %pad_maximum_fusion), channel_id=1, source_target_pairs={{0,2},{1,3},{2,0},{3,1},{4,6},{5,7},{6,4},{7,5},{8,10},{9,11},{10,... | collective-permute-start | bytes 491528 | tf_op jit(solution)/shard_map/ppermute | solution.py:329
  33.7 6.8 %collective-permute-start.6 = (bf16[80,512]{1,0:T(8,128)(2,1)S(1)}, bf16[80,512]{1,0:T(8,128)(2,1)S(1)}, u32[]{:S(2)}, u32[]{:S(2)}) collective-permute-start(bf16[80,512]{1,0:T(8,128)(2,1)S(1)} %maximum_maximum_fusion), channel_id=1, source_target_pairs={{0,8},{1,9},{2,10},{3,11},{4,12},{5,13},{6,14},{7,15},{8,0},{9,1},... | collective-permute-start | bytes 245768 | tf_op jit(solution)/shard_map/ppermute | solution.py:313
  36.2 5.0 %collective-permute-start.8 = (bf16[80,512]{1,0:T(8,128)(2,1)S(1)}, bf16[80,512]{1,0:T(8,128)(2,1)S(1)}, u32[]{:S(2)}, u32[]{:S(2)}) collective-permute-start(bf16[80,512]{1,0:T(8,128)(2,1)S(1)} %fusion.3), channel_id=1, source_target_pairs={{0,4},{1,5},{2,6},{3,7},{4,0},{5,1},{6,2},{7,3},{8,12},{9,13},{10,... | collective-permute-start | bytes 245768 | tf_op jit(solution)/shard_map/ppermute | solution.py:332
  41.2 5.4 %collective-permute-start.9 = (bf16[80,512]{1,0:T(8,128)(2,1)S(1)}, bf16[80,512]{1,0:T(8,128)(2,1)S(1)}, u32[]{:S(2)}, u32[]{:S(2)}) collective-permute-start(bf16[80,512]{1,0:T(8,128)(2,1)S(1)} %fusion.5), channel_id=1, source_target_pairs={{0,8},{1,9},{2,10},{3,11},{4,12},{5,13},{6,14},{7,15},{8,0},{9,1},... | collective-permute-start | bytes 245768 | tf_op jit(solution)/shard_map/ppermute | solution.py:310
  44.8 7.7 %collective-permute-start.11 = (bf16[128,512]{1,0:T(8,128)(2,1)S(1)}, bf16[128,512]{1,0:T(8,128)(2,1)S(1)}, u32[]{:S(2)}, u32[]{:S(2)}) collective-permute-start(bf16[128,512]{1,0:T(8,128)(2,1)S(1)} %pad_maximum_fusion.14), channel_id=1, source_target_pairs={{0,2},{1,3},{2,0},{3,1},{4,6},{5,7},{6,4},{7,5},{8,10},{9,11},{10,... | collective-permute-start | bytes 393224 | tf_op jit(solution)/shard_map/ppermute | solution.py:349
  46.7 7.9 %collective-permute-start.14 = (bf16[80,512]{1,0:T(8,128)(2,1)S(1)}, bf16[80,512]{1,0:T(8,128)(2,1)S(1)}, u32[]{:S(2)}, u32[]{:S(2)}) collective-permute-start(bf16[80,512]{1,0:T(8,128)(2,1)S(1)} %get-tuple-element.43), channel_id=1, source_target_pairs={{0,6},{1,7},{2,4},{3,5},{4,2},{5,3},{6,0},{7,1},{8,14},{9,15},{10,... | collective-permute-start | bytes 245768 | tf_op jit(solution)/shard_map/ppermute | solution.py:346
  49.4 5.0 %collective-permute-start.13 = (bf16[80,512]{1,0:T(8,128)(2,1)S(1)}, bf16[80,512]{1,0:T(8,128)(2,1)S(1)}, u32[]{:S(2)}, u32[]{:S(2)}) collective-permute-start(bf16[80,512]{1,0:T(8,128)(2,1)S(1)} %get-tuple-element.43), channel_id=1, source_target_pairs={{0,4},{1,5},{2,6},{3,7},{4,0},{5,1},{6,2},{7,3},{8,12},{9,13},{10,... | collective-permute-start | bytes 245768 | tf_op jit(solution)/shard_map/ppermute | solution.py:346
  50.0 4.4 %collective-permute-start.12 = (bf16[80,512]{1,0:T(8,128)(2,1)S(1)}, bf16[80,512]{1,0:T(8,128)(2,1)S(1)}, u32[]{:S(2)}, u32[]{:S(2)}) collective-permute-start(bf16[80,512]{1,0:T(8,128)(2,1)S(1)} %get-tuple-element.43), channel_id=1, source_target_pairs={{0,2},{1,3},{2,0},{3,1},{4,6},{5,7},{6,4},{7,5},{8,10},{9,11},{10,... | collective-permute-start | bytes 245768 | tf_op jit(solution)/shard_map/ppermute | solution.py:346
  63.7 6.6 %collective-permute-start.17 = (bf16[80,512]{1,0:T(8,128)(2,1)S(1)}, bf16[80,512]{1,0:T(8,128)(2,1)S(1)}, u32[]{:S(2)}, u32[]{:S(2)}) collective-permute-start(bf16[80,512]{1,0:T(8,128)(2,1)S(1)} %get-tuple-element.64), channel_id=1, source_target_pairs={{0,2},{1,3},{2,0},{3,1},{4,6},{5,7},{6,4},{7,5},{8,10},{9,11},{10,... | collective-permute-start | bytes 245768 | tf_op jit(solution)/shard_map/ppermute | solution.py:313
  64.1 6.2 %collective-permute-start.19 = (bf16[80,512]{1,0:T(8,128)(2,1)S(1)}, bf16[80,512]{1,0:T(8,128)(2,1)S(1)}, u32[]{:S(2)}, u32[]{:S(2)}) collective-permute-start(bf16[80,512]{1,0:T(8,128)(2,1)S(1)} %get-tuple-element.65), channel_id=1, source_target_pairs={{0,6},{1,7},{2,4},{3,5},{4,2},{5,3},{6,0},{7,1},{8,14},{9,15},{10,... | collective-permute-start | bytes 245768 | tf_op jit(solution)/shard_map/ppermute | solution.py:313
  66.7 4.7 %collective-permute-start.18 = (bf16[80,512]{1,0:T(8,128)(2,1)S(1)}, bf16[80,512]{1,0:T(8,128)(2,1)S(1)}, u32[]{:S(2)}, u32[]{:S(2)}) collective-permute-start(bf16[80,512]{1,0:T(8,128)(2,1)S(1)} %get-tuple-element.66), channel_id=1, source_target_pairs={{0,4},{1,5},{2,6},{3,7},{4,0},{5,1},{6,2},{7,3},{8,12},{9,13},{10,... | collective-permute-start | bytes 245768 | tf_op jit(solution)/shard_map/ppermute | solution.py:313
  67.3 7.8 %collective-permute-start.21 = (bf16[160,512]{1,0:T(8,128)(2,1)S(1)}, bf16[160,512]{1,0:T(8,128)(2,1)S(1)}, u32[]{:S(2)}, u32[]{:S(2)}) collective-permute-start(bf16[160,512]{1,0:T(8,128)(2,1)S(1)} %pad_maximum_fusion.1), channel_id=1, source_target_pairs={{0,2},{1,3},{2,0},{3,1},{4,6},{5,7},{6,4},{7,5},{8,10},{9,11},{10,... | collective-permute-start | bytes 491528 | tf_op jit(solution)/shard_map/ppermute | solution.py:329
  71.6 7.2 %collective-permute-start.20 = (bf16[80,512]{1,0:T(8,128)(2,1)S(1)}, bf16[80,512]{1,0:T(8,128)(2,1)S(1)}, u32[]{:S(2)}, u32[]{:S(2)}) collective-permute-start(bf16[80,512]{1,0:T(8,128)(2,1)S(1)} %maximum_maximum_fusion.1), channel_id=1, source_target_pairs={{0,8},{1,9},{2,10},{3,11},{4,12},{5,13},{6,14},{7,15},{8,0},{9,1},... | collective-permute-start | bytes 245768 | tf_op jit(solution)/shard_map/ppermute | solution.py:313
  75.1 4.6 %collective-permute-start.22 = (bf16[80,512]{1,0:T(8,128)(2,1)S(1)}, bf16[80,512]{1,0:T(8,128)(2,1)S(1)}, u32[]{:S(2)}, u32[]{:S(2)}) collective-permute-start(bf16[80,512]{1,0:T(8,128)(2,1)S(1)} %fusion), channel_id=1, source_target_pairs={{0,4},{1,5},{2,6},{3,7},{4,0},{5,1},{6,2},{7,3},{8,12},{9,13},{10,... | collective-permute-start | bytes 245768 | tf_op jit(solution)/shard_map/ppermute | solution.py:332
  78.8 4.4 %collective-permute-start.24 = (bf16[64,512]{1,0:T(8,128)(2,1)S(1)}, bf16[64,512]{1,0:T(8,128)(2,1)S(1)}, u32[]{:S(2)}, u32[]{:S(2)}) collective-permute-start(bf16[64,512]{1,0:T(8,128)(2,1)S(1)} %get-tuple-element.35), channel_id=1, source_target_pairs={{0,4},{1,5},{2,6},{3,7},{4,0},{5,1},{6,2},{7,3},{8,12},{9,13},{10,... | collective-permute-start | bytes 196616 | tf_op jit(solution)/shard_map/ppermute | solution.py:348
  79.7 5.8 %collective-permute-start.23 = (bf16[80,512]{1,0:T(8,128)(2,1)S(1)}, bf16[80,512]{1,0:T(8,128)(2,1)S(1)}, u32[]{:S(2)}, u32[]{:S(2)}) collective-permute-start(bf16[80,512]{1,0:T(8,128)(2,1)S(1)} %fusion.2), channel_id=1, source_target_pairs={{0,8},{1,9},{2,10},{3,11},{4,12},{5,13},{6,14},{7,15},{8,0},{9,1},... | collective-permute-start | bytes 245768 | tf_op jit(solution)/shard_map/ppermute | solution.py:310
  83.2 6.8 %collective-permute-start.25 = (bf16[128,512]{1,0:T(8,128)(2,1)S(1)}, bf16[128,512]{1,0:T(8,128)(2,1)S(1)}, u32[]{:S(2)}, u32[]{:S(2)}) collective-permute-start(bf16[128,512]{1,0:T(8,128)(2,1)S(1)} %pad_maximum_fusion.15), channel_id=1, source_target_pairs={{0,2},{1,3},{2,0},{3,1},{4,6},{5,7},{6,4},{7,5},{8,10},{9,11},{10,... | collective-permute-start | bytes 393224 | tf_op jit(solution)/shard_map/ppermute | solution.py:349
  85.5 6.5 %collective-permute-start.28 = (bf16[80,512]{1,0:T(8,128)(2,1)S(1)}, bf16[80,512]{1,0:T(8,128)(2,1)S(1)}, u32[]{:S(2)}, u32[]{:S(2)}) collective-permute-start(bf16[80,512]{1,0:T(8,128)(2,1)S(1)} %get-tuple-element.33), channel_id=1, source_target_pairs={{0,6},{1,7},{2,4},{3,5},{4,2},{5,3},{6,0},{7,1},{8,14},{9,15},{10,... | collective-permute-start | bytes 245768 | tf_op jit(solution)/shard_map/ppermute | solution.py:346
  87.1 4.9 %collective-permute-start.27 = (bf16[80,512]{1,0:T(8,128)(2,1)S(1)}, bf16[80,512]{1,0:T(8,128)(2,1)S(1)}, u32[]{:S(2)}, u32[]{:S(2)}) collective-permute-start(bf16[80,512]{1,0:T(8,128)(2,1)S(1)} %get-tuple-element.33), channel_id=1, source_target_pairs={{0,4},{1,5},{2,6},{3,7},{4,0},{5,1},{6,2},{7,3},{8,12},{9,13},{10,... | collective-permute-start | bytes 245768 | tf_op jit(solution)/shard_map/ppermute | solution.py:346
  87.5 4.4 %collective-permute-start.26 = (bf16[80,512]{1,0:T(8,128)(2,1)S(1)}, bf16[80,512]{1,0:T(8,128)(2,1)S(1)}, u32[]{:S(2)}, u32[]{:S(2)}) collective-permute-start(bf16[80,512]{1,0:T(8,128)(2,1)S(1)} %get-tuple-element.33), channel_id=1, source_target_pairs={{0,2},{1,3},{2,0},{3,1},{4,6},{5,7},{6,4},{7,5},{8,10},{9,11},{10,... | collective-permute-start | bytes 245768 | tf_op jit(solution)/shard_map/ppermute | solution.py:346
  (6 other events, 14.6 us)

commit v7 on v6

--- a/solution.py
+++ b/solution.py
@@ -33,11 +33,8 @@
 
 
 def row_blocks(rows):
-    if rows < TILE:
-        return [(0, rows)]
-    first = rows % TILE
-    cuts = [0] + list(range(first + TILE if first else TILE, rows + 1, TILE))
-    return list(zip(cuts[:-1], cuts[1:]))
+    cuts = list(range(0, max(rows - TILE, 0) + 1, TILE))
+    return list(zip(cuts, cuts[1:] + [rows]))
 
 
 def analyse_kernel(rows, at_ref, halo_ref, a_hbm, k_hbm, w_hbm, h_hbm, p_ref, new_ref, w_ref,

time: 95.8 us -> 97 us (1.013)
    ppermute x2, waiting for transfers between devices: 2.54 us -> 3.53 us  [swap(): return (lax.ppermute(send, 'tm', perm), None)]
  transfers between devices with their start and end apart: 30 -> 30, of which waited for: 18 -> 17; matrix products, arithmetic and copies ran while one was open for 1% -> 1% of each run, Pallas kernels for 8% -> 8%
where the time goes in v7:
time: 97 us; the launch traced here: 96.8 us
  starting transfers between devices  38.4 us (40%)
  Pallas kernels  28.6 us (29%)
  waiting for transfers between devices  26.3 us (27%)
  other arithmetic  2.07 us (2%)
  between operations  1.2 us (1%)
    pallas_call x11, Pallas kernels, call(): pl.pallas_call(kernel, out_shape=tuple(outs), in_specs=specs or [VMEM] *...  28.6 us
    ppermute x8, starting transfers between devices, swap(): lax.ppermute(jnp.concatenate([send, halves[0][None], halves[1][None], pad...  12.7 us
    ppermute x8, waiting for transfers between devices, swap(): lax.ppermute(jnp.concatenate([send, halves[0][None], halves[1][None], pad...  12 us
    ppermute x6, starting transfers between devices, spread(): return [part] + [lax.ppermute(part, 'tm', perm) for perm in perms]  7.11 us
    ppermute x2, starting transfers between devices, swap(): return (lax.ppermute(send, 'tm', perm), None)  5.69 us
    ppermute x1, starting transfers between devices, halo_rows(): two = lax.ppermute(jnp.where(odd, tail, head), 'tm', outer)  5.44 us
    ppermute x6, waiting for transfers between devices, spread(): return [part] + [lax.ppermute(part, 'tm', perm) for perm in perms]  4.81 us
    ppermute x2, waiting for transfers between devices, swap(): return (lax.ppermute(send, 'tm', perm), None)  3.53 us
  transfers between devices with their start and end apart: 30, of which 17 were waited for; matrix products, arithmetic and copies ran while one was open for 1% of the time, Pallas kernels for 8%

profile of v7, /device:TPU:0, one launch (start us, length us, event | category | flops | bytes accessed | tf_op | source)
XLA Modules:
  0.0 96.8 jit_solution(12900221900967333865)
XLA Ops:
  1.4 5.4 %collective-permute-start.1 = (bf16[2,128]{1,0:T(2,128)(2,1)S(1)}, bf16[2,128]{1,0:T(2,128)(2,1)S(1)}, u32[]{:S(2)}, u32[]{:S(2)}) collective-permute-start(bf16[2,128]{1,0:T(2,128)(2,1)S(1)} %get-tuple-element.52), channel_id=1, source_target_pairs={{0,15},{1,2},{2,1},{3,4},{4,3},{5,6},{6,5},{7,8},{8,7},{9,10},{10,... | collective-permute-start | bytes 1544 | tf_op jit(solution)/shard_map/ppermute | solution.py:276
  8.1 13.4 %shard_map.59 = (bf16[1152,1024]{1,0:T(8,128)(2,1)S(1)}, bf16[512,1024]{1,0:T(8,128)(2,1)S(1)}, bf16[1152,512]{1,0:T(8,128)(2,1)S(1)}) custom-call(s32[8]{0:T(128)S(1)} %stack.40.at_ref, f32[4,128]{1,0:T(4,128)S(1)} %maximum_convert_fusion.halo_ref, bf16[4096,128]{1,0:T(8,128)(2,1)} %bitcast.19, bf16[2304,1024]{1,0:T(8,128)(2,1)} %k_hbm.1, ...), custom_call_target="tpu_custom_call" | custom-call | flops 7247757312 | bytes 12584992 | tf_op jit(solution)/shard_map/pallas_call | solution.py:195
  21.5 1.7 %shard_map.61 = bf16[592,512]{1,0:T(8,128)(2,1)S(1)} custom-call(bf16[1152,1024]{1,0:T(8,128)(2,1)S(1)} %get-tuple-element.17.p_ref, bf16[1152,512]{1,0:T(8,128)(2,1)S(1)} %get-tuple-element.18.w_ref, bf16[512,1024]{1,0:T(8,128)(2,1)S(1)} %get-tuple-element.19.h_ref), custom_call_target="tpu_custom_call" | custom-call | flops 1207959552 | bytes 5193728 | tf_op jit(solution)/shard_map/pallas_call | solution.py:195
  27.4 1.9 %collective-permute-start.4 = (bf16[80,512]{1,0:T(8,128)(2,1)S(1)}, bf16[80,512]{1,0:T(8,128)(2,1)S(1)}, u32[]{:S(2)}, u32[]{:S(2)}) collective-permute-start(bf16[80,512]{1,0:T(8,128)(2,1)S(1)} %get-tuple-element.69), channel_id=1, source_target_pairs={{0,4},{1,5},{2,6},{3,7},{4,0},{5,1},{6,2},{7,3},{8,12},{9,13},{10,... | collective-permute-start | bytes 245768 | tf_op jit(solution)/shard_map/ppermute | solution.py:310
  29.5 3.3 %collective-permute-done.3 = bf16[80,512]{1,0:T(8,128)(2,1)S(1)} collective-permute-done((bf16[80,512]{1,0:T(8,128)(2,1)S(1)}, bf16[80,512]{1,0:T(8,128)(2,1)S(1)}, u32[]{:S(2)}, u32[]{:S(2)}) %collective-permute-start.3) | collective-permute-done | bytes 81952 | tf_op jit(solution)/shard_map/ppermute | solution.py:310
  33.7 2.3 %collective-permute-start.6 = (bf16[80,512]{1,0:T(8,128)(2,1)S(1)}, bf16[80,512]{1,0:T(8,128)(2,1)S(1)}, u32[]{:S(2)}, u32[]{:S(2)}) collective-permute-start(bf16[80,512]{1,0:T(8,128)(2,1)S(1)} %maximum_maximum_fusion), channel_id=1, source_target_pairs={{0,8},{1,9},{2,10},{3,11},{4,12},{5,13},{6,14},{7,15},{8,0},{9,1},... | collective-permute-start | bytes 245768 | tf_op jit(solution)/shard_map/ppermute | solution.py:310
  36.1 1.8 %collective-permute-start.8 = (bf16[80,512]{1,0:T(8,128)(2,1)S(1)}, bf16[80,512]{1,0:T(8,128)(2,1)S(1)}, u32[]{:S(2)}, u32[]{:S(2)}) collective-permute-start(bf16[80,512]{1,0:T(8,128)(2,1)S(1)} %fusion.3), channel_id=1, source_target_pairs={{0,4},{1,5},{2,6},{3,7},{4,0},{5,1},{6,2},{7,3},{8,12},{9,13},{10,... | collective-permute-start | bytes 245768 | tf_op jit(solution)/shard_map/ppermute | solution.py:329
  37.9 2.3 %collective-permute-done.6 = bf16[80,512]{1,0:T(8,128)(2,1)S(1)} collective-permute-done((bf16[80,512]{1,0:T(8,128)(2,1)S(1)}, bf16[80,512]{1,0:T(8,128)(2,1)S(1)}, u32[]{:S(2)}, u32[]{:S(2)}) %collective-permute-start.6) | collective-permute-done | bytes 81952 | tf_op jit(solution)/shard_map/ppermute | solution.py:310
  41.1 3.2 %collective-permute-start.9 = (bf16[80,512]{1,0:T(8,128)(2,1)S(1)}, bf16[80,512]{1,0:T(8,128)(2,1)S(1)}, u32[]{:S(2)}, u32[]{:S(2)}) collective-permute-start(bf16[80,512]{1,0:T(8,128)(2,1)S(1)} %fusion.5), channel_id=1, source_target_pairs={{0,8},{1,9},{2,10},{3,11},{4,12},{5,13},{6,14},{7,15},{8,0},{9,1},... | collective-permute-start | bytes 245768 | tf_op jit(solution)/shard_map/ppermute | solution.py:307
  46.8 2.5 %collective-permute-start.14 = (bf16[80,512]{1,0:T(8,128)(2,1)S(1)}, bf16[80,512]{1,0:T(8,128)(2,1)S(1)}, u32[]{:S(2)}, u32[]{:S(2)}) collective-permute-start(bf16[80,512]{1,0:T(8,128)(2,1)S(1)} %get-tuple-element.43), channel_id=1, source_target_pairs={{0,6},{1,7},{2,4},{3,5},{4,2},{5,3},{6,0},{7,1},{8,14},{9,15},{10,... | collective-permute-start | bytes 245768 | tf_op jit(solution)/shard_map/ppermute | solution.py:343
  50.3 2.4 %collective-permute-done.11 = bf16[128,512]{1,0:T(8,128)(2,1)S(1)} collective-permute-done((bf16[128,512]{1,0:T(8,128)(2,1)S(1)}, bf16[128,512]{1,0:T(8,128)(2,1)S(1)}, u32[]{:S(2)}, u32[]{:S(2)}) %collective-permute-start.11) | collective-permute-done | bytes 131104 | tf_op jit(solution)/shard_map/ppermute | solution.py:346
  52.7 1.7 %collective-permute-done.12 = bf16[80,512]{1,0:T(8,128)(2,1)S(1)} collective-permute-done((bf16[80,512]{1,0:T(8,128)(2,1)S(1)}, bf16[80,512]{1,0:T(8,128)(2,1)S(1)}, u32[]{:S(2)}, u32[]{:S(2)}) %collective-permute-start.12) | collective-permute-done | bytes 81952 | tf_op jit(solution)/shard_map/ppermute | solution.py:343
  54.6 2.0 %shard_map.63 = (f32[512,1024]{1,0:T(8,128)S(1)}, f32[512,128]{1,0:T(8,128)S(1)}) custom-call(bf16[1152,1024]{1,0:T(8,128)(2,1)S(1)} %get-tuple-element.17.p_ref, bf16[576,512]{1,0:T(8,128)(2,1)S(1)} %constant_dynamic-update-slice_fusion.w_ref, bf16[512,1024]{1,0:T(8,128)(2,1)S(1)} %get-tuple-element.19.h_ref), custom_call_target="tpu_custom_call" | custom-call | flops 1207959552 | bytes 6356992 | tf_op jit(solution)/shard_map/pallas_call | solution.py:195
  56.6 2.7 %shard_map.64.h_ref.acts_ref = bf16[512,1024]{1,0:T(8,128)(2,1)S(1)} custom-call(bf16[1152,1024]{1,0:T(8,128)(2,1)S(1)} %get-tuple-element.17.p_ref, bf16[576,512]{1,0:T(8,128)(2,1)S(1)} %collective-permute-done.15.w_ref, bf16[512,1024]{1,0:T(8,128)(2,1)S(1)} %get-tuple-element.19.h_ref, f32[512,1024]{1,0:T(8,128)S(1)} %get-tuple-element.24.refs_0_, ...), custom_call_target="tpu_custom_call" | custom-call | flops 1207959552 | bytes 7405568 | tf_op jit(solution)/shard_map/pallas_call | solution.py:195
  59.3 1.7 %shard_map.66 = bf16[592,512]{1,0:T(8,128)(2,1)S(1)} custom-call(bf16[1152,1024]{1,0:T(8,128)(2,1)S(1)} %get-tuple-element.17.p_ref, bf16[576,512]{1,0:T(8,128)(2,1)S(1)} %collective-permute-done.15.w_ref, bf16[512,1024]{1,0:T(8,128)(2,1)S(1)} %shard_map.64.h_ref.acts_ref), custom_call_target="tpu_custom_call" | custom-call | flops 1207959552 | bytes 4603904 | tf_op jit(solution)/shard_map/pallas_call | solution.py:195
  64.3 2.5 %collective-permute-start.19 = (bf16[80,512]{1,0:T(8,128)(2,1)S(1)}, bf16[80,512]{1,0:T(8,128)(2,1)S(1)}, u32[]{:S(2)}, u32[]{:S(2)}) collective-permute-start(bf16[80,512]{1,0:T(8,128)(2,1)S(1)} %get-tuple-element.65), channel_id=1, source_target_pairs={{0,6},{1,7},{2,4},{3,5},{4,2},{5,3},{6,0},{7,1},{8,14},{9,15},{10,... | collective-permute-start | bytes 245768 | tf_op jit(solution)/shard_map/ppermute | solution.py:310
  67.9 2.5 %collective-permute-done.17 = bf16[80,512]{1,0:T(8,128)(2,1)S(1)} collective-permute-done((bf16[80,512]{1,0:T(8,128)(2,1)S(1)}, bf16[80,512]{1,0:T(8,128)(2,1)S(1)}, u32[]{:S(2)}, u32[]{:S(2)}) %collective-permute-start.17) | collective-permute-done | bytes 81952 | tf_op jit(solution)/shard_map/ppermute | solution.py:310
  71.6 3.3 %collective-permute-start.20 = (bf16[80,512]{1,0:T(8,128)(2,1)S(1)}, bf16[80,512]{1,0:T(8,128)(2,1)S(1)}, u32[]{:S(2)}, u32[]{:S(2)}) collective-permute-start(bf16[80,512]{1,0:T(8,128)(2,1)S(1)} %maximum_maximum_fusion.1), channel_id=1, source_target_pairs={{0,8},{1,9},{2,10},{3,11},{4,12},{5,13},{6,14},{7,15},{8,0},{9,1},... | collective-permute-start | bytes 245768 | tf_op jit(solution)/shard_map/ppermute | solution.py:310
  76.2 2.1 %collective-permute-done.20 = bf16[80,512]{1,0:T(8,128)(2,1)S(1)} collective-permute-done((bf16[80,512]{1,0:T(8,128)(2,1)S(1)}, bf16[80,512]{1,0:T(8,128)(2,1)S(1)}, u32[]{:S(2)}, u32[]{:S(2)}) %collective-permute-start.20) | collective-permute-done | bytes 81952 | tf_op jit(solution)/shard_map/ppermute | solution.py:310
  80.1 2.5 %collective-permute-start.23 = (bf16[80,512]{1,0:T(8,128)(2,1)S(1)}, bf16[80,512]{1,0:T(8,128)(2,1)S(1)}, u32[]{:S(2)}, u32[]{:S(2)}) collective-permute-start(bf16[80,512]{1,0:T(8,128)(2,1)S(1)} %fusion.2), channel_id=1, source_target_pairs={{0,8},{1,9},{2,10},{3,11},{4,12},{5,13},{6,14},{7,15},{8,0},{9,1},... | collective-permute-start | bytes 245768 | tf_op jit(solution)/shard_map/ppermute | solution.py:307
  83.7 2.7 %collective-permute-done.23 = bf16[80,512]{1,0:T(8,128)(2,1)S(1)} collective-permute-done((bf16[80,512]{1,0:T(8,128)(2,1)S(1)}, bf16[80,512]{1,0:T(8,128)(2,1)S(1)}, u32[]{:S(2)}, u32[]{:S(2)}) %collective-permute-start.23) | collective-permute-done | bytes 81952 | tf_op jit(solution)/shard_map/ppermute | solution.py:307
  87.0 1.7 %collective-permute-start.27 = (bf16[80,512]{1,0:T(8,128)(2,1)S(1)}, bf16[80,512]{1,0:T(8,128)(2,1)S(1)}, u32[]{:S(2)}, u32[]{:S(2)}) collective-permute-start(bf16[80,512]{1,0:T(8,128)(2,1)S(1)} %get-tuple-element.33), channel_id=1, source_target_pairs={{0,4},{1,5},{2,6},{3,7},{4,0},{5,1},{6,2},{7,3},{8,12},{9,13},{10,... | collective-permute-start | bytes 245768 | tf_op jit(solution)/shard_map/ppermute | solution.py:343
  90.1 3.1 %collective-permute-done.26 = bf16[80,512]{1,0:T(8,128)(2,1)S(1)} collective-permute-done((bf16[80,512]{1,0:T(8,128)(2,1)S(1)}, bf16[80,512]{1,0:T(8,128)(2,1)S(1)}, u32[]{:S(2)}, u32[]{:S(2)}) %collective-permute-start.26) | collective-permute-done | bytes 81952 | tf_op jit(solution)/shard_map/ppermute | solution.py:343
  93.4 1.7 %shard_map.68 = (bf16[1152,512]{1,0:T(8,128)(2,1)}, bf16[512,1024]{1,0:T(8,128)(2,1)}) custom-call(s32[4]{0:T(128)S(1)} %pad_add_fusion.at_ref, bf16[576,512]{1,0:T(8,128)(2,1)S(1)} %constant_dynamic-update-slice_fusion.6.own_ref, bf16[512,1024]{1,0:T(8,128)(2,1)S(1)} %shard_map.64.h_ref.acts_ref), custom_call_target="tpu_custom_call" | custom-call | flops 536870912 | bytes 3866640 | tf_op jit(solution)/shard_map/pallas_call | solution.py:195
  (103 shorter events, 25.2 us)
Async XLA Ops:
  1.4 6.7 %collective-permute-start.1 = (bf16[2,128]{1,0:T(2,128)(2,1)S(1)}, bf16[2,128]{1,0:T(2,128)(2,1)S(1)}, u32[]{:S(2)}, u32[]{:S(2)}) collective-permute-start(bf16[2,128]{1,0:T(2,128)(2,1)S(1)} %get-tuple-element.52), channel_id=1, source_target_pairs={{0,15},{1,2},{2,1},{3,4},{4,3},{5,6},{6,5},{7,8},{8,7},{9,10},{10,... | collective-permute-start | bytes 1544 | tf_op jit(solution)/shard_map/ppermute | solution.py:276
  25.7 7.1 %collective-permute-start.3 = (bf16[80,512]{1,0:T(8,128)(2,1)S(1)}, bf16[80,512]{1,0:T(8,128)(2,1)S(1)}, u32[]{:S(2)}, u32[]{:S(2)}) collective-permute-start(bf16[80,512]{1,0:T(8,128)(2,1)S(1)} %get-tuple-element.67), channel_id=1, source_target_pairs={{0,2},{1,3},{2,0},{3,1},{4,6},{5,7},{6,4},{7,5},{8,10},{9,11},{10,... | collective-permute-start | bytes 245768 | tf_op jit(solution)/shard_map/ppermute | solution.py:310
  25.8 7.0 %collective-permute-start.5 = (bf16[80,512]{1,0:T(8,128)(2,1)S(1)}, bf16[80,512]{1,0:T(8,128)(2,1)S(1)}, u32[]{:S(2)}, u32[]{:S(2)}) collective-permute-start(bf16[80,512]{1,0:T(8,128)(2,1)S(1)} %get-tuple-element.68), channel_id=1, source_target_pairs={{0,6},{1,7},{2,4},{3,5},{4,2},{5,3},{6,0},{7,1},{8,14},{9,15},{10,... | collective-permute-start | bytes 245768 | tf_op jit(solution)/shard_map/ppermute | solution.py:310
  27.4 6.2 %collective-permute-start.4 = (bf16[80,512]{1,0:T(8,128)(2,1)S(1)}, bf16[80,512]{1,0:T(8,128)(2,1)S(1)}, u32[]{:S(2)}, u32[]{:S(2)}) collective-permute-start(bf16[80,512]{1,0:T(8,128)(2,1)S(1)} %get-tuple-element.69), channel_id=1, source_target_pairs={{0,4},{1,5},{2,6},{3,7},{4,0},{5,1},{6,2},{7,3},{8,12},{9,13},{10,... | collective-permute-start | bytes 245768 | tf_op jit(solution)/shard_map/ppermute | solution.py:310
  29.3 6.8 %collective-permute-start.7 = (bf16[160,512]{1,0:T(8,128)(2,1)S(1)}, bf16[160,512]{1,0:T(8,128)(2,1)S(1)}, u32[]{:S(2)}, u32[]{:S(2)}) collective-permute-start(bf16[160,512]{1,0:T(8,128)(2,1)S(1)} %pad_maximum_fusion), channel_id=1, source_target_pairs={{0,2},{1,3},{2,0},{3,1},{4,6},{5,7},{6,4},{7,5},{8,10},{9,11},{10,... | collective-permute-start | bytes 491528 | tf_op jit(solution)/shard_map/ppermute | solution.py:326
  33.7 6.5 %collective-permute-start.6 = (bf16[80,512]{1,0:T(8,128)(2,1)S(1)}, bf16[80,512]{1,0:T(8,128)(2,1)S(1)}, u32[]{:S(2)}, u32[]{:S(2)}) collective-permute-start(bf16[80,512]{1,0:T(8,128)(2,1)S(1)} %maximum_maximum_fusion), channel_id=1, source_target_pairs={{0,8},{1,9},{2,10},{3,11},{4,12},{5,13},{6,14},{7,15},{8,0},{9,1},... | collective-permute-start | bytes 245768 | tf_op jit(solution)/shard_map/ppermute | solution.py:310
  36.1 5.0 %collective-permute-start.8 = (bf16[80,512]{1,0:T(8,128)(2,1)S(1)}, bf16[80,512]{1,0:T(8,128)(2,1)S(1)}, u32[]{:S(2)}, u32[]{:S(2)}) collective-permute-start(bf16[80,512]{1,0:T(8,128)(2,1)S(1)} %fusion.3), channel_id=1, source_target_pairs={{0,4},{1,5},{2,6},{3,7},{4,0},{5,1},{6,2},{7,3},{8,12},{9,13},{10,... | collective-permute-start | bytes 245768 | tf_op jit(solution)/shard_map/ppermute | solution.py:329
  40.3 4.7 %collective-permute-start.10 = (bf16[64,512]{1,0:T(8,128)(2,1)S(1)}, bf16[64,512]{1,0:T(8,128)(2,1)S(1)}, u32[]{:S(2)}, u32[]{:S(2)}) collective-permute-start(bf16[64,512]{1,0:T(8,128)(2,1)S(1)} %get-tuple-element.45), channel_id=1, source_target_pairs={{0,4},{1,5},{2,6},{3,7},{4,0},{5,1},{6,2},{7,3},{8,12},{9,13},{10,... | collective-permute-start | bytes 196616 | tf_op jit(solution)/shard_map/ppermute | solution.py:345
  41.1 5.6 %collective-permute-start.9 = (bf16[80,512]{1,0:T(8,128)(2,1)S(1)}, bf16[80,512]{1,0:T(8,128)(2,1)S(1)}, u32[]{:S(2)}, u32[]{:S(2)}) collective-permute-start(bf16[80,512]{1,0:T(8,128)(2,1)S(1)} %fusion.5), channel_id=1, source_target_pairs={{0,8},{1,9},{2,10},{3,11},{4,12},{5,13},{6,14},{7,15},{8,0},{9,1},... | collective-permute-start | bytes 245768 | tf_op jit(solution)/shard_map/ppermute | solution.py:307
  45.0 7.7 %collective-permute-start.11 = (bf16[128,512]{1,0:T(8,128)(2,1)S(1)}, bf16[128,512]{1,0:T(8,128)(2,1)S(1)}, u32[]{:S(2)}, u32[]{:S(2)}) collective-permute-start(bf16[128,512]{1,0:T(8,128)(2,1)S(1)} %pad_maximum_fusion.14), channel_id=1, source_target_pairs={{0,2},{1,3},{2,0},{3,1},{4,6},{5,7},{6,4},{7,5},{8,10},{9,11},{10,... | collective-permute-start | bytes 393224 | tf_op jit(solution)/shard_map/ppermute | solution.py:346
  46.8 7.7 %collective-permute-start.14 = (bf16[80,512]{1,0:T(8,128)(2,1)S(1)}, bf16[80,512]{1,0:T(8,128)(2,1)S(1)}, u32[]{:S(2)}, u32[]{:S(2)}) collective-permute-start(bf16[80,512]{1,0:T(8,128)(2,1)S(1)} %get-tuple-element.43), channel_id=1, source_target_pairs={{0,6},{1,7},{2,4},{3,5},{4,2},{5,3},{6,0},{7,1},{8,14},{9,15},{10,... | collective-permute-start | bytes 245768 | tf_op jit(solution)/shard_map/ppermute | solution.py:343
  49.3 5.2 %collective-permute-start.13 = (bf16[80,512]{1,0:T(8,128)(2,1)S(1)}, bf16[80,512]{1,0:T(8,128)(2,1)S(1)}, u32[]{:S(2)}, u32[]{:S(2)}) collective-permute-start(bf16[80,512]{1,0:T(8,128)(2,1)S(1)} %get-tuple-element.43), channel_id=1, source_target_pairs={{0,4},{1,5},{2,6},{3,7},{4,0},{5,1},{6,2},{7,3},{8,12},{9,13},{10,... | collective-permute-start | bytes 245768 | tf_op jit(solution)/shard_map/ppermute | solution.py:343
  50.0 4.4 %collective-permute-start.12 = (bf16[80,512]{1,0:T(8,128)(2,1)S(1)}, bf16[80,512]{1,0:T(8,128)(2,1)S(1)}, u32[]{:S(2)}, u32[]{:S(2)}) collective-permute-start(bf16[80,512]{1,0:T(8,128)(2,1)S(1)} %get-tuple-element.43), channel_id=1, source_target_pairs={{0,2},{1,3},{2,0},{3,1},{4,6},{5,7},{6,4},{7,5},{8,10},{9,11},{10,... | collective-permute-start | bytes 245768 | tf_op jit(solution)/shard_map/ppermute | solution.py:343
  63.9 6.5 %collective-permute-start.17 = (bf16[80,512]{1,0:T(8,128)(2,1)S(1)}, bf16[80,512]{1,0:T(8,128)(2,1)S(1)}, u32[]{:S(2)}, u32[]{:S(2)}) collective-permute-start(bf16[80,512]{1,0:T(8,128)(2,1)S(1)} %get-tuple-element.64), channel_id=1, source_target_pairs={{0,2},{1,3},{2,0},{3,1},{4,6},{5,7},{6,4},{7,5},{8,10},{9,11},{10,... | collective-permute-start | bytes 245768 | tf_op jit(solution)/shard_map/ppermute | solution.py:310
  64.3 6.1 %collective-permute-start.19 = (bf16[80,512]{1,0:T(8,128)(2,1)S(1)}, bf16[80,512]{1,0:T(8,128)(2,1)S(1)}, u32[]{:S(2)}, u32[]{:S(2)}) collective-permute-start(bf16[80,512]{1,0:T(8,128)(2,1)S(1)} %get-tuple-element.65), channel_id=1, source_target_pairs={{0,6},{1,7},{2,4},{3,5},{4,2},{5,3},{6,0},{7,1},{8,14},{9,15},{10,... | collective-permute-start | bytes 245768 | tf_op jit(solution)/shard_map/ppermute | solution.py:310
  66.8 4.7 %collective-permute-start.18 = (bf16[80,512]{1,0:T(8,128)(2,1)S(1)}, bf16[80,512]{1,0:T(8,128)(2,1)S(1)}, u32[]{:S(2)}, u32[]{:S(2)}) collective-permute-start(bf16[80,512]{1,0:T(8,128)(2,1)S(1)} %get-tuple-element.66), channel_id=1, source_target_pairs={{0,4},{1,5},{2,6},{3,7},{4,0},{5,1},{6,2},{7,3},{8,12},{9,13},{10,... | collective-permute-start | bytes 245768 | tf_op jit(solution)/shard_map/ppermute | solution.py:310
  67.5 7.4 %collective-permute-start.21 = (bf16[160,512]{1,0:T(8,128)(2,1)S(1)}, bf16[160,512]{1,0:T(8,128)(2,1)S(1)}, u32[]{:S(2)}, u32[]{:S(2)}) collective-permute-start(bf16[160,512]{1,0:T(8,128)(2,1)S(1)} %pad_maximum_fusion.1), channel_id=1, source_target_pairs={{0,2},{1,3},{2,0},{3,1},{4,6},{5,7},{6,4},{7,5},{8,10},{9,11},{10,... | collective-permute-start | bytes 491528 | tf_op jit(solution)/shard_map/ppermute | solution.py:326
  71.6 6.6 %collective-permute-start.20 = (bf16[80,512]{1,0:T(8,128)(2,1)S(1)}, bf16[80,512]{1,0:T(8,128)(2,1)S(1)}, u32[]{:S(2)}, u32[]{:S(2)}) collective-permute-start(bf16[80,512]{1,0:T(8,128)(2,1)S(1)} %maximum_maximum_fusion.1), channel_id=1, source_target_pairs={{0,8},{1,9},{2,10},{3,11},{4,12},{5,13},{6,14},{7,15},{8,0},{9,1},... | collective-permute-start | bytes 245768 | tf_op jit(solution)/shard_map/ppermute | solution.py:310
  75.0 5.1 %collective-permute-start.22 = (bf16[80,512]{1,0:T(8,128)(2,1)S(1)}, bf16[80,512]{1,0:T(8,128)(2,1)S(1)}, u32[]{:S(2)}, u32[]{:S(2)}) collective-permute-start(bf16[80,512]{1,0:T(8,128)(2,1)S(1)} %fusion), channel_id=1, source_target_pairs={{0,4},{1,5},{2,6},{3,7},{4,0},{5,1},{6,2},{7,3},{8,12},{9,13},{10,... | collective-permute-start | bytes 245768 | tf_op jit(solution)/shard_map/ppermute | solution.py:329
  78.3 4.5 %collective-permute-start.24 = (bf16[64,512]{1,0:T(8,128)(2,1)S(1)}, bf16[64,512]{1,0:T(8,128)(2,1)S(1)}, u32[]{:S(2)}, u32[]{:S(2)}) collective-permute-start(bf16[64,512]{1,0:T(8,128)(2,1)S(1)} %get-tuple-element.35), channel_id=1, source_target_pairs={{0,4},{1,5},{2,6},{3,7},{4,0},{5,1},{6,2},{7,3},{8,12},{9,13},{10,... | collective-permute-start | bytes 196616 | tf_op jit(solution)/shard_map/ppermute | solution.py:345
  80.1 6.4 %collective-permute-start.23 = (bf16[80,512]{1,0:T(8,128)(2,1)S(1)}, bf16[80,512]{1,0:T(8,128)(2,1)S(1)}, u32[]{:S(2)}, u32[]{:S(2)}) collective-permute-start(bf16[80,512]{1,0:T(8,128)(2,1)S(1)} %fusion.2), channel_id=1, source_target_pairs={{0,8},{1,9},{2,10},{3,11},{4,12},{5,13},{6,14},{7,15},{8,0},{9,1},... | collective-permute-start | bytes 245768 | tf_op jit(solution)/shard_map/ppermute | solution.py:307
  82.8 7.2 %collective-permute-start.25 = (bf16[128,512]{1,0:T(8,128)(2,1)S(1)}, bf16[128,512]{1,0:T(8,128)(2,1)S(1)}, u32[]{:S(2)}, u32[]{:S(2)}) collective-permute-start(bf16[128,512]{1,0:T(8,128)(2,1)S(1)} %pad_maximum_fusion.15), channel_id=1, source_target_pairs={{0,2},{1,3},{2,0},{3,1},{4,6},{5,7},{6,4},{7,5},{8,10},{9,11},{10,... | collective-permute-start | bytes 393224 | tf_op jit(solution)/shard_map/ppermute | solution.py:346
  86.5 6.7 %collective-permute-start.28 = (bf16[80,512]{1,0:T(8,128)(2,1)S(1)}, bf16[80,512]{1,0:T(8,128)(2,1)S(1)}, u32[]{:S(2)}, u32[]{:S(2)}) collective-permute-start(bf16[80,512]{1,0:T(8,128)(2,1)S(1)} %get-tuple-element.33), channel_id=1, source_target_pairs={{0,6},{1,7},{2,4},{3,5},{4,2},{5,3},{6,0},{7,1},{8,14},{9,15},{10,... | collective-permute-start | bytes 245768 | tf_op jit(solution)/shard_map/ppermute | solution.py:343
  87.0 6.1 %collective-permute-start.27 = (bf16[80,512]{1,0:T(8,128)(2,1)S(1)}, bf16[80,512]{1,0:T(8,128)(2,1)S(1)}, u32[]{:S(2)}, u32[]{:S(2)}) collective-permute-start(bf16[80,512]{1,0:T(8,128)(2,1)S(1)} %get-tuple-element.33), channel_id=1, source_target_pairs={{0,4},{1,5},{2,6},{3,7},{4,0},{5,1},{6,2},{7,3},{8,12},{9,13},{10,... | collective-permute-start | bytes 245768 | tf_op jit(solution)/shard_map/ppermute | solution.py:343
  (6 other events, 14.7 us)
